TPU v7x, 128 devices: a whole 4x4x4 slice. The times are simulated.
128 devices in a mesh: tm: 4 (over z_lo, core), tile: 32 (over y, x, z_hi).
Axes of the slice: x: 4, y: 4, z: 4 (z_hi: 2, z_lo: 2; z = z_hi * 2 + z_lo), core: 2. Of those that a mesh axis runs over, the one named last changes fastest.
Arguments:
- pcs: float32 [2, 256], P(None, 'tm'), may hold values from -6 to 6
- st_eof: float32 [2, 120, 512], replicated, may hold values from -6 to 6
- spatial_eof: bfloat16 [2, 512, 256, 2048], P(None, 'tm', 'tile'), may hold values from -1 to 1
- land_sea: int32 [256, 2048], P('tile'), may hold values 0 or 1
Outputs:
- vorticity: float32 [256, 256, 2048], P('tm', 'tile')
- divergence: float32 [256, 256, 2048], P('tm', 'tile')
All inputs are finite; a program needn't handle non-finite values. No bound on the sum of `land_sea` on one device may be relied on, other than what follows from the above.
Results may differ from a plain program's by a relative error of at most 0.0041.
Values may be sent and summed in bfloat16 or wider, within the bound.
No kernel may reach another device: no remote copies, remote signals or barrier semaphores. Data moves between devices by JAX's collectives and lax.ppermute only.
A program may use at most 128 MiB of HBM per device.

v0:
```python
import math

import jax
import jax.numpy as jnp
from jax import lax
from jax.sharding import PartitionSpec as P


def padded_2(block, sides, width):
    for axis, dim in sides:
        count = lax.axis_size(axis)
        forward = [(i, i + 1) for i in range(count - 1)]
        backward = [(target, source) for source, target in forward]
        low = lax.ppermute(
            lax.slice_in_dim(block, block.shape[dim] - width, None, axis=dim), axis, forward
        )
        high = lax.ppermute(lax.slice_in_dim(block, 0, width, axis=dim), axis, backward)
        block = jnp.concatenate([low, block, high], axis=dim)
    return block


def lagged_rc(series, st_eof, first, count):
    day_index = first + jnp.arange(count, dtype=jnp.int32)
    lag_steps = jnp.arange(st_eof.shape[1], dtype=jnp.int32)
    lag_index = day_index[:, None] - lag_steps[None, :]
    inside = lag_index >= 0
    safe_index = jnp.maximum(lag_index, 0)
    values_lag = jnp.where(inside[None], series[:, safe_index], 0.0)
    lag_total = st_eof.shape[0] * st_eof.shape[1]
    lagged = jnp.transpose(values_lag, (1, 0, 2)).reshape(count, lag_total)
    lagged_sums = jnp.dot(
        lagged,
        st_eof.reshape(lag_total, -1),
        precision=lax.Precision.HIGHEST,
        preferred_element_type=jnp.float32,
    )
    window_len = jnp.minimum(day_index + 1, st_eof.shape[1]).astype(jnp.float32)
    return lagged_sums / window_len[:, None]


def curl_div(east_pad, north_pad, latitude):
    cosine = jnp.cos(latitude)
    cos_east = east_pad * cosine[None, :, None]
    cos_north = north_pad * cosine[None, :, None]
    inner_east = east_pad[:, 1:-1]
    inner_north = north_pad[:, 1:-1]
    zonal_east = jnp.roll(inner_east, -1, axis=2) - jnp.roll(inner_east, 1, axis=2)
    zonal_north = jnp.roll(inner_north, -1, axis=2) - jnp.roll(inner_north, 1, axis=2)
    denominator = 2.0 * cosine[1:-1][None, :, None]
    vorticity = (zonal_north - (cos_east[:, 2:] - cos_east[:, :-2])) / denominator
    divergence = (zonal_east + (cos_north[:, 2:] - cos_north[:, :-2])) / denominator
    return (vorticity, divergence)


def shards(pcs, st_eof, spatial_eof, land_sea):
    day_dev = pcs.shape[1]
    all_pcs = lax.all_gather(pcs, "tm", axis=1, tiled=True)
    own_index = lax.axis_index("tm")
    lat_rows, lon_cells = land_sea.shape
    cell_count = lat_rows * lon_cells
    chan_share = spatial_eof.shape[1]
    local_eof = spatial_eof.reshape(2, chan_share, cell_count)
    own_rc = lagged_rc(all_pcs, st_eof, own_index * day_dev, day_dev).astype(jnp.bfloat16)
    fields = jnp.einsum(
        "tc,xcn->txn",
        own_rc,
        lax.all_gather(local_eof, "tm", axis=1, tiled=True),
        preferred_element_type=jnp.float32,
    )
    ocean_mask = land_sea.astype(jnp.float32)
    velocity = (
        (fields * ocean_mask.reshape(1, 1, cell_count))
        .astype(jnp.bfloat16)
        .reshape(day_dev, 2, lat_rows, lon_cells)
    )
    padded = padded_2(velocity, (("tile", 2),), 1)
    total_rows = lat_rows * lax.axis_size("tile")
    global_rows = (lax.axis_index("tile") * lat_rows).astype(jnp.float32) + jnp.arange(
        -1, lat_rows + 1, dtype=jnp.float32
    )
    latitude = (-70.0 + 140.0 * (global_rows + 0.5) / total_rows) * (math.pi / 180.0)
    vorticity, divergence = curl_div(
        padded[:, 0].astype(jnp.float32), padded[:, 1].astype(jnp.float32), latitude
    )
    return (vorticity * ocean_mask[None], divergence * ocean_mask[None])


def solution(mesh):
    return jax.shard_map(
        shards,
        mesh=mesh,
        in_specs=(P(None, "tm"), P(), P(None, "tm", "tile", None), P("tile", None)),
        out_specs=(P("tm", "tile", None), P("tm", "tile", None)),
        check_vma=False,
    )
```

profile of v0, /device:TPU:1, one launch (start us, length us, event | category | flops | bytes accessed | tf_op | source)
XLA Modules:
  0.0 445.5 jit_solution(5867885944150111973)
XLA Ops:
  7.2 0.0 all-gather.3.cloned.1.call-start
  7.2 13.6 %reshape.93 = bf16[2,128,16384]{2,1,0:T(8,128)(2,1)} reshape(bf16[2,128,8,2048]{3,2,1,0:T(8,128)(2,1)} %param.6) | data formatting | bytes 16777216 | tf_op jit(solution)/shard_map/reshape | solution.py:62
  20.8 0.0 all-gather.3.cloned.1.call-update
  20.8 0.1 subtract_maximum_fusion
  20.9 0.1 reshape.99
  21.0 0.4 copy-done.4
  21.5 6.3 %all-gather = f32[4,64,2]{1,2,0:T(2,128)S(1)} all-gather(f32[1,64,2]{1,2,0:T(2,128)S(1)} %bitcast.56), channel_id=1, replica_groups=mesh['tm'=4,'tile'=32] {'tm'}, dimensions={0}, use_global_device_ids=true | all-gather | bytes 2560 | tf_op jit(solution)/shard_map/all_gather | solution.py:57
  27.8 0.1 copy.8
  27.9 14.9 %gather_fusion = f32[7680,2]{1,0:T(8,128)} fusion(f32[2,256]{0,1:T(8,128)S(1)} %bitcast.54, s32[8192]{0:T(1024)S(1)} %pad_clamp_fusion), kind=kCustom, calls=%fused_computation | custom fusion | bytes 153600 | tf_op jit(solution)/shard_map/gather | solution.py:28
  42.8 3.2 copy.9
  46.1 0.1 subtract_compare_fusion
  46.2 0.4 fusion.11
  46.6 269.0 %all-gather.3.cloned.1.call-done = bf16[2,512,16384]{2,1,0:T(8,128)(2,1)} async-done(((bf16[2,128,16384]{2,1,0:T(8,128)(2,1)}), bf16[2,512,16384]{2,1,0:T(8,128)(2,1)}) %all-gather.3.cloned.1.call-update) | async-done | bytes 33554448 | tf_op jit(solution)/shard_map/all_gather | solution.py:67
  315.6 18.5 %fusion = bf16[64,2,16384]{2,0,1:T(8,128)(2,1)} fusion(bf16[64,512,1]{1,0,2:T(8,128)(2,1)S(1)} %fusion.11, bf16[2,512,16384]{2,1,0:T(8,128)(2,1)} %all-gather.3.cloned.1.call-done, f32[16384]{0:T(1024)S(1)} %bitcast.55), kind=kOutput, calls=%fused_computation.2 | convolution fusion | flops 2151677952 | bytes 37879808 | tf_op jit(solution)/shard_map/tc,xcn->txn/dot_general | solution.py:64
  334.1 5.0 %copy.17 = bf16[16,8,8,2048]{3,2,1,0:T(8,128)(2,1)S(1)} copy(bf16[16,8,8,2048]{3,1,2,0:T(8,128)(2,1)} %bitcast.50) | data formatting | bytes 8388608
  339.1 2.0 copy-done.2
  341.1 1.4 fusion.21
  342.5 0.3 copy.14
  342.8 4.5 %collective-permute-start = (bf16[64,2,1,2048]{3,0,2,1:T(8,128)(2,1)S(1)}, bf16[64,2,1,2048]{3,0,2,1:T(8,128)(2,1)S(1)}, u32[]{:S(2)}, u32[]{:S(2)}) collective-permute-start(bf16[64,2,1,2048]{3,0,2,1:T(8,128)(2,1)S(1)} %copy.14), channel_id=1, source_target_pairs={{0,1},{1,2},{2,3},{3,4},{4,5},{5,6},{6,7},{7,8},{8,9},{9,10},{10,1... | collective-permute-start | bytes 1572872 | tf_op jit(solution)/shard_map/ppermute | solution.py:14
  347.4 0.3 copy.15
  347.7 1.5 collective-permute-start.1
  349.2 0.1 multiply_cosine_fusion
  349.2 0.1 slice_multiply_fusion
  349.3 20.2 %collective-permute-done = bf16[64,2,1,2048]{3,0,2,1:T(8,128)(2,1)S(1)} collective-permute-done((bf16[64,2,1,2048]{3,0,2,1:T(8,128)(2,1)S(1)}, bf16[64,2,1,2048]{3,0,2,1:T(8,128)(2,1)S(1)}, u32[]{:S(2)}, u32[]{:S(2)}) %collective-permute-start) | collective-permute-done | bytes 524320 | tf_op jit(solution)/shard_map/ppermute | solution.py:14
  369.5 0.8 copy.12
  370.3 0.8 copy.13
  371.2 8.5 %pad_maximum_fusion = bf16[64,2,10,2048]{3,2,0,1:T(8,128)(2,1)} fusion(bf16[64,2,1,2048]{3,2,0,1:T(2,128)(2,1)S(1)} %copy.13, bf16[64,2,8,2048]{3,2,0,1:T(8,128)(2,1)} %bitcast.52, bf16[64,2,1,2048]{3,2,0,1:T(2,128)(2,1)S(1)} %copy.12), kind=kLoop, calls=%fused_computation.3 | loop fusion | flops 15728640 | bytes 10485760 | tf_op jit(solution)/shard_map/concatenate | solution.py:18
  379.7 11.3 %fusion.7 = (f32[64,10,2048]{2,1,0:T(8,128)}, f32[64,10,2048]{2,1,0:T(8,128)}) fusion(bf16[64,2,10,2048]{3,2,0,1:T(8,128)(2,1)} %pad_maximum_fusion), kind=kLoop, calls=%fused_computation.13 | loop fusion | flops 2621440 | bytes 15728640 | tf_op jit(solution)/shard_map/convert_element_type | solution.py:83
  391.0 17.3 %fusion.18 = (f32[64,8,2047]{2,1,0:T(8,128)S(1)}, f32[64,8,2047]{2,1,0:T(8,128)}, f32[64,8,2047]{2,1,0:T(8,128)}, f32[64,8,2047]{2,1,0:T(8,128)}) fusion(f32[64,10,2048]{2,1,0:T(8,128)} %get-tuple-element.8, f32[64,10,2048]{2,1,0:T(8,128)} %get-tuple-element.9), kind=kLoop, calls=%fused_computation.38 | loop fusion | bytes 33538048 | tf_op jit(solution)/shard_map/jit(_roll_static)/slice | solution.py:47
  408.3 2.6 fusion.17
  410.9 9.3 %broadcast_multiply_fusion = (f32[64,10,2048]{2,1,0:T(8,128)}, f32[64,10,2048]{2,1,0:T(8,128)}) fusion(f32[10]{0:T(128)S(1)} %multiply_cosine_fusion, bf16[64,2,10,2048]{3,2,0,1:T(8,128)(2,1)} %pad_maximum_fusion), kind=kLoop, calls=%fused_computation.18 | loop fusion | flops 5242880 | bytes 15728680 | tf_op jit(solution)/shard_map/mul | solution.py:44
  420.3 18.3 %fusion.3 = (f32[64,8,2048]{2,1,0:T(8,128)}, f32[64,8,2048]{2,1,0:T(8,128)}) fusion(f32[64,10,2048]{2,1,0:T(8,128)} %get-tuple-element.2, f32[64,8,1]{2,1,0:T(8,128)} %get-tuple-element.5, f32[64,8,2047]{2,1,0:T(8,128)} %get-tuple-element.7, f32[64,8,2047]{2,1,0:T(8,128)S(1)} %get-tuple-element.6, f32[64,8,1]{2,1,0:T(8,128)S(1)} %get-tuple-element.4, ...), kind=kLoop, calls=%fused_computation.7 | loop fusion | flops 14680064 | bytes 42008608 | tf_op jit(solution)/shard_map/mul | solution.py:85
  (14 shorter events, 0.1 us)
Async XLA Ops:
  7.2 39.0 %copy-start = (f32[2,120,512]{2,1,0:T(8,128)S(1)}, f32[2,120,512]{2,1,0:T(8,128)}, u32[]{:S(2)}) copy-start(f32[2,120,512]{2,1,0:T(8,128)} %param.5) | copy-start | bytes 1474564
  7.2 308.4 %all-gather.3.cloned.1.call-start = ((), (), s32[]{:S(2)}) async-start(), calls=%async_computation | async-start | bytes 41943040 | tf_op jit(solution)/shard_map/all_gather | solution.py:67
  20.8 0.7 copy-start.4
  20.8 25.2 %copy-start.3 = (s32[8,2048]{1,0:T(8,128)S(1)}, s32[8,2048]{1,0:T(8,128)}, u32[]{:S(2)}) copy-start(s32[8,2048]{1,0:T(8,128)} %param.7) | copy-start | bytes 196612
  339.1 2.0 copy-start.2
  342.8 26.7 %collective-permute-start = (bf16[64,2,1,2048]{3,0,2,1:T(8,128)(2,1)S(1)}, bf16[64,2,1,2048]{3,0,2,1:T(8,128)(2,1)S(1)}, u32[]{:S(2)}, u32[]{:S(2)}) collective-permute-start(bf16[64,2,1,2048]{3,0,2,1:T(8,128)(2,1)S(1)} %copy.14), channel_id=1, source_target_pairs={{0,1},{1,2},{2,3},{3,4},{4,5},{5,6},{6,7},{7,8},{8,9},{9,10},{10,1... | collective-permute-start | bytes 1572872 | tf_op jit(solution)/shard_map/ppermute | solution.py:14
  347.7 22.6 %collective-permute-start.1 = (bf16[64,2,1,2048]{3,0,2,1:T(8,128)(2,1)S(1)}, bf16[64,2,1,2048]{3,0,2,1:T(8,128)(2,1)S(1)}, u32[]{:S(2)}, u32[]{:S(2)}) collective-permute-start(bf16[64,2,1,2048]{3,0,2,1:T(8,128)(2,1)S(1)} %copy.15), channel_id=1, source_target_pairs={{1,0},{2,1},{3,2},{4,3},{5,4},{6,5},{7,6},{8,7},{9,8},{10,9},{11,1... | collective-permute-start | bytes 1572872 | tf_op jit(solution)/shard_map/ppermute | solution.py:17
  420.3 18.3 %copy-start.1 = (f32[2,120,512]{2,1,0:T(8,128)S(1)}, f32[2,120,512]{2,1,0:T(8,128)}, u32[]{:S(2)}) copy-start(f32[2,120,512]{2,1,0:T(8,128)} %param.5) | copy-start | bytes 1474564
Sparse Core Ops, SparseCore 0:
  20.9 294.6 all-gather.2
where the time goes:
time: 448 us; the launch traced here: 445 us
  waiting for transfers between devices  289 us (65%)
  local copies, waits for them, and re-layouts  63 us (14%)
  other arithmetic  47.8 us (11%)
  matrix products  18.9 us (4%)
  between operations  14.2 us (3%)
  blocking collectives  6.29 us (1%)
  starting transfers between devices  6.02 us (1%)
    all_gather x1, waiting for transfers between devices, shards(): lax.all_gather(local_eof, 'tm', axis=1, tiled=True)  269 us
    ppermute x1, waiting for transfers between devices, padded_2(): lax.ppermute(lax.slice_in_dim(block, block.shape[dim] - width, None, axis...  20.2 us
    slice x2, local copies, waits for them, and re-layouts, curl_div(): jnp.roll(inner_east, 1, axis=2)  19.9 us
    dot_general x1, matrix products, shards(): jnp.einsum('tc,xcn->txn', own_rc, lax.all_gather(local_eof, 'tm', axis=1,...  18.5 us
    mul x1, other arithmetic, shards(): return (vorticity * ocean_mask[None], divergence * ocean_mask[None])  18.3 us
    gather x2, local copies, waits for them, and re-layouts, lagged_rc(): values_lag = jnp.where(inside[None], series[:, safe_index], 0.0)  18.1 us
    reshape x1, local copies, waits for them, and re-layouts, shards(): local_eof = spatial_eof.reshape(2, chan_share, cell_count)  13.6 us
    convert_element_type x1, other arithmetic, shards(): padded[:, 0].astype(jnp.float32)  11.3 us
  transfers between devices with their start and end apart: 3, of which 2 were waited for; matrix products, arithmetic and copies ran while one was open for 5% of the time, Pallas kernels for 0%

commit v1 on v0

v1 whole, which is shorter than its diff:
```python
import functools
import math

import jax
import jax.numpy as jnp
from jax import lax
from jax.experimental import pallas as pl
from jax.experimental.pallas import tpu as pltpu
from jax.sharding import PartitionSpec as P

F32 = jnp.float32
BF16 = jnp.bfloat16
VMEM = pltpu.VMEM
DAY_CHUNK = 16
LON_BLOCK = 512


def iota(shape, dim):
    return lax.broadcasted_iota(jnp.int32, shape, dim)


def components_kernel(place, pcs_ref, st_ref, comp_ref, all_ref):
    pairs, lags, _ = st_ref.shape
    days = pcs_ref.shape[1]
    share = comp_ref.shape[1] // 2
    window = jnp.minimum(iota((days, share), 0) + 1, lags).astype(F32)
    lagged = []
    for k in range(pairs):
        row = jnp.concatenate([jnp.zeros((1, 128), F32), pcs_ref[pl.ds(k, 1), :], jnp.zeros((1, 128), F32)], axis=1)
        wide = jnp.broadcast_to(row, (lags, days + 256))
        shifted = pltpu.roll(wide, 0, 1, stride=1, stride_axis=0)
        lagged.append(shifted[:, 128:128 + days].T)
    for half in range(2):
        first = pl.multiple_of(place[2 + half], share)
        total = jnp.zeros((days, share), F32)
        for k in range(pairs):
            total += jnp.dot(lagged[k], st_ref[k, :, pl.ds(first, share)], precision=lax.Precision.HIGHEST, preferred_element_type=F32)
        all_ref[...] = total / window
        count = comp_ref.shape[0] // 2
        for side in range(2):
            rows = all_ref[pl.ds(pl.multiple_of(place[side], count), count), :]
            comp_ref[side * count:(side + 1) * count, half * share:(half + 1) * share] = rows.astype(BF16)


def spread(comp, lat):
    share = comp.shape[1]
    shape = (share, share * lat)
    rep = jnp.where(iota(shape, 1) // lat == iota(shape, 0), 1.0, 0.0).astype(BF16)
    return jnp.dot(comp, rep, preferred_element_type=F32)


def only_row(wide, row, lat):
    return jnp.where(iota(wide.shape, 1) % lat == row, wide, 0.0).astype(BF16)


def edge_kernel(lat, comp_ref, own_ref, oth_ref, send_ref, keep_ref, x_ref):
    days, chans = comp_ref.shape
    share = chans // 2
    depth = share * lat

    @pl.when(pl.program_id(0) == 0)
    def _():
        for half in range(2):
            wide = spread(comp_ref[:, half * share:(half + 1) * share], lat)
            for side, row in enumerate((0, lat - 1)):
                x_ref[side * days:(side + 1) * days, half * depth:(half + 1) * depth] = only_row(wide, row, lat)

    acc = jnp.dot(x_ref[:, :depth], own_ref[0], preferred_element_type=F32)
    acc += jnp.dot(x_ref[:, depth:], oth_ref[0], preferred_element_type=F32)
    send_ref[...] = acc.astype(BF16)
    for side in range(2):
        keep_ref[side] = acc[side * days:side * days + days // 2]


def edge_call(comp, own, oth, x, lat, block):
    days = comp.shape[0]
    depth, lon = own.shape[1:]
    return pl.pallas_call(
        functools.partial(edge_kernel, lat),
        grid=(lon // block,),
        in_specs=[
            pl.BlockSpec(comp.shape, lambda n: (0, 0)),
            pl.BlockSpec((1, depth, block), lambda n: (x, 0, n)),
            pl.BlockSpec((1, depth, block), lambda n: (0, 0, n)),
        ],
        out_specs=[
            pl.BlockSpec((2 * days, block), lambda n: (0, n)),
            pl.BlockSpec((2, days // 2, block), lambda n: (0, 0, n)),
        ],
        out_shape=[
            jax.ShapeDtypeStruct((2 * days, lon), BF16),
            jax.ShapeDtypeStruct((2, days // 2, lon), F32),
        ],
        scratch_shapes=[VMEM((2 * days, 2 * depth), BF16)],
        compiler_params=pltpu.CompilerParams(vmem_limit_bytes=40 << 20),
        cost_estimate=pl.CostEstimate(flops=2 * 2 * days * 2 * depth * lon, bytes_accessed=4 * depth * lon + 8 * days * lon, transcendentals=0),
        name="edge_partials",
    )(comp, own, oth)


def inner_kernel(lat, first, chunk, comp_ref, own_ref, oth_u_ref, oth_v_ref, send_ref, keep_ref, x_ref):
    days, chans = comp_ref.shape
    share = chans // 2
    depth = share * lat
    inner = (lat - 2) * chunk

    @pl.when((pl.program_id(0) == 0) & (pl.program_id(1) == 0))
    def _():
        for half in range(2):
            chan = slice(half * share, (half + 1) * share)
            cols = slice(half * depth, (half + 1) * depth)
            wide = spread(comp_ref[first:first + chunk, chan], lat)
            for row in range(1, lat - 1):
                x_ref[(row - 1) * chunk:row * chunk, cols] = only_row(wide, row, lat)
            wide = spread(comp_ref[days // 2 + first:days // 2 + first + chunk, chan], lat)
            shape = (chunk, lat, depth)
            tall = jnp.where(iota(shape, 2) % lat == iota(shape, 1), jnp.broadcast_to(wide[:, None, :], shape), 0.0)
            x_ref[inner:, cols] = tall.reshape(chunk * lat, depth).astype(BF16)

    def add(oth_ref):
        acc = jnp.dot(x_ref[:, :depth], own_ref[0], preferred_element_type=F32)
        acc += jnp.dot(x_ref[:, depth:], oth_ref[0], preferred_element_type=F32)
        send_ref[0] = acc[:inner].astype(BF16)
        keep_ref[0] = acc[inner:]

    pl.when(pl.program_id(0) == 0)(lambda: add(oth_u_ref))
    pl.when(pl.program_id(0) == 1)(lambda: add(oth_v_ref))


def inner_call(comp, own, oth_u, oth_v, lat, first, chunk, block):
    depth, lon = own.shape[1:]
    steps = lon // block
    inner = (lat - 2) * chunk
    rows = inner + lat * chunk
    return pl.pallas_call(
        functools.partial(inner_kernel, lat, first, chunk),
        grid=(2, steps),
        in_specs=[
            pl.BlockSpec(comp.shape, lambda x, n: (0, 0)),
            pl.BlockSpec((1, depth, block), lambda x, n: (x, 0, n)),
            pl.BlockSpec((1, depth, block), lambda x, n: (0, 0, jnp.where(x == 0, n, steps - 1))),
            pl.BlockSpec((1, depth, block), lambda x, n: (0, 0, jnp.where(x == 1, n, 0))),
        ],
        out_specs=[
            pl.BlockSpec((1, inner, block), lambda x, n: (x, 0, n)),
            pl.BlockSpec((1, lat * chunk, block), lambda x, n: (x, 0, n)),
        ],
        out_shape=[
            jax.ShapeDtypeStruct((2, inner, lon), BF16),
            jax.ShapeDtypeStruct((2, lat * chunk, lon), F32),
        ],
        scratch_shapes=[VMEM((rows, 2 * depth), BF16)],
        compiler_params=pltpu.CompilerParams(vmem_limit_bytes=40 << 20),
        cost_estimate=pl.CostEstimate(flops=2 * rows * 2 * depth * 2 * lon, bytes_accessed=8 * depth * lon + 2 * lon * (2 * inner + 4 * lat * chunk), transcendentals=0),
        name="inner_partials",
    )(comp, own, oth_u, oth_v)


def select(shape, of_row, of_col):
    row, col = iota(shape, 0), iota(shape, 1)
    return jnp.where(of_row(row) == of_col(col), 1.0, 0.0).astype(BF16)


def curl_kernel(lat, chunk, keep_ref, inner_ref, edge_u_ref, edge_v_ref, low_u_ref, low_v_ref, high_u_ref, high_v_ref, land_ref, coef_ref, *rest):
    vort_ref, div_ref = rest[-2:]
    lon = land_ref.shape[1]
    rows = chunk * lat
    mask = land_ref[...].astype(F32)
    from_inner = select((rows, (lat - 2) * chunk), lambda r: (r % lat) * chunk + r // lat, lambda c: c + chunk)
    from_low = select((rows, chunk), lambda r: (r % lat) * chunk + r // lat, lambda c: c)
    from_high = select((rows, chunk), lambda r: (r % lat) * chunk + r // lat, lambda c: c + (lat - 1) * chunk)
    up = jnp.where(iota((rows, rows), 0) % lat < lat - 1, jnp.where(iota((rows, rows), 1) == iota((rows, rows), 0) + 1, 1.0, 0.0), 0.0).astype(BF16)
    down = jnp.where(iota((rows, rows), 0) % lat > 0, jnp.where(iota((rows, rows), 1) + 1 == iota((rows, rows), 0), 1.0, 0.0), 0.0).astype(BF16)
    dot = functools.partial(jnp.dot, preferred_element_type=F32)
    zonal, merid = [], []
    cos_up = coef_ref[0][None, :, :1]
    cos_down = coef_ref[1][None, :, :1]
    scale = coef_ref[2][None, :, :1] * mask[None]
    for x in range(2):
        edge_ref = (edge_u_ref, edge_v_ref)[x]
        total = keep_ref[x] + dot(from_inner, inner_ref[x]) + dot(from_low, edge_ref[0]) + dot(from_high, edge_ref[1])
        vel = (total.reshape(chunk, lat, lon) * mask[None]).reshape(rows, lon).astype(BF16)
        above = dot(up, vel) + dot(from_high, (high_u_ref, high_v_ref)[x][...])
        below = dot(down, vel) + dot(from_low, (low_u_ref, low_v_ref)[x][...])
        wide = vel.astype(F32)
        zonal.append((pltpu.roll(wide, lon - 1, 1) - pltpu.roll(wide, 1, 1)).reshape(chunk, lat, lon))
        merid.append(cos_up * above.reshape(chunk, lat, lon) - cos_down * below.reshape(chunk, lat, lon))
    vort_ref[...] = (zonal[1] - merid[0]) * scale
    div_ref[...] = (zonal[0] + merid[1]) * scale


def curl_call(keep, inner, edges, halos, land, coef, outs, lat, days, at, chunk):
    lon = land.shape[1]
    day_rows = pl.BlockSpec((chunk, lon), lambda i: (at, 0))
    whole = lambda shape: pl.BlockSpec(shape, lambda i: (0,) * len(shape))
    out_spec = pl.BlockSpec((chunk, lat, lon), lambda i: (at, 0, 0))
    return pl.pallas_call(
        functools.partial(curl_kernel, lat, chunk),
        grid=(1,),
        in_specs=[whole(keep.shape), whole(inner.shape)]
        + [pl.BlockSpec((2, chunk, lon), lambda i: (0, at, 0))] * 2
        + [day_rows] * 4
        + [whole(land.shape), whole(coef.shape)]
        + [pl.BlockSpec(memory_space=pl.ANY)] * len(outs),
        out_specs=[out_spec] * 2,
        out_shape=[jax.ShapeDtypeStruct((days, lat, lon), F32)] * 2,
        input_output_aliases={10: 0, 11: 1} if outs else {},
        compiler_params=pltpu.CompilerParams(vmem_limit_bytes=56 << 20),
        cost_estimate=pl.CostEstimate(flops=20 * 2 * chunk * lat * lon, bytes_accessed=20 * chunk * lat * lon, transcendentals=0),
        name="curl_div",
    )(keep, inner, *edges, *halos, land, coef, *outs)


def shards(pcs, st_eof, spatial_eof, land_sea):
    day_dev = pcs.shape[1]
    _, share, lat, lon = spatial_eof.shape
    depth = share * lat
    tm = lax.axis_index("tm")
    tiles = lax.axis_size("tile")
    tile = lax.axis_index("tile")
    swap_core = [(i, i ^ 1) for i in range(4)]
    swap_chip = [(i, i ^ 2) for i in range(4)]
    north = [(t * tiles + i, (t ^ 2) * tiles + i + 1) for t in range(4) for i in range(tiles - 1)]
    south = [(t * tiles + i + 1, (t ^ 2) * tiles + i) for t in range(4) for i in range(tiles - 1)]

    own = spatial_eof.reshape(2, depth, lon)
    oth_u = lax.ppermute(own[0:1], "tm", swap_core)
    oth_v = lax.ppermute(own[1:2], "tm", swap_core)

    all_pcs = lax.all_gather(pcs, "tm", axis=1, tiled=True)
    place = jnp.stack([(tm ^ 2) * day_dev, tm * day_dev, tm * share, (tm ^ 1) * share]).astype(jnp.int32)
    comp = pl.pallas_call(
        components_kernel,
        in_specs=[pl.BlockSpec(memory_space=pltpu.SMEM)] + [pl.BlockSpec(memory_space=VMEM)] * 2,
        out_specs=pl.BlockSpec(memory_space=VMEM),
        out_shape=jax.ShapeDtypeStruct((2 * day_dev, 2 * share), BF16),
        scratch_shapes=[VMEM((all_pcs.shape[1], share), F32)],
        compiler_params=pltpu.CompilerParams(vmem_limit_bytes=24 << 20),
        name="components",
    )(place, all_pcs, st_eof)

    edges, keeps = [], []
    for x, oth in enumerate((oth_u, oth_v)):
        send, keep = edge_call(comp, own, oth, x, lat, LON_BLOCK)
        edges.append(lax.ppermute(send, "tm", swap_chip).reshape(2, 2 * day_dev, lon))
        keeps.append(keep)

    inners = []
    for first in range(0, day_dev, DAY_CHUNK):
        send, keep = inner_call(comp, own, oth_u, oth_v, lat, first, DAY_CHUNK, LON_BLOCK)
        inners.append((lax.ppermute(send, "tm", swap_chip), keep))

    ends = jnp.stack([land_sea[0], land_sea[lat - 1]]).astype(F32)[:, None, :]
    lows, highs = [], []
    for x in range(2):
        sums = keeps[x] + edges[x][:, day_dev:].astype(F32)
        vel = (sums * ends).astype(BF16)
        lows.append(lax.ppermute(vel[1], ("tm", "tile"), north))
        highs.append(lax.ppermute(vel[0], ("tm", "tile"), south))

    rows = (tile * lat).astype(F32) + jnp.arange(-1, lat + 1, dtype=F32)
    latitude = (-70.0 + 140.0 * (rows + 0.5) / (lat * tiles)) * (math.pi / 180.0)
    cosine = jnp.cos(latitude)
    coef = jnp.stack([cosine[2:], cosine[:-2], 0.5 / cosine[1:-1]])
    coef = jnp.broadcast_to(coef[:, :, None], (3, lat, 128))

    outs = []
    for at, (inner, keep) in enumerate(inners):
        outs = curl_call(keep, inner, edges, lows + highs, land_sea, coef, outs, lat, day_dev, at, DAY_CHUNK)
    return tuple(outs)


def solution(mesh):
    return jax.shard_map(
        shards,
        mesh=mesh,
        in_specs=(P(None, "tm"), P(), P(None, "tm", "tile", None), P("tile", None)),
        out_specs=(P("tm", "tile", None), P("tm", "tile", None)),
        check_vma=False,
    )
```

time: 448 us -> 152 us (0.34)
  waiting for transfers between devices: 289 us -> 24.3 us
  Pallas kernels: 0 us -> 77.2 us
  local copies, waits for them, and re-layouts: 63 us -> 15.3 us
  other arithmetic: 47.8 us -> 0.53 us
  matrix products: 18.9 us -> 0 us
  starting transfers between devices: 6.02 us -> 19.7 us
  between operations: 14.2 us -> 0.89 us
  blocking collectives: 6.29 us -> 13.8 us
    all_gather x1 -> x0, waiting for transfers between devices: 269 us -> none  [shards(): lax.all_gather(local_eof, 'tm', axis=1, tiled=True)]
    pallas_call x0 -> x11, Pallas kernels: none -> 77.2 us  [the longest x4 42.9 us: inner_call(): pl.pallas_call(functools.partial(inner_kernel, lat, first, chunk), grid=(...]
    mul x3 -> x0, other arithmetic: 27.7 us -> none  [the longest x1 18.3 us: shards(): return (vorticity * ocean_mask[None], divergence * ocean_mask[None])]
    dot_general x2 -> x0, matrix products: 18.9 us -> none  [the longest x1 18.5 us: shards(): jnp.einsum('tc,xcn->txn', own_rc, lax.all_gather(local_eof, 'tm', axis=1,...]
    gather x2 -> x0, local copies, waits for them, and re-layouts: 18.1 us -> none  [lagged_rc(): values_lag = jnp.where(inside[None], series[:, safe_index], 0.0)]
    slice x3 -> x2, local copies, waits for them, and re-layouts: 21.4 us -> 7.13 us  [the longest x1 6.2 us: shards(): oth_v = lax.ppermute(own[1:2], 'tm', swap_core)]
    ppermute x2 -> x12, starting transfers between devices: 5.99 us -> 19.7 us  [the longest x2 10.8 us: shards(): lows.append(lax.ppermute(vel[1], ('tm', 'tile'), north))]
    reshape x1 -> x0, local copies, waits for them, and re-layouts: 13.6 us -> none  [shards(): local_eof = spatial_eof.reshape(2, chan_share, cell_count)]
  transfers between devices with their start and end apart: 3 -> 12, of which waited for: 2 -> 4; matrix products, arithmetic and copies ran while one was open for 5% -> 2% of each run, Pallas kernels for 0% -> 47%
where the time goes in v1:
time: 152 us
  Pallas kernels  77.2 us (51%)
  waiting for transfers between devices  24.3 us (16%)
  starting transfers between devices  19.7 us (13%)
  local copies, waits for them, and re-layouts  15.3 us (10%)
  blocking collectives  13.8 us (9%)
    pallas_call x4, Pallas kernels, inner_call(): pl.pallas_call(functools.partial(inner_kernel, lat, first, chunk), grid=(...  42.9 us
    pallas_call x4, Pallas kernels, curl_call(): pl.pallas_call(functools.partial(curl_kernel, lat, chunk), grid=(1,), in_...  21.4 us
    all_gather x1, blocking collectives, shards(): all_pcs = lax.all_gather(pcs, 'tm', axis=1, tiled=True)  13.8 us
    ppermute x2, waiting for transfers between devices, shards(): lows.append(lax.ppermute(vel[1], ('tm', 'tile'), north))  13 us
    pallas_call x2, Pallas kernels, edge_call(): pl.pallas_call(functools.partial(edge_kernel, lat), grid=(lon // block,),...  11.6 us
    ppermute x4, waiting for transfers between devices, shards(): inners.append((lax.ppermute(send, 'tm', swap_chip), keep))  11.3 us
    ppermute x2, starting transfers between devices, shards(): lows.append(lax.ppermute(vel[1], ('tm', 'tile'), north))  10.8 us
    unnamed x31, local copies, waits for them, and re-layouts  7.35 us
  transfers between devices with their start and end apart: 12, of which 4 were waited for; matrix products, arithmetic and copies ran while one was open for 2% of the time, Pallas kernels for 47%

profile of v1, /device:TPU:1, one launch (start us, length us, event | category | flops | bytes accessed | tf_op | source)
XLA Modules:
  0.0 151.7 jit_solution(3247044658694888585)
XLA Ops:
  0.6 6.2 %slice_bitcast_fusion = (bf16[1,1024,2048]{2,1,0:T(8,128)(2,1)}, bf16[1,1024,2048]{2,1,0:T(8,128)(2,1)}) fusion(bf16[2,128,8,2048]{3,2,1,0:T(8,128)(2,1)} %param.6), kind=kLoop, calls=%fused_computation | loop fusion | bytes 16777216 | tf_op jit(solution)/shard_map/slice | solution.py:228
  6.9 1.4 collective-permute-start.1
  8.3 13.8 %all-gather = f32[4,64,2]{1,2,0:T(2,128)S(1)} all-gather(f32[1,64,2]{1,2,0:T(2,128)S(1)} %bitcast.48), channel_id=1, replica_groups=mesh['tm'=4,'tile'=32] {'tm'}, dimensions={0}, use_global_device_ids=true | all-gather | bytes 2560 | tf_op jit(solution)/shard_map/all_gather | solution.py:230
  22.2 1.3 components.1.comp_ref
  23.5 0.9 fusion
  24.5 5.8 %edge_partials.3 = (bf16[256,2048]{1,0:T(8,128)(2,1)S(1)}, f32[2,64,2048]{2,1,0:T(8,128)S(1)}) custom-call(bf16[128,256]{1,0:T(8,128)(2,1)S(1)} %components.1.comp_ref, bf16[2,1024,2048]{2,1,0:T(8,128)(2,1)} %bitcast.32, bf16[1,1024,2048]{2,1,0:T(8,128)(2,1)} %collective-permute-done.1.oth_v_ref.oth_ref), custom_call_target="tpu_custom_call" | custom-call | flops 2147483648 | bytes 10485760 | tf_op jit(solution)/shard_map/edge_partials/pallas_call | solution.py:78
  30.3 1.8 %collective-permute-start.4 = (bf16[256,2048]{1,0:T(8,128)(2,1)S(1)}, bf16[256,2048]{1,0:T(8,128)(2,1)S(1)}, u32[]{:S(2)}, u32[]{:S(2)}) collective-permute-start(bf16[256,2048]{1,0:T(8,128)(2,1)S(1)} %get-tuple-element.23), channel_id=1, source_target_pairs={{0,64},{32,96},{64,0},{96,32},{1,65},{33,97},{65,1},{97,33},{2,66}... | collective-permute-start | bytes 3145736 | tf_op jit(solution)/shard_map/ppermute | solution.py:245
  32.1 5.8 %edge_partials.2 = (bf16[256,2048]{1,0:T(8,128)(2,1)S(1)}, f32[2,64,2048]{2,1,0:T(8,128)S(1)}) custom-call(bf16[128,256]{1,0:T(8,128)(2,1)S(1)} %components.1.comp_ref, bf16[2,1024,2048]{2,1,0:T(8,128)(2,1)} %bitcast.33, bf16[1,1024,2048]{2,1,0:T(8,128)(2,1)} %collective-permute-done.oth_u_ref.oth_ref), custom_call_target="tpu_custom_call" | custom-call | flops 2147483648 | bytes 10485760 | tf_op jit(solution)/shard_map/edge_partials/pallas_call | solution.py:78
  38.0 10.7 %inner_partials.7 = (bf16[2,96,2048]{2,1,0:T(8,128)(2,1)S(1)}, f32[2,128,2048]{2,1,0:T(8,128)S(1)}) custom-call(bf16[128,256]{1,0:T(8,128)(2,1)S(1)} %components.1.comp_ref, bf16[2,1024,2048]{2,1,0:T(8,128)(2,1)} %bitcast.34, bf16[1,1024,2048]{2,1,0:T(8,128)(2,1)} %collective-permute-done.oth_u_ref.oth_ref, ...), custom_call_target="tpu_custom_call" | custom-call | flops 3758096384 | bytes 19660800 | tf_op jit(solution)/shard_map/inner_partials/pallas_call | solution.py:135
  48.8 1.3 copy-done
  50.1 1.4 collective-permute-start.11
  51.5 10.7 %inner_partials.6 = (bf16[2,96,2048]{2,1,0:T(8,128)(2,1)S(1)}, f32[2,128,2048]{2,1,0:T(8,128)S(1)}) custom-call(bf16[128,256]{1,0:T(8,128)(2,1)S(1)} %components.1.comp_ref, bf16[2,1024,2048]{2,1,0:T(8,128)(2,1)} %bitcast.35, bf16[1,1024,2048]{2,1,0:T(8,128)(2,1)} %collective-permute-done.oth_u_ref.oth_ref, ...), custom_call_target="tpu_custom_call" | custom-call | flops 3758096384 | bytes 19660800 | tf_op jit(solution)/shard_map/inner_partials/pallas_call | solution.py:135
  62.3 1.4 copy-done.3
  63.7 10.7 %inner_partials.5 = (bf16[2,96,2048]{2,1,0:T(8,128)(2,1)S(1)}, f32[2,128,2048]{2,1,0:T(8,128)S(1)}) custom-call(bf16[128,256]{1,0:T(8,128)(2,1)S(1)} %components.1.comp_ref, bf16[2,1024,2048]{2,1,0:T(8,128)(2,1)} %bitcast.36, bf16[1,1024,2048]{2,1,0:T(8,128)(2,1)} %collective-permute-done.oth_u_ref.oth_ref, ...), custom_call_target="tpu_custom_call" | custom-call | flops 3758096384 | bytes 19660800 | tf_op jit(solution)/shard_map/inner_partials/pallas_call | solution.py:135
  74.4 1.4 copy-done.2
  75.8 1.4 collective-permute-start.9
  77.2 10.7 %inner_partials.4 = (bf16[2,96,2048]{2,1,0:T(8,128)(2,1)S(1)}, f32[2,128,2048]{2,1,0:T(8,128)S(1)}) custom-call(bf16[128,256]{1,0:T(8,128)(2,1)S(1)} %components.1.comp_ref, bf16[2,1024,2048]{2,1,0:T(8,128)(2,1)} %bitcast.37, bf16[1,1024,2048]{2,1,0:T(8,128)(2,1)} %collective-permute-done.oth_u_ref.oth_ref, ...), custom_call_target="tpu_custom_call" | custom-call | flops 3758096384 | bytes 19660800 | tf_op jit(solution)/shard_map/inner_partials/pallas_call | solution.py:135
  88.0 1.3 copy-done.1
  89.7 1.3 collective-permute-start.8
  91.0 3.8 %collective-permute-done.11.inner_ref = bf16[2,96,2048]{2,1,0:T(8,128)(2,1)S(1)} collective-permute-done((bf16[2,96,2048]{2,1,0:T(8,128)(2,1)S(1)}, bf16[2,96,2048]{2,1,0:T(8,128)(2,1)S(1)}, u32[]{:S(2)}, u32[]{:S(2)}) %collective-permute-start.11) | collective-permute-done | bytes 786464 | tf_op jit(solution)/shard_map/ppermute | solution.py:251
  94.8 5.2 %collective-permute-start.6 = (bf16[64,2048]{1,0:T(8,128)(2,1)S(1)}, bf16[64,2048]{1,0:T(8,128)(2,1)S(1)}, u32[]{:S(2)}, u32[]{:S(2)}) collective-permute-start(bf16[64,2048]{1,0:T(8,128)(2,1)S(1)} %get-tuple-element.41), channel_id=1, source_target_pairs={{0,65},{1,66},{2,67},{3,68},{4,69},{5,70},{6,71},{7,72},{8,73},{9,... | collective-permute-start | bytes 786440 | tf_op jit(solution)/shard_map/ppermute | solution.py:258
  100.1 1.3 collective-permute-start.7
  101.4 8.6 %collective-permute-done.6.low_v_ref = bf16[64,2048]{1,0:T(8,128)(2,1)S(1)} collective-permute-done((bf16[64,2048]{1,0:T(8,128)(2,1)S(1)}, bf16[64,2048]{1,0:T(8,128)(2,1)S(1)}, u32[]{:S(2)}, u32[]{:S(2)}) %collective-permute-start.6) | collective-permute-done | bytes 262176 | tf_op jit(solution)/shard_map/ppermute | solution.py:258
  110.0 5.6 %collective-permute-start.5 = (bf16[64,2048]{1,0:T(8,128)(2,1)S(1)}, bf16[64,2048]{1,0:T(8,128)(2,1)S(1)}, u32[]{:S(2)}, u32[]{:S(2)}) collective-permute-start(bf16[64,2048]{1,0:T(8,128)(2,1)S(1)} %get-tuple-element.43), channel_id=1, source_target_pairs={{0,65},{1,66},{2,67},{3,68},{4,69},{5,70},{6,71},{7,72},{8,73},{9,... | collective-permute-start | bytes 786440 | tf_op jit(solution)/shard_map/ppermute | solution.py:258
  115.8 4.4 %collective-permute-done.5.low_u_ref = bf16[64,2048]{1,0:T(8,128)(2,1)S(1)} collective-permute-done((bf16[64,2048]{1,0:T(8,128)(2,1)S(1)}, bf16[64,2048]{1,0:T(8,128)(2,1)S(1)}, u32[]{:S(2)}, u32[]{:S(2)}) %collective-permute-start.5) | collective-permute-done | bytes 262176 | tf_op jit(solution)/shard_map/ppermute | solution.py:258
  121.0 5.3 %curl_div.4 = (f32[64,8,2048]{2,1,0:T(8,128)}, f32[64,8,2048]{2,1,0:T(8,128)}) custom-call(f32[2,128,2048]{2,1,0:T(8,128)} %copy-done, bf16[2,96,2048]{2,1,0:T(8,128)(2,1)} %copy-done.11, bf16[2,128,2048]{2,1,0:T(8,128)(2,1)} %bitcast.44, bf16[2,128,2048]{2,1,0:T(8,128)(2,1)} %bitcast.39, bf16[64,2048]{1,0:T(8,128)(2,1)} %copy-done.10, ...), custom_call_target="tpu_custom_call" | custom-call | flops 10485760 | bytes 5242880 | tf_op jit(solution)/shard_map/curl_div/pallas_call | solution.py:197
  126.3 5.3 %curl_div.5 = (f32[64,8,2048]{2,1,0:T(8,128)}, f32[64,8,2048]{2,1,0:T(8,128)}) custom-call(f32[2,128,2048]{2,1,0:T(8,128)} %copy-done.3, bf16[2,96,2048]{2,1,0:T(8,128)(2,1)} %collective-permute-done.10.inner_ref, bf16[2,128,2048]{2,1,0:T(8,128)(2,1)} %bitcast.45, bf16[2,128,2048]{2,1,0:T(8,128)(2,1)} %bitcast.40, ...), custom_call_target="tpu_custom_call", output_to_operand_aliasing={{0}: (10, {}), {1}: (11, {})} | custom-call | flops 10485760 | bytes 5242880 | tf_op jit(solution)/shard_map/curl_div/pallas_call | solution.py:197
  131.7 0.9 copy-done.13
  132.6 5.4 %curl_div.6 = (f32[64,8,2048]{2,1,0:T(8,128)}, f32[64,8,2048]{2,1,0:T(8,128)}) custom-call(f32[2,128,2048]{2,1,0:T(8,128)} %copy-done.2, bf16[2,96,2048]{2,1,0:T(8,128)(2,1)} %copy-done.13, bf16[2,128,2048]{2,1,0:T(8,128)(2,1)} %bitcast.46, bf16[2,128,2048]{2,1,0:T(8,128)(2,1)} %bitcast.41, ...), custom_call_target="tpu_custom_call", output_to_operand_aliasing={{0}: (10, {}), {1}: (11, {})} | custom-call | flops 10485760 | bytes 5242880 | tf_op jit(solution)/shard_map/curl_div/pallas_call | solution.py:197
  138.0 7.4 %collective-permute-done.2.inner_ref = bf16[2,96,2048]{2,1,0:T(8,128)(2,1)S(1)} collective-permute-done((bf16[2,96,2048]{2,1,0:T(8,128)(2,1)S(1)}, bf16[2,96,2048]{2,1,0:T(8,128)(2,1)S(1)}, u32[]{:S(2)}, u32[]{:S(2)}) %collective-permute-start.2) | collective-permute-done | bytes 786464 | tf_op jit(solution)/shard_map/ppermute | solution.py:251
  145.4 0.9 copy-done.12
  146.3 5.3 %curl_div.7 = (f32[64,8,2048]{2,1,0:T(8,128)}, f32[64,8,2048]{2,1,0:T(8,128)}) custom-call(f32[2,128,2048]{2,1,0:T(8,128)} %copy-done.1, bf16[2,96,2048]{2,1,0:T(8,128)(2,1)} %copy-done.12, bf16[2,128,2048]{2,1,0:T(8,128)(2,1)} %bitcast.47, bf16[2,128,2048]{2,1,0:T(8,128)(2,1)} %bitcast.42, ...), custom_call_target="tpu_custom_call", output_to_operand_aliasing={{0}: (10, {}), {1}: (11, {})} | custom-call | flops 10485760 | bytes 5242880 | tf_op jit(solution)/shard_map/curl_div/pallas_call | solution.py:197
  (47 shorter events, 1.7 us)
Async XLA Ops:
  0.6 7.7 %copy-start.14 = (f32[2,64]{1,0:T(2,128)S(1)}, f32[2,64]{1,0:T(2,128)}, u32[]{:S(2)}) copy-start(f32[2,64]{1,0:T(2,128)} %param.4) | copy-start | bytes 1540
  0.6 21.6 %copy-start.4 = (f32[2,120,512]{2,1,0:T(8,128)S(1)}, f32[2,120,512]{2,1,0:T(8,128)}, u32[]{:S(2)}) copy-start(f32[2,120,512]{2,1,0:T(8,128)} %st_ref.1) | copy-start | bytes 1474564
  6.9 17.6 %collective-permute-start.1 = (bf16[1,1024,2048]{2,1,0:T(8,128)(2,1)}, bf16[1,1024,2048]{2,1,0:T(8,128)(2,1)}, u32[]{:S(2)}, u32[]{:S(2)}) collective-permute-start(bf16[1,1024,2048]{2,1,0:T(8,128)(2,1)} %get-tuple-element.38), channel_id=1, source_target_pairs={{0,32},{32,0},{64,96},{96,64},{1,33},{33,1},{65,97},{97,65},{2,34}... | collective-permute-start | bytes 12582920 | tf_op jit(solution)/shard_map/ppermute | solution.py:228
  8.3 23.8 %collective-permute-start = (bf16[1,1024,2048]{2,1,0:T(8,128)(2,1)}, bf16[1,1024,2048]{2,1,0:T(8,128)(2,1)}, u32[]{:S(2)}, u32[]{:S(2)}) collective-permute-start(bf16[1,1024,2048]{2,1,0:T(8,128)(2,1)} %get-tuple-element.39), channel_id=1, source_target_pairs={{0,32},{32,0},{64,96},{96,64},{1,33},{33,1},{65,97},{97,65},{2,34}... | collective-permute-start | bytes 12582920 | tf_op jit(solution)/shard_map/ppermute | solution.py:227
  30.3 59.0 %collective-permute-start.4 = (bf16[256,2048]{1,0:T(8,128)(2,1)S(1)}, bf16[256,2048]{1,0:T(8,128)(2,1)S(1)}, u32[]{:S(2)}, u32[]{:S(2)}) collective-permute-start(bf16[256,2048]{1,0:T(8,128)(2,1)S(1)} %get-tuple-element.23), channel_id=1, source_target_pairs={{0,64},{32,96},{64,0},{96,32},{1,65},{33,97},{65,1},{97,33},{2,66}... | collective-permute-start | bytes 3145736 | tf_op jit(solution)/shard_map/ppermute | solution.py:245
  37.9 51.5 %collective-permute-start.3 = (bf16[256,2048]{1,0:T(8,128)(2,1)S(1)}, bf16[256,2048]{1,0:T(8,128)(2,1)S(1)}, u32[]{:S(2)}, u32[]{:S(2)}) collective-permute-start(bf16[256,2048]{1,0:T(8,128)(2,1)S(1)} %get-tuple-element.22), channel_id=1, source_target_pairs={{0,64},{32,96},{64,0},{96,32},{1,65},{33,97},{65,1},{97,33},{2,66}... | collective-permute-start | bytes 3145736 | tf_op jit(solution)/shard_map/ppermute | solution.py:245
  48.8 1.3 copy-start
  50.1 44.8 %collective-permute-start.11 = (bf16[2,96,2048]{2,1,0:T(8,128)(2,1)S(1)}, bf16[2,96,2048]{2,1,0:T(8,128)(2,1)S(1)}, u32[]{:S(2)}, u32[]{:S(2)}) collective-permute-start(bf16[2,96,2048]{2,1,0:T(8,128)(2,1)S(1)} %get-tuple-element.31), channel_id=1, source_target_pairs={{0,64},{32,96},{64,0},{96,32},{1,65},{33,97},{65,1},{97,33},{2,66}... | collective-permute-start | bytes 2359304 | tf_op jit(solution)/shard_map/ppermute | solution.py:251
  62.2 1.4 copy-start.3
  63.6 62.7 %collective-permute-start.10 = (bf16[2,96,2048]{2,1,0:T(8,128)(2,1)S(1)}, bf16[2,96,2048]{2,1,0:T(8,128)(2,1)}, u32[]{:S(2)}, u32[]{:S(2)}) collective-permute-start(bf16[2,96,2048]{2,1,0:T(8,128)(2,1)S(1)} %get-tuple-element.29), channel_id=1, source_target_pairs={{0,64},{32,96},{64,0},{96,32},{1,65},{33,97},{65,1},{97,33},{2,66}... | collective-permute-start | bytes 2359304 | tf_op jit(solution)/shard_map/ppermute | solution.py:251
  74.4 1.4 copy-start.2
  75.8 55.9 %collective-permute-start.9 = (bf16[2,96,2048]{2,1,0:T(8,128)(2,1)S(1)}, bf16[2,96,2048]{2,1,0:T(8,128)(2,1)S(1)}, u32[]{:S(2)}, u32[]{:S(2)}) collective-permute-start(bf16[2,96,2048]{2,1,0:T(8,128)(2,1)S(1)} %get-tuple-element.27), channel_id=1, source_target_pairs={{0,64},{32,96},{64,0},{96,32},{1,65},{33,97},{65,1},{97,33},{2,66}... | collective-permute-start | bytes 2359304 | tf_op jit(solution)/shard_map/ppermute | solution.py:251
  87.9 1.4 copy-start.1
  89.3 31.6 %copy-start.5 = (bf16[256,2048]{1,0:T(8,128)(2,1)}, bf16[256,2048]{1,0:T(8,128)(2,1)S(1)}, u32[]{:S(2)}) copy-start(bf16[256,2048]{1,0:T(8,128)(2,1)S(1)} %collective-permute-done.4) | copy-start | bytes 3145732
  89.3 56.1 %collective-permute-start.2 = (bf16[2,96,2048]{2,1,0:T(8,128)(2,1)S(1)}, bf16[2,96,2048]{2,1,0:T(8,128)(2,1)S(1)}, u32[]{:S(2)}, u32[]{:S(2)}) collective-permute-start(bf16[2,96,2048]{2,1,0:T(8,128)(2,1)S(1)} %get-tuple-element.21), channel_id=1, source_target_pairs={{0,64},{32,96},{64,0},{96,32},{1,65},{33,97},{65,1},{97,33},{2,66}... | collective-permute-start | bytes 2359304 | tf_op jit(solution)/shard_map/ppermute | solution.py:251
  89.3 31.6 %copy-start.6 = (bf16[256,2048]{1,0:T(8,128)(2,1)}, bf16[256,2048]{1,0:T(8,128)(2,1)S(1)}, u32[]{:S(2)}) copy-start(bf16[256,2048]{1,0:T(8,128)(2,1)S(1)} %collective-permute-done.3) | copy-start | bytes 3145732
  89.7 10.4 %collective-permute-start.8 = (bf16[64,2048]{1,0:T(8,128)(2,1)S(1)}, bf16[64,2048]{1,0:T(8,128)(2,1)S(1)}, u32[]{:S(2)}, u32[]{:S(2)}) collective-permute-start(bf16[64,2048]{1,0:T(8,128)(2,1)S(1)} %get-tuple-element.40), channel_id=1, source_target_pairs={{1,64},{2,65},{3,66},{4,67},{5,68},{6,69},{7,70},{8,71},{9,72},{10... | collective-permute-start | bytes 786440 | tf_op jit(solution)/shard_map/ppermute | solution.py:259
  94.8 26.1 %copy-start.11 = (bf16[2,96,2048]{2,1,0:T(8,128)(2,1)}, bf16[2,96,2048]{2,1,0:T(8,128)(2,1)S(1)}, u32[]{:S(2)}) copy-start(bf16[2,96,2048]{2,1,0:T(8,128)(2,1)S(1)} %collective-permute-done.11.inner_ref) | copy-start | bytes 2359300
  94.8 15.2 %collective-permute-start.6 = (bf16[64,2048]{1,0:T(8,128)(2,1)S(1)}, bf16[64,2048]{1,0:T(8,128)(2,1)S(1)}, u32[]{:S(2)}, u32[]{:S(2)}) collective-permute-start(bf16[64,2048]{1,0:T(8,128)(2,1)S(1)} %get-tuple-element.41), channel_id=1, source_target_pairs={{0,65},{1,66},{2,67},{3,68},{4,69},{5,70},{6,71},{7,72},{8,73},{9,... | collective-permute-start | bytes 786440 | tf_op jit(solution)/shard_map/ppermute | solution.py:258
  100.1 20.8 %copy-start.7 = (bf16[64,2048]{1,0:T(8,128)(2,1)}, bf16[64,2048]{1,0:T(8,128)(2,1)S(1)}, u32[]{:S(2)}) copy-start(bf16[64,2048]{1,0:T(8,128)(2,1)S(1)} %collective-permute-done.8.high_v_ref) | copy-start | bytes 786436
  100.1 15.6 %collective-permute-start.7 = (bf16[64,2048]{1,0:T(8,128)(2,1)S(1)}, bf16[64,2048]{1,0:T(8,128)(2,1)S(1)}, u32[]{:S(2)}, u32[]{:S(2)}) collective-permute-start(bf16[64,2048]{1,0:T(8,128)(2,1)S(1)} %get-tuple-element.42), channel_id=1, source_target_pairs={{1,64},{2,65},{3,66},{4,67},{5,68},{6,69},{7,70},{8,71},{9,72},{10... | collective-permute-start | bytes 786440 | tf_op jit(solution)/shard_map/ppermute | solution.py:259
  110.0 10.9 %copy-start.8 = (bf16[64,2048]{1,0:T(8,128)(2,1)}, bf16[64,2048]{1,0:T(8,128)(2,1)S(1)}, u32[]{:S(2)}) copy-start(bf16[64,2048]{1,0:T(8,128)(2,1)S(1)} %collective-permute-done.6.low_v_ref) | copy-start | bytes 786436
  110.0 10.2 %collective-permute-start.5 = (bf16[64,2048]{1,0:T(8,128)(2,1)S(1)}, bf16[64,2048]{1,0:T(8,128)(2,1)S(1)}, u32[]{:S(2)}, u32[]{:S(2)}) collective-permute-start(bf16[64,2048]{1,0:T(8,128)(2,1)S(1)} %get-tuple-element.43), channel_id=1, source_target_pairs={{0,65},{1,66},{2,67},{3,68},{4,69},{5,70},{6,71},{7,72},{8,73},{9,... | collective-permute-start | bytes 786440 | tf_op jit(solution)/shard_map/ppermute | solution.py:258
  115.8 5.2 %copy-start.9 = (bf16[64,2048]{1,0:T(8,128)(2,1)}, bf16[64,2048]{1,0:T(8,128)(2,1)S(1)}, u32[]{:S(2)}) copy-start(bf16[64,2048]{1,0:T(8,128)(2,1)S(1)} %collective-permute-done.7.high_u_ref) | copy-start | bytes 786436
  120.2 0.7 copy-start.10
  131.7 0.9 copy-start.13
  145.4 0.9 copy-start.12

commit v2 on v1

v2 whole, which is shorter than its diff:
```python
import functools
import math

import jax
import jax.numpy as jnp
from jax import lax
from jax.experimental import pallas as pl
from jax.experimental.pallas import tpu as pltpu
from jax.sharding import PartitionSpec as P

F32 = jnp.float32
BF16 = jnp.bfloat16
VMEM = pltpu.VMEM
DAY_GROUPS = (32, 24, 8)
SUB_DAYS = 8
LON_BLOCK = 512
PIECES = (1, 3)
BLOCK_DAYS = 16
VMEM_LIMIT = 40 << 20


def iota(shape, dim):
    return lax.broadcasted_iota(jnp.int32, shape, dim)


def after(value, *earlier):
    return lax.optimization_barrier((value, *earlier))[0]


def spread(comp, lat):
    share = comp.shape[1]
    shape = (share, share * lat)
    rep = jnp.where(iota(shape, 1) // lat == iota(shape, 0), 1.0, 0.0).astype(BF16)
    return jnp.dot(comp, rep, preferred_element_type=F32)


def only_row(wide, row, lat):
    return jnp.where(iota(wide.shape, 1) % lat == row, wide, 0.0).astype(BF16)


def components_kernel(lat, place, *refs):
    pcs_refs, (st_ref, comp_ref, edge_ref, all_ref) = refs[:-4], refs[-4:]
    pairs, lags, _ = st_ref.shape
    day_dev = pcs_refs[0].shape[1]
    days = day_dev * len(pcs_refs)
    share = comp_ref.shape[1] // 2
    count = comp_ref.shape[0] // 2
    depth = share * lat
    lane_owner = iota((pairs, days), 1) // day_dev
    series = jnp.zeros((pairs, days), F32)
    for other, ref in enumerate(pcs_refs):
        tiled = jnp.concatenate([ref[...]] * len(pcs_refs), axis=1)
        series = jnp.where(lane_owner == place[4] ^ other, tiled, series)
    window = jnp.minimum(iota((days, share), 0) + 1, lags).astype(F32)
    lagged = []
    for k in range(pairs):
        row = jnp.concatenate([jnp.zeros((1, 128), F32), series[k:k + 1], jnp.zeros((1, 128), F32)], axis=1)
        wide = jnp.broadcast_to(row, (lags, days + 256))
        shifted = pltpu.roll(wide, 0, 1, stride=1, stride_axis=0)
        lagged.append(shifted[:, 128:128 + days].T)
    for half in range(2):
        first = pl.multiple_of(place[2 + half], share)
        total = jnp.zeros((days, share), F32)
        for k in range(pairs):
            total += jnp.dot(lagged[k], st_ref[k, :, pl.ds(first, share)], precision=lax.Precision.HIGHEST, preferred_element_type=F32)
        all_ref[...] = total / window
        for side in range(2):
            rows = all_ref[pl.ds(pl.multiple_of(place[side], count), count), :].astype(BF16)
            comp_ref[side * count:(side + 1) * count, half * share:(half + 1) * share] = rows
            wide = spread(rows, lat)
            for end, row in enumerate((0, lat - 1)):
                at = (2 * end + side) * count
                edge_ref[at:at + count, half * depth:(half + 1) * depth] = only_row(wide, row, lat)


def components_call(place, pcs_all, st_eof, share, lat):
    day_dev = pcs_all[0].shape[1]
    return pl.pallas_call(
        functools.partial(components_kernel, lat),
        in_specs=[pl.BlockSpec(memory_space=pltpu.SMEM)] + [pl.BlockSpec(memory_space=VMEM)] * (len(pcs_all) + 1),
        out_specs=[pl.BlockSpec(memory_space=VMEM)] * 2,
        out_shape=[
            jax.ShapeDtypeStruct((2 * day_dev, 2 * share), BF16),
            jax.ShapeDtypeStruct((4 * day_dev, 2 * share * lat), BF16),
        ],
        scratch_shapes=[VMEM((len(pcs_all) * day_dev, share), F32)],
        compiler_params=pltpu.CompilerParams(vmem_limit_bytes=12 << 20),
        name="components",
    )(place, *pcs_all, st_eof)


def edge_kernel(x_ref, own_ref, oth_ref, send_ref, keep_ref):
    rows = x_ref.shape[0]
    depth = own_ref.shape[1]
    acc = jnp.dot(x_ref[:, :depth], own_ref[0], preferred_element_type=F32)
    acc += jnp.dot(x_ref[:, depth:], oth_ref[0], preferred_element_type=F32)
    send_ref[0] = acc.astype(BF16)
    for end in range(2):
        keep_ref[0, end] = acc[end * rows // 2:end * rows // 2 + rows // 4]


def edge_call(x_edge, own, oth, first, width, block):
    rows = x_edge.shape[0]
    depth = oth.shape[1]
    at = first // block
    return pl.pallas_call(
        edge_kernel,
        grid=(width // block, 2),
        in_specs=[
            pl.BlockSpec(x_edge.shape, lambda n, x: (0, 0)),
            pl.BlockSpec((1, depth, block), lambda n, x: (x, 0, at + n)),
            pl.BlockSpec((1, depth, block), lambda n, x: (x, 0, at + n)),
        ],
        out_specs=[
            pl.BlockSpec((1, rows, block), lambda n, x: (x, 0, n)),
            pl.BlockSpec((1, 2, rows // 4, block), lambda n, x: (x, 0, 0, n)),
        ],
        out_shape=[
            jax.ShapeDtypeStruct((2, rows, width), BF16),
            jax.ShapeDtypeStruct((2, 2, rows // 4, width), F32),
        ],
        compiler_params=pltpu.CompilerParams(vmem_limit_bytes=57 << 20),
        cost_estimate=pl.CostEstimate(flops=2 * rows * 2 * depth * 2 * width, bytes_accessed=8 * depth * width + 8 * rows * width, transcendentals=0),
        name="edge_partials",
    )(x_edge, own, oth)


def inner_kernel(lat, first, span, pieces, comp_ref, own_ref, *refs):
    oth_refs, (send_ref, keep_ref, x_ref) = refs[:len(pieces)], refs[len(pieces):]
    days, chans = comp_ref.shape
    share = chans // 2
    depth = share * lat
    cut = send_ref.shape[1]

    @pl.when((pl.program_id(0) == 0) & (pl.program_id(1) == 0))
    def _():
        for half in range(2):
            chan = slice(half * share, (half + 1) * share)
            cols = slice(half * depth, (half + 1) * depth)
            wide = spread(comp_ref[first:first + span, chan], lat)
            tall = []
            for day in range(0, span, SUB_DAYS):
                tall += [only_row(wide[day:day + SUB_DAYS], row, lat) for row in range(1, lat - 1)]
            for at in range(0, len(tall), 2):
                x_ref[at * SUB_DAYS:(at + 2) * SUB_DAYS, cols] = jnp.concatenate(tall[at:at + 2], axis=0)
            wide = spread(comp_ref[days // 2 + first:days // 2 + first + span, chan], lat)
            shape = (span, lat, depth)
            tall = jnp.where(iota(shape, 2) % lat == iota(shape, 1), jnp.broadcast_to(wide[:, None, :], shape), 0.0)
            x_ref[cut:, cols] = tall.reshape(span * lat, depth).astype(BF16)

    def add(oth_ref):
        acc = jnp.dot(x_ref[:, :depth], own_ref[0], preferred_element_type=F32)
        acc += jnp.dot(x_ref[:, depth:], oth_ref[0], preferred_element_type=F32)
        send_ref[0] = acc[:cut].astype(BF16)
        keep_ref[0] = acc[cut:]

    start = 0
    for ref, piece in zip(oth_refs, pieces):
        inside = (pl.program_id(0) >= start) & (pl.program_id(0) < start + piece)
        pl.when(inside)(functools.partial(add, ref))
        start += piece


def inner_call(comp, own, oths, lat, first, span, block):
    depth, lon = own.shape[1:]
    pieces = [oth.shape[2] // block for oth in oths]
    rows = span * (2 * lat - 2)

    def piece_spec(start, piece):
        def at(n, x):
            before, past = n < start, n >= start + piece
            block_at = jnp.clip(n - start, 0, piece - 1)
            return (jnp.where(before, 0, jnp.where(past, 1, x)), 0, block_at)
        return pl.BlockSpec((1, depth, block), at)

    kinds = (((lat - 2) * span, BF16), (lat * span, F32))
    return pl.pallas_call(
        functools.partial(inner_kernel, lat, first, span, pieces),
        grid=(lon // block, 2),
        in_specs=[
            pl.BlockSpec(comp.shape, lambda n, x: (0, 0)),
            pl.BlockSpec((1, depth, block), lambda n, x: (x, 0, n)),
        ] + [piece_spec(sum(pieces[:i]), piece) for i, piece in enumerate(pieces)],
        out_specs=[pl.BlockSpec((1, height, block), lambda n, x: (x, 0, n)) for height, _ in kinds],
        out_shape=[jax.ShapeDtypeStruct((2, height, lon), dtype) for height, dtype in kinds],
        scratch_shapes=[VMEM((rows, 2 * depth), BF16)],
        compiler_params=pltpu.CompilerParams(vmem_limit_bytes=VMEM_LIMIT),
        cost_estimate=pl.CostEstimate(flops=2 * rows * 2 * depth * 2 * lon, bytes_accessed=8 * depth * lon + 6 * lon * rows, transcendentals=0),
        name="inner_partials",
    )(comp, own, *oths)


def halo_kernel(count, land_ref, *refs):
    keeps, edges, (low_ref, high_ref) = refs[:count], refs[count:2 * count], refs[2 * count:]
    lat, lon = land_ref.shape
    days = low_ref.shape[1]
    start = 0
    for keep, edge in zip(keeps, edges):
        width = keep.shape[3]
        for end, out in ((lat - 1, low_ref), (0, high_ref)):
            side = int(end > 0)
            mask = land_ref[end:end + 1, start:start + width].astype(F32)
            for x in range(2):
                total = keep[x, side] + edge[x, (2 * side + 1) * days:(2 * side + 2) * days, :].astype(F32)
                out[x, :, start:start + width] = (total * mask).astype(BF16)
        start += width


def halo_call(land, keeps, edges):
    days = keeps[0].shape[2]
    shape = jax.ShapeDtypeStruct((2, days, land.shape[1]), BF16)
    return pl.pallas_call(
        functools.partial(halo_kernel, len(keeps)),
        in_specs=[pl.BlockSpec(memory_space=VMEM)] * (1 + 2 * len(keeps)),
        out_specs=[pl.BlockSpec(memory_space=VMEM)] * 2,
        out_shape=[shape] * 2,
        compiler_params=pltpu.CompilerParams(vmem_limit_bytes=VMEM_LIMIT),
        cost_estimate=pl.CostEstimate(flops=8 * days * land.shape[1], bytes_accessed=48 * days * land.shape[1], transcendentals=0),
        name="halo_rows",
    )(land, *keeps, *edges)


def select(shape, of_row, of_col):
    row, col = iota(shape, 0), iota(shape, 1)
    return jnp.where(of_row(row) == of_col(col), 1.0, 0.0).astype(BF16)


def curl_kernel(lat, first, count, keep_ref, inner_ref, low_ref, high_ref, land_ref, coef_ref, *rest):
    edges, (vort_ref, div_ref) = rest[:count], rest[-2:]
    lon = land_ref.shape[1]
    chunk = SUB_DAYS
    rows = chunk * lat
    seen = low_ref.shape[1]
    skip = (first + pl.program_id(0) * chunk) % seen
    mask = land_ref[...].astype(F32)
    from_inner = select((rows, (lat - 2) * chunk), lambda r: (r % lat) * chunk + r // lat, lambda c: c + chunk)
    from_low = select((rows, seen), lambda r: (r % lat) * seen + r // lat + skip, lambda c: c)
    from_high = select((rows, seen), lambda r: (r % lat) * seen + r // lat + skip, lambda c: c + (lat - 1) * seen)
    row, col = iota((rows, rows), 0), iota((rows, rows), 1)
    up = jnp.where(row % lat < lat - 1, jnp.where(col == row + 1, 1.0, 0.0), 0.0).astype(BF16)
    down = jnp.where(row % lat > 0, jnp.where(col + 1 == row, 1.0, 0.0), 0.0).astype(BF16)
    dot = functools.partial(jnp.dot, preferred_element_type=F32)
    zonal, merid = [], []
    cos_up = coef_ref[0][None, :, :1]
    cos_down = coef_ref[1][None, :, :1]
    scale = coef_ref[2][None, :, :1] * mask[None]
    for x in range(2):
        ends = [dot(from_low, e[x, 0]) + dot(from_high, e[x, 1]) for e in edges]
        total = keep_ref[x] + dot(from_inner, inner_ref[x]) + jnp.concatenate(ends, axis=1)
        vel = (total.reshape(chunk, lat, lon) * mask[None]).reshape(rows, lon).astype(BF16)
        above = dot(up, vel) + dot(from_high, high_ref[x])
        below = dot(down, vel) + dot(from_low, low_ref[x])
        wide = vel.astype(F32)
        zonal.append((pltpu.roll(wide, lon - 1, 1) - pltpu.roll(wide, 1, 1)).reshape(chunk, lat, lon))
        merid.append(cos_up * above.reshape(chunk, lat, lon) - cos_down * below.reshape(chunk, lat, lon))
    vort_ref[...] = (zonal[1] - merid[0]) * scale
    div_ref[...] = (zonal[0] + merid[1]) * scale


def curl_call(keep, inner, edges, halos, land, coef, outs, lat, days, first, span):
    lon = land.shape[1]
    per = BLOCK_DAYS // SUB_DAYS
    block = first // SUB_DAYS
    whole = lambda shape: pl.BlockSpec(shape, lambda i: (0,) * len(shape))
    out_spec = pl.BlockSpec((SUB_DAYS, lat, lon), lambda i: (block + i, 0, 0))
    return pl.pallas_call(
        functools.partial(curl_kernel, lat, first, len(edges)),
        grid=(span // SUB_DAYS,),
        in_specs=[
            pl.BlockSpec((2, lat * SUB_DAYS, lon), lambda i: (0, i, 0)),
            pl.BlockSpec((2, (lat - 2) * SUB_DAYS, lon), lambda i: (0, i, 0)),
        ]
        + [pl.BlockSpec((2, BLOCK_DAYS, lon), lambda i: (0, (block + i) // per, 0))] * 2
        + [whole(land.shape), whole(coef.shape)]
        + [pl.BlockSpec((2, 2, BLOCK_DAYS, e.shape[3]), lambda i: (0, 0, (block + i) // per, 0)) for e in edges]
        + [pl.BlockSpec(memory_space=pl.ANY)] * len(outs),
        out_specs=[out_spec] * 2,
        out_shape=[jax.ShapeDtypeStruct((days, lat, lon), F32)] * 2,
        input_output_aliases={6 + len(edges): 0, 7 + len(edges): 1} if outs else {},
        compiler_params=pltpu.CompilerParams(vmem_limit_bytes=VMEM_LIMIT),
        cost_estimate=pl.CostEstimate(flops=20 * 2 * span * lat * lon, bytes_accessed=20 * span * lat * lon, transcendentals=0),
        name="curl_div",
    )(keep, inner, *halos, land, coef, *edges, *outs)


def shards(pcs, st_eof, spatial_eof, land_sea):
    day_dev = pcs.shape[1]
    _, share, lat, lon = spatial_eof.shape
    depth = share * lat
    tm = lax.axis_index("tm")
    tiles = lax.axis_size("tile")
    tile = lax.axis_index("tile")
    swap_core = [(i, i ^ 1) for i in range(4)]
    swap_chip = [(i, i ^ 2) for i in range(4)]
    north = [(t * tiles + i, (t ^ 2) * tiles + i + 1) for t in range(4) for i in range(tiles - 1)]
    south = [(t * tiles + i + 1, (t ^ 2) * tiles + i) for t in range(4) for i in range(tiles - 1)]

    pcs_all = [pcs] + [lax.ppermute(pcs, "tm", [(i, i ^ s) for i in range(4)]) for s in (1, 2, 3)]
    own = spatial_eof.reshape(2, depth, lon)
    widths = [LON_BLOCK * piece for piece in PIECES]
    spans = [(sum(widths[:i]), width) for i, width in enumerate(widths)]
    oth = lax.ppermute(after(own, pcs_all[1]), "tm", swap_core)

    place = jnp.stack([(tm ^ 2) * day_dev, tm * day_dev, tm * share, (tm ^ 1) * share, tm]).astype(jnp.int32)
    comp, x_edge = components_call(place, pcs_all, st_eof, share, lat)

    edges, keeps = [], []
    for start, width in spans:
        send, keep = edge_call(x_edge, own, oth, start, width, LON_BLOCK)
        x_edge = after(x_edge, send)
        edges.append(lax.ppermute(send, "tm", swap_chip))
        keeps.append(keep)

    inners = []
    first = 0
    sent = list(edges)
    for span in DAY_GROUPS:
        comp = after(comp, send, sent[-2])
        if len(sent) == len(edges) + 1:
            low, high = halo_call(after(land_sea, send), keeps, edges)
            comp = after(comp, low)
            halos = [lax.ppermute(low, ("tm", "tile"), north), lax.ppermute(high, ("tm", "tile"), south)]
        send, keep = inner_call(comp, own, [oth], lat, first, span, LON_BLOCK)
        sent.append(lax.ppermute(send, "tm", swap_chip))
        inners.append((sent[-1], keep))
        first += span

    rows = (tile * lat).astype(F32) + jnp.arange(-1, lat + 1, dtype=F32)
    latitude = (-70.0 + 140.0 * (rows + 0.5) / (lat * tiles)) * (math.pi / 180.0)
    cosine = jnp.cos(latitude)
    coef = jnp.stack([cosine[2:], cosine[:-2], 0.5 / cosine[1:-1]])
    coef = jnp.broadcast_to(coef[:, :, None], (3, lat, 128))

    edges = [e.reshape(2, 2, 2 * day_dev, -1) for e in edges]
    outs = []
    first = 0
    for span, (inner, keep) in zip(DAY_GROUPS, inners):
        outs = curl_call(keep, inner, edges, halos, land_sea, coef, outs, lat, day_dev, first, span)
        first += span
    return tuple(outs)


def solution(mesh):
    return jax.shard_map(
        shards,
        mesh=mesh,
        in_specs=(P(None, "tm"), P(), P(None, "tm", "tile", None), P("tile", None)),
        out_specs=(P("tm", "tile", None), P("tm", "tile", None)),
        check_vma=False,
    )
```

time: 152 us -> 138 us (0.908)
  waiting for transfers between devices: 24.3 us -> 41.6 us
  blocking collectives: 13.8 us -> 0 us
  Pallas kernels: 77.2 us -> 63.8 us
  starting transfers between devices: 19.7 us -> 15.3 us
    ppermute x12 -> x11, waiting for transfers between devices: 24.3 us -> 41.6 us  [the longest x3 17.7 us: shards(): sent.append(lax.ppermute(send, 'tm', swap_chip))]
    all_gather x1 -> x0, blocking collectives: 13.8 us -> none  [shards(): all_pcs = lax.all_gather(pcs, 'tm', axis=1, tiled=True)]
    pallas_call x11 -> x10, Pallas kernels: 77.2 us -> 63.8 us  [the longest x3 32.6 us: inner_call(): pl.pallas_call(functools.partial(inner_kernel, lat, first, span, pieces),...]
    unnamed x31 -> x32, local copies, waits for them, and re-layouts: 7.35 us -> 15.6 us
    slice x2 -> x0, local copies, waits for them, and re-layouts: 7.13 us -> none  [the longest x1 6.2 us: shards(): oth_v = lax.ppermute(own[1:2], 'tm', swap_core)]
    ppermute x12 -> x11, starting transfers between devices: 19.7 us -> 15.3 us  [the longest x3 4.55 us: shards(): sent.append(lax.ppermute(send, 'tm', swap_chip))]
  transfers between devices with their start and end apart: 12 -> 11, of which waited for: 4 -> 9; matrix products, arithmetic and copies ran while one was open for 2% -> 0% of each run, Pallas kernels for 47% -> 42%
where the time goes in v2:
time: 138 us; the launch traced here: 137 us
  Pallas kernels  63.8 us (46%)
  waiting for transfers between devices  41.6 us (30%)
  local copies, waits for them, and re-layouts  15.7 us (11%)
  starting transfers between devices  15.3 us (11%)
    pallas_call x3, Pallas kernels, inner_call(): pl.pallas_call(functools.partial(inner_kernel, lat, first, span, pieces),...  32.6 us
    ppermute x3, waiting for transfers between devices, shards(): sent.append(lax.ppermute(send, 'tm', swap_chip))  17.7 us
    ppermute x2, waiting for transfers between devices, shards(): edges.append(lax.ppermute(send, 'tm', swap_chip))  16.5 us
    unnamed x32, local copies, waits for them, and re-layouts  15.6 us
    pallas_call x3, Pallas kernels, curl_call(): pl.pallas_call(functools.partial(curl_kernel, lat, first, len(edges)), gr...  15 us
    pallas_call x2, Pallas kernels, edge_call(): pl.pallas_call(edge_kernel, grid=(width // block, 2), in_specs=[pl.BlockS...  13.7 us
    ppermute x3, starting transfers between devices, shards(): sent.append(lax.ppermute(send, 'tm', swap_chip))  4.55 us
    ppermute x3, waiting for transfers between devices, shards(): lax.ppermute(pcs, 'tm', [(i, i ^ s) for i in range(4)])  4.11 us
  transfers between devices with their start and end apart: 11, of which 9 were waited for; matrix products, arithmetic and copies ran while one was open for 0% of the time, Pallas kernels for 42%

profile of v2, /device:TPU:1, one launch (start us, length us, event | category | flops | bytes accessed | tf_op | source)
XLA Modules:
  0.0 137.4 jit_solution(11401261139626065411)
XLA Ops:
  0.6 1.5 %collective-permute-start = (f32[2,64]{1,0:T(2,128)}, f32[2,64]{1,0:T(2,128)S(1)}, u32[]{:S(2)}, u32[]{:S(2)}) collective-permute-start(f32[2,64]{1,0:T(2,128)} %refs_0_.1), channel_id=1, source_target_pairs={{0,32},{32,0},{64,96},{96,64},{1,33},{33,1},{65,97},{97,65},{2,34}... | collective-permute-start | bytes 1544 | tf_op jit(solution)/shard_map/ppermute | solution.py:298
  2.1 1.0 collective-permute-done.refs_1_
  3.5 1.7 %collective-permute-start.1 = (f32[2,64]{1,0:T(2,128)}, f32[2,64]{1,0:T(2,128)S(1)}, u32[]{:S(2)}, u32[]{:S(2)}) collective-permute-start(f32[2,64]{1,0:T(2,128)} %refs_0_.1), channel_id=1, source_target_pairs={{0,64},{32,96},{64,0},{96,32},{1,65},{33,97},{65,1},{97,33},{2,66}... | collective-permute-start | bytes 1544 | tf_op jit(solution)/shard_map/ppermute | solution.py:298
  6.4 2.1 %collective-permute-done.2.refs_3_ = f32[2,64]{1,0:T(2,128)S(1)} collective-permute-done((f32[2,64]{1,0:T(2,128)}, f32[2,64]{1,0:T(2,128)S(1)}, u32[]{:S(2)}, u32[]{:S(2)}) %collective-permute-start.2) | collective-permute-done | bytes 544 | tf_op jit(solution)/shard_map/ppermute | solution.py:298
  8.5 1.0 copy-done.10
  10.2 2.2 %components.1 = (bf16[128,256]{1,0:T(8,128)(2,1)S(1)}, bf16[256,2048]{1,0:T(8,128)(2,1)S(1)}) custom-call(s32[5]{0:T(128)S(1)} %stack.35.place, f32[2,64]{1,0:T(2,128)S(1)} %copy-done.11, f32[2,64]{1,0:T(2,128)S(1)} %collective-permute-done.refs_1_, f32[2,64]{1,0:T(2,128)S(1)} %collective-permute-done.1.refs_2_, f32[2,64]{1,0:T(2,128)S(1)} %collective-permute-done.2.refs_3_, ...), custom_call_target="tpu_custom_call" | custom-call | tf_op jit(solution)/shard_map/components/pallas_call | solution.py:78
  13.4 3.3 %collective-permute-done.3.oth_ref.refs_0_ = bf16[2,1024,2048]{2,1,0:T(8,128)(2,1)} collective-permute-done((bf16[2,1024,2048]{2,1,0:T(8,128)(2,1)}, bf16[2,1024,2048]{2,1,0:T(8,128)(2,1)}, u32[]{:S(2)}, u32[]{:S(2)}) %collective-permute-start.3) | collective-permute-done | bytes 8388640 | tf_op jit(solution)/shard_map/ppermute | solution.py:302
  16.7 4.1 %edge_partials.2 = (bf16[2,256,512]{2,1,0:T(8,128)(2,1)}, f32[2,2,64,512]{3,2,1,0:T(8,128)}) custom-call(bf16[256,2048]{1,0:T(8,128)(2,1)} %copy-done.2, bf16[2,1024,2048]{2,1,0:T(8,128)(2,1)} %bitcast.15, bf16[2,1024,2048]{2,1,0:T(8,128)(2,1)} %collective-permute-done.3.oth_ref.refs_0_), custom_call_target="tpu_custom_call" | custom-call | flops 1073741824 | bytes 5242880 | tf_op jit(solution)/shard_map/edge_partials/pallas_call | solution.py:106
  20.8 1.7 %collective-permute-start.4 = (bf16[2,256,512]{2,1,0:T(8,128)(2,1)}, bf16[2,256,512]{2,1,0:T(8,128)(2,1)S(1)}, u32[]{:S(2)}, u32[]{:S(2)}) collective-permute-start(bf16[2,256,512]{2,1,0:T(8,128)(2,1)} %get-tuple-element.30), channel_id=1, source_target_pairs={{0,64},{32,96},{64,0},{96,32},{1,65},{33,97},{65,1},{97,33},{2,66}... | collective-permute-start | bytes 1572872 | tf_op jit(solution)/shard_map/ppermute | solution.py:311
  22.5 9.6 %edge_partials.3 = (bf16[2,256,1536]{2,1,0:T(8,128)(2,1)}, f32[2,2,64,1536]{3,2,1,0:T(8,128)}) custom-call(bf16[256,2048]{1,0:T(8,128)(2,1)} %copy-done.2, bf16[2,1024,2048]{2,1,0:T(8,128)(2,1)} %bitcast.16, bf16[2,1024,2048]{2,1,0:T(8,128)(2,1)} %collective-permute-done.3.oth_ref.refs_0_), custom_call_target="tpu_custom_call" | custom-call | flops 3221225472 | bytes 15728640 | tf_op jit(solution)/shard_map/edge_partials/pallas_call | solution.py:106
  32.1 2.6 %collective-permute-done.4.refs_2_ = bf16[2,256,512]{2,1,0:T(8,128)(2,1)S(1)} collective-permute-done((bf16[2,256,512]{2,1,0:T(8,128)(2,1)}, bf16[2,256,512]{2,1,0:T(8,128)(2,1)S(1)}, u32[]{:S(2)}, u32[]{:S(2)}) %collective-permute-start.4) | collective-permute-done | bytes 524320 | tf_op jit(solution)/shard_map/ppermute | solution.py:311
  34.7 3.4 %copy-done = bf16[2,128,8,2048]{3,2,1,0:T(8,128)(2,1)S(1)} copy-done((bf16[2,128,8,2048]{3,2,1,0:T(8,128)(2,1)S(1)}, bf16[2,128,8,2048]{3,2,1,0:T(8,128)(2,1)}, u32[]{:S(2)}) %copy-start) | copy-done | bytes 8388632
  38.1 12.7 %inner_partials.3 = (bf16[2,192,2048]{2,1,0:T(8,128)(2,1)}, f32[2,256,2048]{2,1,0:T(8,128)S(1)}) custom-call(bf16[128,256]{1,0:T(8,128)(2,1)S(1)} %get-tuple-element.42.comp_ref, bf16[2,1024,2048]{2,1,0:T(8,128)(2,1)S(1)} %bitcast.17, bf16[2,1024,2048]{2,1,0:T(8,128)(2,1)} %collective-permute-done.3.oth_ref.refs_0_), custom_call_target="tpu_custom_call" | custom-call | flops 7516192768 | bytes 22282240 | tf_op jit(solution)/shard_map/inner_partials/pallas_call | solution.py:177
  50.8 2.0 %copy-done.3 = f32[2,256,2048]{2,1,0:T(8,128)} copy-done((f32[2,256,2048]{2,1,0:T(8,128)}, f32[2,256,2048]{2,1,0:T(8,128)S(1)}, u32[]{:S(2)}) %copy-start.3) | copy-done | bytes 4194328
  52.8 1.2 collective-permute-start.6
  54.0 14.0 %collective-permute-done.5.refs_3_ = bf16[2,256,1536]{2,1,0:T(8,128)(2,1)S(1)} collective-permute-done((bf16[2,256,1536]{2,1,0:T(8,128)(2,1)}, bf16[2,256,1536]{2,1,0:T(8,128)(2,1)S(1)}, u32[]{:S(2)}, u32[]{:S(2)}) %collective-permute-start.5) | collective-permute-done | bytes 1572896 | tf_op jit(solution)/shard_map/ppermute | solution.py:311
  67.9 1.4 %copy-done.7 = f32[2,2,64,1536]{3,2,1,0:T(8,128)S(1)} copy-done((f32[2,2,64,1536]{3,2,1,0:T(8,128)S(1)}, f32[2,2,64,1536]{3,2,1,0:T(8,128)}, u32[]{:S(2)}) %copy-start.7) | copy-done | bytes 1572888
  69.4 1.0 copy-done.9
  70.7 11.5 %inner_partials.4 = (bf16[2,144,2048]{2,1,0:T(8,128)(2,1)}, f32[2,192,2048]{2,1,0:T(8,128)S(1)}) custom-call(bf16[128,256]{1,0:T(8,128)(2,1)S(1)} %get-tuple-element.42.comp_ref, bf16[2,1024,2048]{2,1,0:T(8,128)(2,1)S(1)} %bitcast.20, bf16[2,1024,2048]{2,1,0:T(8,128)(2,1)} %collective-permute-done.3.oth_ref.refs_0_), custom_call_target="tpu_custom_call" | custom-call | flops 5637144576 | bytes 20905984 | tf_op jit(solution)/shard_map/inner_partials/pallas_call | solution.py:177
  82.2 1.6 %copy-done.5 = f32[2,192,2048]{2,1,0:T(8,128)} copy-done((f32[2,192,2048]{2,1,0:T(8,128)}, f32[2,192,2048]{2,1,0:T(8,128)S(1)}, u32[]{:S(2)}) %copy-start.5) | copy-done | bytes 3145752
  83.8 1.7 %collective-permute-start.10 = (bf16[2,144,2048]{2,1,0:T(8,128)(2,1)}, bf16[2,144,2048]{2,1,0:T(8,128)(2,1)}, u32[]{:S(2)}, u32[]{:S(2)}) collective-permute-start(bf16[2,144,2048]{2,1,0:T(8,128)(2,1)} %get-tuple-element.41), channel_id=1, source_target_pairs={{0,64},{32,96},{64,0},{96,32},{1,65},{33,97},{65,1},{97,33},{2,66}... | collective-permute-start | bytes 3538952 | tf_op jit(solution)/shard_map/ppermute | solution.py:324
  85.5 4.1 %collective-permute-start.8 = (bf16[2,64,2048]{2,1,0:T(8,128)(2,1)}, bf16[2,64,2048]{2,1,0:T(8,128)(2,1)S(1)}, u32[]{:S(2)}, u32[]{:S(2)}) collective-permute-start(bf16[2,64,2048]{2,1,0:T(8,128)(2,1)} %copy-done.13), channel_id=1, source_target_pairs={{0,65},{1,66},{2,67},{3,68},{4,69},{5,70},{6,71},{7,72},{8,73},{9,... | collective-permute-start | bytes 1572872 | tf_op jit(solution)/shard_map/ppermute | solution.py:322
  89.6 1.3 collective-permute-start.9
  90.9 10.9 %collective-permute-done.6.inner_ref = bf16[2,192,2048]{2,1,0:T(8,128)(2,1)} collective-permute-done((bf16[2,192,2048]{2,1,0:T(8,128)(2,1)}, bf16[2,192,2048]{2,1,0:T(8,128)(2,1)}, u32[]{:S(2)}, u32[]{:S(2)}) %collective-permute-start.6) | collective-permute-done | bytes 1572896 | tf_op jit(solution)/shard_map/ppermute | solution.py:324
  101.8 3.4 %copy-done.1 = bf16[2,128,8,2048]{3,2,1,0:T(8,128)(2,1)S(1)} copy-done((bf16[2,128,8,2048]{3,2,1,0:T(8,128)(2,1)S(1)}, bf16[2,128,8,2048]{3,2,1,0:T(8,128)(2,1)}, u32[]{:S(2)}) %copy-start.1) | copy-done | bytes 8388632
  105.1 8.5 %inner_partials.5 = (bf16[2,48,2048]{2,1,0:T(8,128)(2,1)S(1)}, f32[2,64,2048]{2,1,0:T(8,128)S(1)}) custom-call(bf16[128,256]{1,0:T(8,128)(2,1)S(1)} %get-tuple-element.42.comp_ref, bf16[2,1024,2048]{2,1,0:T(8,128)(2,1)S(1)} %bitcast.21, bf16[2,1024,2048]{2,1,0:T(8,128)(2,1)} %collective-permute-done.3.oth_ref.refs_0_), custom_call_target="tpu_custom_call" | custom-call | flops 1879048192 | bytes 18153472 | tf_op jit(solution)/shard_map/inner_partials/pallas_call | solution.py:177
  113.6 1.7 %collective-permute-start.7 = (bf16[2,48,2048]{2,1,0:T(8,128)(2,1)S(1)}, bf16[2,48,2048]{2,1,0:T(8,128)(2,1)S(1)}, u32[]{:S(2)}, u32[]{:S(2)}) collective-permute-start(bf16[2,48,2048]{2,1,0:T(8,128)(2,1)S(1)} %get-tuple-element.44), channel_id=1, source_target_pairs={{0,64},{32,96},{64,0},{96,32},{1,65},{33,97},{65,1},{97,33},{2,66}... | collective-permute-start | bytes 1179656 | tf_op jit(solution)/shard_map/ppermute | solution.py:324
  115.6 7.2 %curl_div.3 = (f32[64,8,2048]{2,1,0:T(8,128)}, f32[64,8,2048]{2,1,0:T(8,128)}) custom-call(f32[2,256,2048]{2,1,0:T(8,128)S(1)} %copy-done.4, bf16[2,192,2048]{2,1,0:T(8,128)(2,1)} %collective-permute-done.6.inner_ref, bf16[2,64,2048]{2,1,0:T(8,128)(2,1)S(1)} %collective-permute-done.8.low_ref, bf16[2,64,2048]{2,1,0:T(8,128)(2,1)S(1)} %collective-permute-done.9.high_ref, ...), custom_call_target="tpu_custom_call" | custom-call | flops 20971520 | bytes 10485760 | tf_op jit(solution)/shard_map/curl_div/pallas_call | solution.py:266
  122.8 4.2 %collective-permute-done.10.inner_ref = bf16[2,144,2048]{2,1,0:T(8,128)(2,1)} collective-permute-done((bf16[2,144,2048]{2,1,0:T(8,128)(2,1)}, bf16[2,144,2048]{2,1,0:T(8,128)(2,1)}, u32[]{:S(2)}, u32[]{:S(2)}) %collective-permute-start.10) | collective-permute-done | bytes 1179680 | tf_op jit(solution)/shard_map/ppermute | solution.py:324
  127.0 5.7 %curl_div.4 = (f32[64,8,2048]{2,1,0:T(8,128)}, f32[64,8,2048]{2,1,0:T(8,128)}) custom-call(f32[2,192,2048]{2,1,0:T(8,128)S(1)} %copy-done.6, bf16[2,144,2048]{2,1,0:T(8,128)(2,1)} %collective-permute-done.10.inner_ref, bf16[2,64,2048]{2,1,0:T(8,128)(2,1)S(1)} %collective-permute-done.8.low_ref, ...), custom_call_target="tpu_custom_call", output_to_operand_aliasing={{0}: (8, {}), {1}: (9, {})} | custom-call | flops 15728640 | bytes 7864320 | tf_op jit(solution)/shard_map/curl_div/pallas_call | solution.py:266
  132.8 2.6 %collective-permute-done.7.inner_ref = bf16[2,48,2048]{2,1,0:T(8,128)(2,1)S(1)} collective-permute-done((bf16[2,48,2048]{2,1,0:T(8,128)(2,1)S(1)}, bf16[2,48,2048]{2,1,0:T(8,128)(2,1)S(1)}, u32[]{:S(2)}, u32[]{:S(2)}) %collective-permute-start.7) | collective-permute-done | bytes 393248 | tf_op jit(solution)/shard_map/ppermute | solution.py:324
  135.4 2.0 %curl_div.5 = (f32[64,8,2048]{2,1,0:T(8,128)}, f32[64,8,2048]{2,1,0:T(8,128)}) custom-call(f32[2,64,2048]{2,1,0:T(8,128)S(1)} %get-tuple-element.43.keep_ref, bf16[2,48,2048]{2,1,0:T(8,128)(2,1)S(1)} %collective-permute-done.7.inner_ref, bf16[2,64,2048]{2,1,0:T(8,128)(2,1)S(1)} %collective-permute-done.8.low_ref, ...), custom_call_target="tpu_custom_call", output_to_operand_aliasing={{0}: (8, {}), {1}: (9, {})} | custom-call | flops 5242880 | bytes 2621440 | tf_op jit(solution)/shard_map/curl_div/pallas_call | solution.py:266
  (38 shorter events, 3.6 us)
Async XLA Ops:
  0.6 2.5 %collective-permute-start = (f32[2,64]{1,0:T(2,128)}, f32[2,64]{1,0:T(2,128)S(1)}, u32[]{:S(2)}, u32[]{:S(2)}) collective-permute-start(f32[2,64]{1,0:T(2,128)} %refs_0_.1), channel_id=1, source_target_pairs={{0,32},{32,0},{64,96},{96,64},{1,33},{33,1},{65,97},{97,65},{2,34}... | collective-permute-start | bytes 1544 | tf_op jit(solution)/shard_map/ppermute | solution.py:298
  3.2 13.5 %collective-permute-start.3 = (bf16[2,1024,2048]{2,1,0:T(8,128)(2,1)}, bf16[2,1024,2048]{2,1,0:T(8,128)(2,1)}, u32[]{:S(2)}, u32[]{:S(2)}) collective-permute-start(bf16[2,1024,2048]{2,1,0:T(8,128)(2,1)} %bitcast.14), channel_id=1, source_target_pairs={{0,32},{32,0},{64,96},{96,64},{1,33},{33,1},{65,97},{97,65},{2,34}... | collective-permute-start | bytes 25165832 | tf_op jit(solution)/shard_map/ppermute | solution.py:302
  3.5 2.9 %collective-permute-start.1 = (f32[2,64]{1,0:T(2,128)}, f32[2,64]{1,0:T(2,128)S(1)}, u32[]{:S(2)}, u32[]{:S(2)}) collective-permute-start(f32[2,64]{1,0:T(2,128)} %refs_0_.1), channel_id=1, source_target_pairs={{0,64},{32,96},{64,0},{96,32},{1,65},{33,97},{65,1},{97,33},{2,66}... | collective-permute-start | bytes 1544 | tf_op jit(solution)/shard_map/ppermute | solution.py:298
  5.2 3.3 %collective-permute-start.2 = (f32[2,64]{1,0:T(2,128)}, f32[2,64]{1,0:T(2,128)S(1)}, u32[]{:S(2)}, u32[]{:S(2)}) collective-permute-start(f32[2,64]{1,0:T(2,128)} %refs_0_.1), channel_id=1, source_target_pairs={{0,96},{32,64},{64,32},{96,0},{1,97},{33,65},{65,33},{97,1},{2,98}... | collective-permute-start | bytes 1544 | tf_op jit(solution)/shard_map/ppermute | solution.py:298
  8.5 1.0 copy-start.10
  9.5 0.7 copy-start.11
  12.4 1.0 copy-start.2
  20.8 14.0 %collective-permute-start.4 = (bf16[2,256,512]{2,1,0:T(8,128)(2,1)}, bf16[2,256,512]{2,1,0:T(8,128)(2,1)S(1)}, u32[]{:S(2)}, u32[]{:S(2)}) collective-permute-start(bf16[2,256,512]{2,1,0:T(8,128)(2,1)} %get-tuple-element.30), channel_id=1, source_target_pairs={{0,64},{32,96},{64,0},{96,32},{1,65},{33,97},{65,1},{97,33},{2,66}... | collective-permute-start | bytes 1572872 | tf_op jit(solution)/shard_map/ppermute | solution.py:311
  22.5 48.2 %slice-start = ((s8[8388608]{0:T(1024)(128)(4,1)}), s8[4194304]{0:T(1024)(128)(4,1)S(1)}, s32[]{:S(2)}) async-start(s8[8388608]{0:T(1024)(128)(4,1)} %bitcast.18), calls=%async_computation | async-start | bytes 8388608
  32.1 35.8 %collective-permute-start.5 = (bf16[2,256,1536]{2,1,0:T(8,128)(2,1)}, bf16[2,256,1536]{2,1,0:T(8,128)(2,1)S(1)}, u32[]{:S(2)}, u32[]{:S(2)}) collective-permute-start(bf16[2,256,1536]{2,1,0:T(8,128)(2,1)} %get-tuple-element.32), channel_id=1, source_target_pairs={{0,64},{32,96},{64,0},{96,32},{1,65},{33,97},{65,1},{97,33},{2,66}... | collective-permute-start | bytes 4718600 | tf_op jit(solution)/shard_map/ppermute | solution.py:311
  34.7 3.4 %copy-start = (bf16[2,128,8,2048]{3,2,1,0:T(8,128)(2,1)S(1)}, bf16[2,128,8,2048]{3,2,1,0:T(8,128)(2,1)}, u32[]{:S(2)}) copy-start(bf16[2,128,8,2048]{3,2,1,0:T(8,128)(2,1)} %param.6) | copy-start | bytes 25165828
  38.1 29.8 %copy-start.8 = (s32[8,2048]{1,0:T(8,128)S(1)}, s32[8,2048]{1,0:T(8,128)}, u32[]{:S(2)}) copy-start(s32[8,2048]{1,0:T(8,128)} %land_ref.6) | copy-start | bytes 196612
  38.1 32.6 %slice-start.1 = ((s8[8388608]{0:T(1024)(128)(4,1)}), s8[4194304]{0:T(1024)(128)(4,1)S(1)}, s32[]{:S(2)}) async-start(s8[8388608]{0:T(1024)(128)(4,1)} %bitcast.18), calls=%async_computation.1 | async-start | bytes 8388608
  50.8 2.0 %copy-start.3 = (f32[2,256,2048]{2,1,0:T(8,128)}, f32[2,256,2048]{2,1,0:T(8,128)S(1)}, u32[]{:S(2)}) copy-start(f32[2,256,2048]{2,1,0:T(8,128)S(1)} %get-tuple-element.47.keep_ref) | copy-start | bytes 12582916
  52.8 48.9 %collective-permute-start.6 = (bf16[2,192,2048]{2,1,0:T(8,128)(2,1)}, bf16[2,192,2048]{2,1,0:T(8,128)(2,1)}, u32[]{:S(2)}, u32[]{:S(2)}) collective-permute-start(bf16[2,192,2048]{2,1,0:T(8,128)(2,1)} %get-tuple-element.34), channel_id=1, source_target_pairs={{0,64},{32,96},{64,0},{96,32},{1,65},{33,97},{65,1},{97,33},{2,66}... | collective-permute-start | bytes 4718600 | tf_op jit(solution)/shard_map/ppermute | solution.py:324
  67.9 1.4 %copy-start.7 = (f32[2,2,64,1536]{3,2,1,0:T(8,128)S(1)}, f32[2,2,64,1536]{3,2,1,0:T(8,128)}, u32[]{:S(2)}) copy-start(f32[2,2,64,1536]{3,2,1,0:T(8,128)} %get-tuple-element.38.refs_1_) | copy-start | bytes 4718596
  69.4 1.0 copy-start.9
  70.6 11.5 %copy-start.12 = (bf16[2,64,2048]{2,1,0:T(8,128)(2,1)}, bf16[2,64,2048]{2,1,0:T(8,128)(2,1)S(1)}, u32[]{:S(2)}) copy-start(bf16[2,64,2048]{2,1,0:T(8,128)(2,1)S(1)} %get-tuple-element.45) | copy-start | bytes 1572868
  70.7 11.5 %copy-start.13 = (bf16[2,64,2048]{2,1,0:T(8,128)(2,1)}, bf16[2,64,2048]{2,1,0:T(8,128)(2,1)S(1)}, u32[]{:S(2)}) copy-start(bf16[2,64,2048]{2,1,0:T(8,128)(2,1)S(1)} %get-tuple-element.39) | copy-start | bytes 1572868
  82.2 1.6 %copy-start.5 = (f32[2,192,2048]{2,1,0:T(8,128)}, f32[2,192,2048]{2,1,0:T(8,128)S(1)}, u32[]{:S(2)}) copy-start(f32[2,192,2048]{2,1,0:T(8,128)S(1)} %get-tuple-element.46.keep_ref) | copy-start | bytes 9437188
  83.8 43.2 %collective-permute-start.10 = (bf16[2,144,2048]{2,1,0:T(8,128)(2,1)}, bf16[2,144,2048]{2,1,0:T(8,128)(2,1)}, u32[]{:S(2)}, u32[]{:S(2)}) collective-permute-start(bf16[2,144,2048]{2,1,0:T(8,128)(2,1)} %get-tuple-element.41), channel_id=1, source_target_pairs={{0,64},{32,96},{64,0},{96,32},{1,65},{33,97},{65,1},{97,33},{2,66}... | collective-permute-start | bytes 3538952 | tf_op jit(solution)/shard_map/ppermute | solution.py:324
  85.5 30.0 %collective-permute-start.8 = (bf16[2,64,2048]{2,1,0:T(8,128)(2,1)}, bf16[2,64,2048]{2,1,0:T(8,128)(2,1)S(1)}, u32[]{:S(2)}, u32[]{:S(2)}) collective-permute-start(bf16[2,64,2048]{2,1,0:T(8,128)(2,1)} %copy-done.13), channel_id=1, source_target_pairs={{0,65},{1,66},{2,67},{3,68},{4,69},{5,70},{6,71},{7,72},{8,73},{9,... | collective-permute-start | bytes 1572872 | tf_op jit(solution)/shard_map/ppermute | solution.py:322
  89.6 25.9 %collective-permute-start.9 = (bf16[2,64,2048]{2,1,0:T(8,128)(2,1)}, bf16[2,64,2048]{2,1,0:T(8,128)(2,1)S(1)}, u32[]{:S(2)}, u32[]{:S(2)}) collective-permute-start(bf16[2,64,2048]{2,1,0:T(8,128)(2,1)} %copy-done.12), channel_id=1, source_target_pairs={{1,64},{2,65},{3,66},{4,67},{5,68},{6,69},{7,70},{8,71},{9,72},{10... | collective-permute-start | bytes 1572872 | tf_op jit(solution)/shard_map/ppermute | solution.py:322
  101.8 3.4 %copy-start.1 = (bf16[2,128,8,2048]{3,2,1,0:T(8,128)(2,1)S(1)}, bf16[2,128,8,2048]{3,2,1,0:T(8,128)(2,1)}, u32[]{:S(2)}) copy-start(bf16[2,128,8,2048]{3,2,1,0:T(8,128)(2,1)} %param.6) | copy-start | bytes 25165828
  105.1 10.4 %copy-start.4 = (f32[2,256,2048]{2,1,0:T(8,128)S(1)}, f32[2,256,2048]{2,1,0:T(8,128)}, u32[]{:S(2)}) copy-start(f32[2,256,2048]{2,1,0:T(8,128)} %copy-done.3) | copy-start | bytes 12582916
  113.6 21.8 %collective-permute-start.7 = (bf16[2,48,2048]{2,1,0:T(8,128)(2,1)S(1)}, bf16[2,48,2048]{2,1,0:T(8,128)(2,1)S(1)}, u32[]{:S(2)}, u32[]{:S(2)}) collective-permute-start(bf16[2,48,2048]{2,1,0:T(8,128)(2,1)S(1)} %get-tuple-element.44), channel_id=1, source_target_pairs={{0,64},{32,96},{64,0},{96,32},{1,65},{33,97},{65,1},{97,33},{2,66}... | collective-permute-start | bytes 1179656 | tf_op jit(solution)/shard_map/ppermute | solution.py:324
  115.6 11.5 %copy-start.6 = (f32[2,192,2048]{2,1,0:T(8,128)S(1)}, f32[2,192,2048]{2,1,0:T(8,128)}, u32[]{:S(2)}) copy-start(f32[2,192,2048]{2,1,0:T(8,128)} %copy-done.5) | copy-start | bytes 9437188

commit v3 on v2

v3 whole, which is shorter than its diff:
```python
import functools
import math

import jax
import jax.numpy as jnp
from jax import lax
from jax.experimental import pallas as pl
from jax.experimental.pallas import tpu as pltpu
from jax.sharding import PartitionSpec as P

F32 = jnp.float32
BF16 = jnp.bfloat16
VMEM = pltpu.VMEM
DAY_GROUPS = (32, 24, 8)
SUB_DAYS = 8
GROUP = 32
LON_BLOCK = 512
BLOCK_DAYS = 16
VMEM_LIMIT = 40 << 20


def iota(shape, dim):
    return lax.broadcasted_iota(jnp.int32, shape, dim)


def after(value, *earlier):
    return lax.optimization_barrier((value, *earlier))[0]


def spread(comp, lat):
    share = comp.shape[1]
    shape = (share, share * lat)
    rep = jnp.where(iota(shape, 1) // lat == iota(shape, 0), 1.0, 0.0).astype(BF16)
    return jnp.dot(comp, rep, preferred_element_type=F32)


def only_row(wide, row, lat):
    return jnp.where(iota(wide.shape, 1) % lat == row, wide, 0.0).astype(BF16)


def components_kernel(place, *refs):
    pcs_refs, (st_ref, comp_ref, all_ref) = refs[:-3], refs[-3:]
    pairs, lags, _ = st_ref.shape
    day_dev = pcs_refs[0].shape[1]
    days = day_dev * len(pcs_refs)
    share = comp_ref.shape[1] // len(pcs_refs)
    count = comp_ref.shape[0] // 2
    lane_owner = iota((pairs, days), 1) // day_dev
    series = jnp.zeros((pairs, days), F32)
    for other, ref in enumerate(pcs_refs):
        tiled = jnp.concatenate([ref[...]] * len(pcs_refs), axis=1)
        series = jnp.where(lane_owner == place[2] ^ other, tiled, series)
    window = jnp.minimum(iota((days, share), 0) + 1, lags).astype(F32)
    lagged = []
    for k in range(pairs):
        row = jnp.concatenate([jnp.zeros((1, 128), F32), series[k:k + 1], jnp.zeros((1, 128), F32)], axis=1)
        wide = jnp.broadcast_to(row, (lags, days + 256))
        shifted = pltpu.roll(wide, 0, 1, stride=1, stride_axis=0)
        lagged.append(shifted[:, 128:128 + days].T)
    for half in range(len(pcs_refs)):
        first = pl.multiple_of((place[2] ^ half) * share, share)
        total = jnp.zeros((days, share), F32)
        for k in range(pairs):
            total += jnp.dot(lagged[k], st_ref[k, :, pl.ds(first, share)], precision=lax.Precision.HIGHEST, preferred_element_type=F32)
        all_ref[...] = total / window
        for side in range(2):
            rows = all_ref[pl.ds(pl.multiple_of(place[side], count), count), :].astype(BF16)
            comp_ref[side * count:(side + 1) * count, half * share:(half + 1) * share] = rows


def components_call(place, pcs_all, st_eof, share):
    day_dev = pcs_all[0].shape[1]
    return pl.pallas_call(
        components_kernel,
        in_specs=[pl.BlockSpec(memory_space=pltpu.SMEM)] + [pl.BlockSpec(memory_space=VMEM)] * (len(pcs_all) + 1),
        out_specs=pl.BlockSpec(memory_space=VMEM),
        out_shape=jax.ShapeDtypeStruct((2 * day_dev, len(pcs_all) * share), BF16),
        scratch_shapes=[VMEM((len(pcs_all) * day_dev, share), F32)],
        compiler_params=pltpu.CompilerParams(vmem_limit_bytes=12 << 20),
        cost_estimate=pl.CostEstimate(flops=0, bytes_accessed=128 << 20, transcendentals=0),
        name="components",
    )(place, *pcs_all, st_eof)


def pick_kernel(lat, *refs):
    groups, out_ref = refs[:-2], refs[-1]
    depth = groups[0].shape[1]
    chans = depth // lat
    row, col = iota((2 * chans, depth), 0), iota((2 * chans, depth), 1)
    wanted = (row % chans) * lat + (row // chans) * (lat - 1)
    pick = jnp.where(col == wanted, 1.0, 0.0).astype(BF16)
    for n, ref in enumerate(groups):
        found = jnp.dot(pick, ref[0], preferred_element_type=F32).astype(BF16)
        for end in range(2):
            out_ref[end, n * chans:(n + 1) * chans, :] = found[end * chans:(end + 1) * chans]


def pick_call(own, lat, x, token):
    _, depth, lon = own.shape
    share = depth // lat
    count = share // GROUP
    return pl.pallas_call(
        functools.partial(pick_kernel, lat),
        grid=(1,),
        in_specs=[pl.BlockSpec((1, GROUP * lat, lon), lambda i, n=n: (x, n, 0)) for n in range(count)]
        + [pl.BlockSpec(memory_space=pl.ANY)],
        out_specs=pl.BlockSpec((2, share, lon), lambda i: (0, 0, 0)),
        out_shape=jax.ShapeDtypeStruct((2, share, lon), BF16),
        compiler_params=pltpu.CompilerParams(vmem_limit_bytes=57 << 20),
        cost_estimate=pl.CostEstimate(flops=0, bytes_accessed=16 << 20, transcendentals=0),
        name="pick_end_rows",
    )(*[own] * count, token)


def edge_kernel(comp_ref, land_ref, *refs):
    parts, (low_ref, high_ref, ends_ref) = refs[:-3], refs[-3:]
    days = comp_ref.shape[0] // 2
    count = len(parts) // 2
    share = comp_ref.shape[1] // count
    lat = land_ref.shape[0]
    for x in range(2):
        for end in range(2):
            total = None
            for part in range(count):
                eof = parts[x * count + part][end]
                term = jnp.dot(comp_ref[:, part * share:(part + 1) * share], eof, preferred_element_type=F32)
                total = term if total is None else total + term
            at = end * (lat - 1)
            vel = (total * land_ref[at:at + 1, :].astype(F32)).astype(BF16)
            (high_ref, low_ref)[end][x] = vel[:days]
            ends_ref[x, end] = vel[days:]


def edge_call(comp, land, parts, block):
    days = comp.shape[0] // 2
    lat, lon = land.shape
    share = parts[0].shape[1]
    halo_spec = pl.BlockSpec((2, days, block), lambda n: (0, 0, n))
    halo_shape = jax.ShapeDtypeStruct((2, days, lon), BF16)
    return pl.pallas_call(
        edge_kernel,
        grid=(lon // block,),
        in_specs=[pl.BlockSpec(comp.shape, lambda n: (0, 0)), pl.BlockSpec((lat, block), lambda n: (0, n))]
        + [pl.BlockSpec((2, share, block), lambda n: (0, 0, n))] * len(parts),
        out_specs=[halo_spec, halo_spec, pl.BlockSpec((2, 2, days, block), lambda n: (0, 0, 0, n))],
        out_shape=[halo_shape, halo_shape, jax.ShapeDtypeStruct((2, 2, days, lon), BF16)],
        compiler_params=pltpu.CompilerParams(vmem_limit_bytes=24 << 20),
        name="end_rows",
    )(comp, land, *parts)


def inner_kernel(lat, first, span, comp_ref, own_ref, oth_ref, send_ref, keep_ref, x_ref):
    days = comp_ref.shape[0]
    depth = own_ref.shape[1]
    share = depth // lat
    cut = send_ref.shape[1]

    @pl.when((pl.program_id(0) == 0) & (pl.program_id(1) == 0))
    def _():
        for half in range(2):
            chan = slice(half * share, (half + 1) * share)
            cols = slice(half * depth, (half + 1) * depth)
            wide = spread(comp_ref[first:first + span, chan], lat)
            tall = []
            for day in range(0, span, SUB_DAYS):
                tall += [only_row(wide[day:day + SUB_DAYS], row, lat) for row in range(1, lat - 1)]
            for at in range(0, len(tall), 2):
                x_ref[at * SUB_DAYS:(at + 2) * SUB_DAYS, cols] = jnp.concatenate(tall[at:at + 2], axis=0)
            wide = spread(comp_ref[days // 2 + first:days // 2 + first + span, chan], lat)
            shape = (span, lat, depth)
            tall = jnp.where(iota(shape, 2) % lat == iota(shape, 1), jnp.broadcast_to(wide[:, None, :], shape), 0.0)
            x_ref[cut:, cols] = tall.reshape(span * lat, depth).astype(BF16)

    acc = jnp.dot(x_ref[:, :depth], own_ref[0], preferred_element_type=F32)
    acc += jnp.dot(x_ref[:, depth:], oth_ref[0], preferred_element_type=F32)
    send_ref[0] = acc[:cut].astype(BF16)
    keep_ref[0] = acc[cut:]


def inner_call(comp, own, oth, lat, lon, first, span, block):
    depth = own.shape[1]
    rows = span * (2 * lat - 2)

    kinds = (((lat - 2) * span, BF16), (lat * span, F32))
    return pl.pallas_call(
        functools.partial(inner_kernel, lat, first, span),
        grid=(lon // block, 2),
        in_specs=[
            pl.BlockSpec(comp.shape, lambda n, x: (0, 0)),
            pl.BlockSpec((1, depth, block), lambda n, x: (x, 0, n)),
            pl.BlockSpec((1, depth, block), lambda n, x: (x, 0, n)),
        ],
        out_specs=[pl.BlockSpec((1, height, block), lambda n, x: (x, 0, n)) for height, _ in kinds],
        out_shape=[jax.ShapeDtypeStruct((2, height, lon), dtype) for height, dtype in kinds],
        scratch_shapes=[VMEM((rows, 2 * depth), BF16)],
        compiler_params=pltpu.CompilerParams(vmem_limit_bytes=VMEM_LIMIT),
        cost_estimate=pl.CostEstimate(flops=2 * rows * 2 * depth * 2 * lon, bytes_accessed=8 * depth * lon + 6 * lon * rows, transcendentals=0),
        name="inner_partials",
    )(comp, own, oth)


def select(shape, of_row, of_col):
    row, col = iota(shape, 0), iota(shape, 1)
    return jnp.where(of_row(row) == of_col(col), 1.0, 0.0).astype(BF16)


def curl_kernel(lat, first, keep_ref, inner_ref, low_ref, high_ref, ends_ref, land_ref, coef_ref, *rest):
    vort_ref, div_ref = rest[-2:]
    lon = land_ref.shape[1]
    chunk = SUB_DAYS
    rows = chunk * lat
    seen = low_ref.shape[1]
    skip = (first + pl.program_id(0) * chunk) % seen
    mask = land_ref[...].astype(F32)
    from_inner = select((rows, (lat - 2) * chunk), lambda r: (r % lat) * chunk + r // lat, lambda c: c + chunk)
    from_low = select((rows, seen), lambda r: (r % lat) * seen + r // lat + skip, lambda c: c)
    from_high = select((rows, seen), lambda r: (r % lat) * seen + r // lat + skip, lambda c: c + (lat - 1) * seen)
    row, col = iota((rows, rows), 0), iota((rows, rows), 1)
    up = jnp.where(row % lat < lat - 1, jnp.where(col == row + 1, 1.0, 0.0), 0.0).astype(BF16)
    down = jnp.where(row % lat > 0, jnp.where(col + 1 == row, 1.0, 0.0), 0.0).astype(BF16)
    dot = functools.partial(jnp.dot, preferred_element_type=F32)
    row = iota(mask.shape, 0)
    inner_mask = jnp.where((row > 0) & (row < lat - 1), mask, 0.0)[None]
    zonal, merid = [], []
    cos_up = coef_ref[0][None, :, :1]
    cos_down = coef_ref[1][None, :, :1]
    scale = coef_ref[2][None, :, :1] * mask[None]
    for x in range(2):
        total = keep_ref[x] + dot(from_inner, inner_ref[x])
        vel = (total.reshape(chunk, lat, lon) * inner_mask).astype(BF16).astype(F32).reshape(rows, lon)
        wide = vel + dot(from_low, ends_ref[x, 0]) + dot(from_high, ends_ref[x, 1])
        vel = wide.astype(BF16)
        above = dot(up, vel) + dot(from_high, high_ref[x])
        below = dot(down, vel) + dot(from_low, low_ref[x])
        zonal.append((pltpu.roll(wide, lon - 1, 1) - pltpu.roll(wide, 1, 1)).reshape(chunk, lat, lon))
        merid.append(cos_up * above.reshape(chunk, lat, lon) - cos_down * below.reshape(chunk, lat, lon))
    vort_ref[...] = (zonal[1] - merid[0]) * scale
    div_ref[...] = (zonal[0] + merid[1]) * scale


def curl_call(keep, inner, ends, halos, land, coef, outs, lat, days, first, span):
    lon = land.shape[1]
    per = BLOCK_DAYS // SUB_DAYS
    block = first // SUB_DAYS
    whole = lambda shape: pl.BlockSpec(shape, lambda i: (0,) * len(shape))
    out_spec = pl.BlockSpec((SUB_DAYS, lat, lon), lambda i: (block + i, 0, 0))
    return pl.pallas_call(
        functools.partial(curl_kernel, lat, first),
        grid=(span // SUB_DAYS,),
        in_specs=[
            pl.BlockSpec((2, lat * SUB_DAYS, lon), lambda i: (0, i, 0)),
            pl.BlockSpec((2, (lat - 2) * SUB_DAYS, lon), lambda i: (0, i, 0)),
        ]
        + [pl.BlockSpec((2, BLOCK_DAYS, lon), lambda i: (0, (block + i) // per, 0))] * 2
        + [pl.BlockSpec((2, 2, BLOCK_DAYS, lon), lambda i: (0, 0, (block + i) // per, 0))]
        + [whole(land.shape), whole(coef.shape)]
        + [pl.BlockSpec(memory_space=pl.ANY)] * len(outs),
        out_specs=[out_spec] * 2,
        out_shape=[jax.ShapeDtypeStruct((days, lat, lon), F32)] * 2,
        input_output_aliases={7: 0, 8: 1} if outs else {},
        compiler_params=pltpu.CompilerParams(vmem_limit_bytes=VMEM_LIMIT),
        cost_estimate=pl.CostEstimate(flops=20 * 2 * span * lat * lon, bytes_accessed=20 * span * lat * lon, transcendentals=0),
        name="curl_div",
    )(keep, inner, *halos, ends, land, coef, *outs)


def shards(pcs, st_eof, spatial_eof, land_sea):
    day_dev = pcs.shape[1]
    _, share, lat, lon = spatial_eof.shape
    depth = share * lat
    tm = lax.axis_index("tm")
    tiles = lax.axis_size("tile")
    tile = lax.axis_index("tile")
    swap_core = [(i, i ^ 1) for i in range(4)]
    swap_chip = [(i, i ^ 2) for i in range(4)]
    north = [(t * tiles + i, (t ^ 2) * tiles + i + 1) for t in range(4) for i in range(tiles - 1)]
    south = [(t * tiles + i + 1, (t ^ 2) * tiles + i) for t in range(4) for i in range(tiles - 1)]

    pcs_all = [pcs] + [lax.ppermute(pcs, "tm", [(i, i ^ s) for i in range(4)]) for s in (1, 2, 3)]
    own = spatial_eof.reshape(2, depth, lon)
    mine = [pick_call(own, lat, 0, pcs_all[1])]
    mine.append(pick_call(own, lat, 1, mine[0]))
    crossed = [lax.ppermute(after(m, *pcs_all[2:]), "tm", swap_chip) for m in mine]
    swapped = [lax.ppermute(m, "tm", swap_core) for m in mine]
    oth = lax.ppermute(after(own, pcs_all[1]), "tm", swap_core)

    place = jnp.stack([(tm ^ 2) * day_dev, tm * day_dev, tm]).astype(jnp.int32)
    comp = components_call(after(place, mine[1]), pcs_all, st_eof, share)

    inners, across = [], []
    first = 0
    for i, span in enumerate(DAY_GROUPS):
        send, keep = inner_call(comp, own, oth, lat, lon, first, span, LON_BLOCK)
        inners.append((lax.ppermute(send, "tm", swap_chip), keep))
        first += span
        if i < 2:
            across.append(lax.ppermute(after(crossed[i], send), "tm", swap_core))
            comp = after(comp, send, across[i])
        if i == 1:
            parts = [a for x in range(2) for a in (mine[x], swapped[x], crossed[x], across[x])]
            low, high, ends = edge_call(comp, land_sea, parts, LON_BLOCK)
            halos = [lax.ppermute(low, ("tm", "tile"), north), lax.ppermute(high, ("tm", "tile"), south)]
            comp = after(comp, low, inners[0][0])

    rows = (tile * lat).astype(F32) + jnp.arange(-1, lat + 1, dtype=F32)
    latitude = (-70.0 + 140.0 * (rows + 0.5) / (lat * tiles)) * (math.pi / 180.0)
    cosine = jnp.cos(latitude)
    coef = jnp.stack([cosine[2:], cosine[:-2], 0.5 / cosine[1:-1]])
    coef = jnp.broadcast_to(coef[:, :, None], (3, lat, 128))

    outs = []
    first = 0
    for span, (inner, keep) in zip(DAY_GROUPS, inners):
        outs = curl_call(keep, inner, ends, halos, land_sea, coef, outs, lat, day_dev, first, span)
        first += span
    return tuple(outs)


def solution(mesh):
    return jax.shard_map(
        shards,
        mesh=mesh,
        in_specs=(P(None, "tm"), P(), P(None, "tm", "tile", None), P("tile", None)),
        out_specs=(P("tm", "tile", None), P("tm", "tile", None)),
        check_vma=False,
    )
```

time: 138 us -> 131 us (0.949)
  waiting for transfers between devices: 41.6 us -> 34.2 us
  starting transfers between devices: 15.3 us -> 19.3 us
  Pallas kernels: 63.8 us -> 61.3 us
  local copies, waits for them, and re-layouts: 15.7 us -> 14 us
    ppermute x1, waiting for transfers between devices: 3.27 us -> 0.01 us  [shards(): oth = lax.ppermute(after(own, pcs_all[1]), 'tm', swap_core)]
    ppermute x3, waiting for transfers between devices: 4.11 us -> 1.04 us  [shards(): lax.ppermute(pcs, 'tm', [(i, i ^ s) for i in range(4)])]
    ppermute x5 -> x9, starting transfers between devices: 6.27 us -> 8.86 us  [the longest x2 3.26 us: shards(): lax.ppermute(after(m, *pcs_all[2:]), 'tm', swap_chip)]
    pallas_call x10, Pallas kernels: 63.8 us -> 61.3 us  [the longest x3 31.9 us: inner_call(): pl.pallas_call(functools.partial(inner_kernel, lat, first, span), grid=(l...]
    ppermute x5 -> x9, waiting for transfers between devices: 34.2 us -> 31.8 us  [the longest x3 18.7 us: shards(): inners.append((lax.ppermute(send, 'tm', swap_chip), keep))]
    unnamed x32 -> x34, local copies, waits for them, and re-layouts: 15.6 us -> 13.9 us
    ppermute x1, starting transfers between devices: 4.1 us -> 5.52 us  [shards(): lax.ppermute(low, ('tm', 'tile'), north)]
    ppermute x1, waiting for transfers between devices: 0.01 us -> 1.39 us  [shards(): lax.ppermute(high, ('tm', 'tile'), south)]
  transfers between devices with their start and end apart: 11 -> 15, of which waited for: 9 -> 9; matrix products, arithmetic and copies ran while one was open for 0% -> 0% of each run, Pallas kernels for 42% -> 46%
where the time goes in v3:
time: 131 us; the launch traced here: 130 us
  Pallas kernels  61.3 us (47%)
  waiting for transfers between devices  34.2 us (26%)
  starting transfers between devices  19.3 us (15%)
  local copies, waits for them, and re-layouts  14 us (11%)
    pallas_call x3, Pallas kernels, inner_call(): pl.pallas_call(functools.partial(inner_kernel, lat, first, span), grid=(l...  31.9 us
    ppermute x3, waiting for transfers between devices, shards(): inners.append((lax.ppermute(send, 'tm', swap_chip), keep))  18.7 us
    pallas_call x3, Pallas kernels, curl_call(): pl.pallas_call(functools.partial(curl_kernel, lat, first), grid=(span //...  14.7 us
    unnamed x34, local copies, waits for them, and re-layouts  13.9 us
    ppermute x2, waiting for transfers between devices, shards(): lax.ppermute(after(m, *pcs_all[2:]), 'tm', swap_chip)  8.8 us
    pallas_call x2, Pallas kernels, pick_call(): pl.pallas_call(functools.partial(pick_kernel, lat), grid=(1,), in_specs=[...  8.08 us
    ppermute x1, starting transfers between devices, shards(): lax.ppermute(low, ('tm', 'tile'), north)  5.52 us
    pallas_call x1, Pallas kernels, edge_call(): pl.pallas_call(edge_kernel, grid=(lon // block,), in_specs=[pl.BlockSpec(...  4.84 us
  transfers between devices with their start and end apart: 15, of which 9 were waited for; matrix products, arithmetic and copies ran while one was open for 0% of the time, Pallas kernels for 46%

profile of v3, /device:TPU:1, one launch (start us, length us, event | category | flops | bytes accessed | tf_op | source)
XLA Modules:
  0.0 129.8 jit_solution(2029568390361613501)
XLA Ops:
  0.6 1.5 %collective-permute-start = (f32[2,64]{1,0:T(2,128)}, f32[2,64]{1,0:T(2,128)S(1)}, u32[]{:S(2)}, u32[]{:S(2)}) collective-permute-start(f32[2,64]{1,0:T(2,128)} %refs_0_.1), channel_id=1, source_target_pairs={{0,32},{32,0},{64,96},{96,64},{1,33},{33,1},{65,97},{97,65},{2,34}... | collective-permute-start | bytes 1544 | tf_op jit(solution)/shard_map/ppermute | solution.py:279
  3.5 1.7 %collective-permute-start.1 = (f32[2,64]{1,0:T(2,128)}, f32[2,64]{1,0:T(2,128)S(1)}, u32[]{:S(2)}, u32[]{:S(2)}) collective-permute-start(f32[2,64]{1,0:T(2,128)} %refs_0_.1), channel_id=1, source_target_pairs={{0,64},{32,96},{64,0},{96,32},{1,65},{33,97},{65,1},{97,33},{2,66}... | collective-permute-start | bytes 1544 | tf_op jit(solution)/shard_map/ppermute | solution.py:279
  5.3 4.0 %pick_end_rows.2.refs_4_.refs_0_ = bf16[2,128,2048]{2,1,0:T(8,128)(2,1)} custom-call(bf16[2,1024,2048]{2,1,0:T(8,128)(2,1)} %bitcast.11, bf16[2,1024,2048]{2,1,0:T(8,128)(2,1)} %bitcast.12, bf16[2,1024,2048]{2,1,0:T(8,128)(2,1)} %bitcast.13, bf16[2,1024,2048]{2,1,0:T(8,128)(2,1)} %bitcast.14, f32[2,64]{1,0:T(2,128)} %copy-done.14), custom_call_target="tpu_custom_call" | custom-call | bytes 16777216 | tf_op jit(solution)/shard_map/pick_end_rows/pallas_call | solution.py:102
  9.3 1.8 %collective-permute-start.4 = (bf16[2,128,2048]{2,1,0:T(8,128)(2,1)}, bf16[2,128,2048]{2,1,0:T(8,128)(2,1)S(1)}, u32[]{:S(2)}, u32[]{:S(2)}) collective-permute-start(bf16[2,128,2048]{2,1,0:T(8,128)(2,1)} %pick_end_rows.2.refs_4_.refs_0_), channel_id=1, source_target_pairs={{0,64},{32,96},{64,0},{96,32},{1,65},{33,97},{65,1},{97,33},{2,66}... | collective-permute-start | bytes 3145736 | tf_op jit(solution)/shard_map/ppermute | solution.py:283
  11.2 4.1 %pick_end_rows.3.refs_4_ = bf16[2,128,2048]{2,1,0:T(8,128)(2,1)} custom-call(bf16[2,1024,2048]{2,1,0:T(8,128)(2,1)} %bitcast.15, bf16[2,1024,2048]{2,1,0:T(8,128)(2,1)} %bitcast.16, bf16[2,1024,2048]{2,1,0:T(8,128)(2,1)} %bitcast.17, bf16[2,1024,2048]{2,1,0:T(8,128)(2,1)} %bitcast.18, bf16[2,128,2048]{2,1,0:T(8,128)(2,1)} %pick_end_rows.2.refs_4_.refs_0_), custom_call_target="tpu_custom_call" | custom-call | bytes 16777216 | tf_op jit(solution)/shard_map/pick_end_rows/pallas_call | solution.py:102
  15.3 1.8 %components.1.comp_ref = bf16[128,512]{1,0:T(8,128)(2,1)S(1)} custom-call(s32[3]{0:T(128)S(1)} %pad_add_fusion.place, f32[2,64]{1,0:T(2,128)S(1)} %copy-done.16, f32[2,64]{1,0:T(2,128)S(1)} %copy-done.15, f32[2,64]{1,0:T(2,128)S(1)} %collective-permute-done.1.refs_2_, f32[2,64]{1,0:T(2,128)S(1)} %collective-permute-done.2.refs_3_, f32[2,120,512]{2,1,0:T(8,128)S(1)} %copy-done.13), custom_call_target="tpu_custom_call" | custom-call | bytes 134217728 | tf_op jit(solution)/shard_map/components/pallas_call | solution.py:73
  17.1 3.4 %copy-done = bf16[2,128,8,2048]{3,2,1,0:T(8,128)(2,1)S(1)} copy-done((bf16[2,128,8,2048]{3,2,1,0:T(8,128)(2,1)S(1)}, bf16[2,128,8,2048]{3,2,1,0:T(8,128)(2,1)}, u32[]{:S(2)}) %copy-start) | copy-done | bytes 8388632
  20.4 12.4 %inner_partials.3 = (bf16[2,192,2048]{2,1,0:T(8,128)(2,1)}, f32[2,256,2048]{2,1,0:T(8,128)S(1)}) custom-call(bf16[128,512]{1,0:T(8,128)(2,1)S(1)} %components.1.comp_ref, bf16[2,1024,2048]{2,1,0:T(8,128)(2,1)S(1)} %bitcast.19, bf16[2,1024,2048]{2,1,0:T(8,128)(2,1)} %collective-permute-done.3.oth_ref), custom_call_target="tpu_custom_call" | custom-call | flops 7516192768 | bytes 22282240 | tf_op jit(solution)/shard_map/inner_partials/pallas_call | solution.py:185
  32.9 2.0 %copy-done.3 = f32[2,256,2048]{2,1,0:T(8,128)} copy-done((f32[2,256,2048]{2,1,0:T(8,128)}, f32[2,256,2048]{2,1,0:T(8,128)S(1)}, u32[]{:S(2)}) %copy-start.3) | copy-done | bytes 4194328
  35.4 1.5 %collective-permute-start.6 = (bf16[2,128,2048]{2,1,0:T(8,128)(2,1)S(1)}, bf16[2,128,2048]{2,1,0:T(8,128)(2,1)}, u32[]{:S(2)}, u32[]{:S(2)}) collective-permute-start(bf16[2,128,2048]{2,1,0:T(8,128)(2,1)S(1)} %copy-done.5), channel_id=1, source_target_pairs={{0,64},{32,96},{64,0},{96,32},{1,65},{33,97},{65,1},{97,33},{2,66}... | collective-permute-start | bytes 3145736 | tf_op jit(solution)/shard_map/ppermute | solution.py:283
  38.7 11.1 %inner_partials.4 = (bf16[2,144,2048]{2,1,0:T(8,128)(2,1)}, f32[2,192,2048]{2,1,0:T(8,128)S(1)}) custom-call(bf16[128,512]{1,0:T(8,128)(2,1)S(1)} %components.1.comp_ref, bf16[2,1024,2048]{2,1,0:T(8,128)(2,1)S(1)} %bitcast.20, bf16[2,1024,2048]{2,1,0:T(8,128)(2,1)} %collective-permute-done.3.oth_ref), custom_call_target="tpu_custom_call" | custom-call | flops 5637144576 | bytes 20905984 | tf_op jit(solution)/shard_map/inner_partials/pallas_call | solution.py:185
  49.8 1.6 %copy-done.6 = f32[2,192,2048]{2,1,0:T(8,128)} copy-done((f32[2,192,2048]{2,1,0:T(8,128)}, f32[2,192,2048]{2,1,0:T(8,128)S(1)}, u32[]{:S(2)}) %copy-start.6) | copy-done | bytes 3145752
  51.5 8.8 %collective-permute-done.6.refs_6_ = bf16[2,128,2048]{2,1,0:T(8,128)(2,1)} collective-permute-done((bf16[2,128,2048]{2,1,0:T(8,128)(2,1)S(1)}, bf16[2,128,2048]{2,1,0:T(8,128)(2,1)}, u32[]{:S(2)}, u32[]{:S(2)}) %collective-permute-start.6) | collective-permute-done | bytes 1048608 | tf_op jit(solution)/shard_map/ppermute | solution.py:283
  60.3 1.3 %collective-permute-start.7 = (bf16[2,128,2048]{2,1,0:T(8,128)(2,1)}, bf16[2,128,2048]{2,1,0:T(8,128)(2,1)}, u32[]{:S(2)}, u32[]{:S(2)}) collective-permute-start(bf16[2,128,2048]{2,1,0:T(8,128)(2,1)} %collective-permute-done.6.refs_6_), channel_id=1, source_target_pairs={{0,32},{32,0},{64,96},{96,64},{1,33},{33,1},{65,97},{97,65},{2,34}... | collective-permute-start | bytes 3145736 | tf_op jit(solution)/shard_map/ppermute | solution.py:297
  62.1 1.5 %collective-permute-start.14 = (bf16[2,144,2048]{2,1,0:T(8,128)(2,1)}, bf16[2,144,2048]{2,1,0:T(8,128)(2,1)S(1)}, u32[]{:S(2)}, u32[]{:S(2)}) collective-permute-start(bf16[2,144,2048]{2,1,0:T(8,128)(2,1)} %get-tuple-element.30), channel_id=1, source_target_pairs={{0,64},{32,96},{64,0},{96,32},{1,65},{33,97},{65,1},{97,33},{2,66}... | collective-permute-start | bytes 3538952 | tf_op jit(solution)/shard_map/ppermute | solution.py:294
  63.6 2.1 %collective-permute-done.7.refs_7_ = bf16[2,128,2048]{2,1,0:T(8,128)(2,1)} collective-permute-done((bf16[2,128,2048]{2,1,0:T(8,128)(2,1)}, bf16[2,128,2048]{2,1,0:T(8,128)(2,1)}, u32[]{:S(2)}, u32[]{:S(2)}) %collective-permute-start.7) | collective-permute-done | bytes 1048608 | tf_op jit(solution)/shard_map/ppermute | solution.py:297
  65.7 1.4 %collective-permute-done.9.refs_5_ = bf16[2,128,2048]{2,1,0:T(8,128)(2,1)} collective-permute-done((bf16[2,128,2048]{2,1,0:T(8,128)(2,1)S(1)}, bf16[2,128,2048]{2,1,0:T(8,128)(2,1)}, u32[]{:S(2)}, u32[]{:S(2)}) %collective-permute-start.9) | collective-permute-done | bytes 1048608 | tf_op jit(solution)/shard_map/ppermute | solution.py:284
  67.0 1.2 copy-done.10
  68.3 1.2 copy-done.12
  69.5 4.8 %end_rows.1 = (bf16[2,64,2048]{2,1,0:T(8,128)(2,1)S(1)}, bf16[2,64,2048]{2,1,0:T(8,128)(2,1)S(1)}, bf16[2,2,64,2048]{3,2,1,0:T(8,128)(2,1)S(1)}) custom-call(bf16[128,512]{1,0:T(8,128)(2,1)S(1)} %components.1.comp_ref, s32[8,2048]{1,0:T(8,128)S(1)} %copy-done.8, bf16[2,128,2048]{2,1,0:T(8,128)(2,1)S(1)} %copy-done.2, ...), custom_call_target="tpu_custom_call" | custom-call | tf_op jit(solution)/shard_map/end_rows/pallas_call | solution.py:140
  74.3 5.5 %collective-permute-start.12 = (bf16[2,64,2048]{2,1,0:T(8,128)(2,1)S(1)}, bf16[2,64,2048]{2,1,0:T(8,128)(2,1)S(1)}, u32[]{:S(2)}, u32[]{:S(2)}) collective-permute-start(bf16[2,64,2048]{2,1,0:T(8,128)(2,1)S(1)} %get-tuple-element.34), channel_id=1, source_target_pairs={{0,65},{1,66},{2,67},{3,68},{4,69},{5,70},{6,71},{7,72},{8,73},{9,... | collective-permute-start | bytes 1572872 | tf_op jit(solution)/shard_map/ppermute | solution.py:302
  79.9 14.1 %collective-permute-done.10.inner_ref = bf16[2,192,2048]{2,1,0:T(8,128)(2,1)} collective-permute-done((bf16[2,192,2048]{2,1,0:T(8,128)(2,1)}, bf16[2,192,2048]{2,1,0:T(8,128)(2,1)}, u32[]{:S(2)}, u32[]{:S(2)}) %collective-permute-start.10) | collective-permute-done | bytes 1572896 | tf_op jit(solution)/shard_map/ppermute | solution.py:294
  94.0 1.3 collective-permute-start.13
  95.3 3.4 %copy-done.1 = bf16[2,128,8,2048]{3,2,1,0:T(8,128)(2,1)S(1)} copy-done((bf16[2,128,8,2048]{3,2,1,0:T(8,128)(2,1)S(1)}, bf16[2,128,8,2048]{3,2,1,0:T(8,128)(2,1)}, u32[]{:S(2)}) %copy-start.1) | copy-done | bytes 8388632
  98.6 8.4 %inner_partials.5 = (bf16[2,48,2048]{2,1,0:T(8,128)(2,1)S(1)}, f32[2,64,2048]{2,1,0:T(8,128)S(1)}) custom-call(bf16[128,512]{1,0:T(8,128)(2,1)S(1)} %components.1.comp_ref, bf16[2,1024,2048]{2,1,0:T(8,128)(2,1)S(1)} %bitcast.21, bf16[2,1024,2048]{2,1,0:T(8,128)(2,1)} %collective-permute-done.3.oth_ref), custom_call_target="tpu_custom_call" | custom-call | flops 1879048192 | bytes 18153472 | tf_op jit(solution)/shard_map/inner_partials/pallas_call | solution.py:185
  107.1 1.7 %collective-permute-start.11 = (bf16[2,48,2048]{2,1,0:T(8,128)(2,1)S(1)}, bf16[2,48,2048]{2,1,0:T(8,128)(2,1)S(1)}, u32[]{:S(2)}, u32[]{:S(2)}) collective-permute-start(bf16[2,48,2048]{2,1,0:T(8,128)(2,1)S(1)} %get-tuple-element.37), channel_id=1, source_target_pairs={{0,64},{32,96},{64,0},{96,32},{1,65},{33,97},{65,1},{97,33},{2,66}... | collective-permute-start | bytes 1179656 | tf_op jit(solution)/shard_map/ppermute | solution.py:294
  108.9 1.4 %collective-permute-done.13.high_ref = bf16[2,64,2048]{2,1,0:T(8,128)(2,1)S(1)} collective-permute-done((bf16[2,64,2048]{2,1,0:T(8,128)(2,1)S(1)}, bf16[2,64,2048]{2,1,0:T(8,128)(2,1)S(1)}, u32[]{:S(2)}, u32[]{:S(2)}) %collective-permute-start.13) | collective-permute-done | bytes 524320 | tf_op jit(solution)/shard_map/ppermute | solution.py:302
  110.4 7.3 %curl_div.3 = (f32[64,8,2048]{2,1,0:T(8,128)}, f32[64,8,2048]{2,1,0:T(8,128)}) custom-call(f32[2,256,2048]{2,1,0:T(8,128)S(1)} %copy-done.4, bf16[2,192,2048]{2,1,0:T(8,128)(2,1)} %collective-permute-done.10.inner_ref, bf16[2,64,2048]{2,1,0:T(8,128)(2,1)S(1)} %collective-permute-done.12.low_ref, bf16[2,64,2048]{2,1,0:T(8,128)(2,1)S(1)} %collective-permute-done.13.high_ref, ...), custom_call_target="tpu_custom_call" | custom-call | flops 20971520 | bytes 10485760 | tf_op jit(solution)/shard_map/curl_div/pallas_call | solution.py:247
  117.7 1.4 %collective-permute-done.14.inner_ref = bf16[2,144,2048]{2,1,0:T(8,128)(2,1)S(1)} collective-permute-done((bf16[2,144,2048]{2,1,0:T(8,128)(2,1)}, bf16[2,144,2048]{2,1,0:T(8,128)(2,1)S(1)}, u32[]{:S(2)}, u32[]{:S(2)}) %collective-permute-start.14) | collective-permute-done | bytes 1179680 | tf_op jit(solution)/shard_map/ppermute | solution.py:294
  119.2 5.2 %curl_div.4 = (f32[64,8,2048]{2,1,0:T(8,128)}, f32[64,8,2048]{2,1,0:T(8,128)}) custom-call(f32[2,192,2048]{2,1,0:T(8,128)S(1)} %copy-done.7, bf16[2,144,2048]{2,1,0:T(8,128)(2,1)S(1)} %collective-permute-done.14.inner_ref, bf16[2,64,2048]{2,1,0:T(8,128)(2,1)S(1)} %collective-permute-done.12.low_ref, ...), custom_call_target="tpu_custom_call", output_to_operand_aliasing={{0}: (7, {}), {1}: (8, {})} | custom-call | flops 15728640 | bytes 7864320 | tf_op jit(solution)/shard_map/curl_div/pallas_call | solution.py:247
  124.3 3.2 %collective-permute-done.11.inner_ref = bf16[2,48,2048]{2,1,0:T(8,128)(2,1)S(1)} collective-permute-done((bf16[2,48,2048]{2,1,0:T(8,128)(2,1)S(1)}, bf16[2,48,2048]{2,1,0:T(8,128)(2,1)S(1)}, u32[]{:S(2)}, u32[]{:S(2)}) %collective-permute-start.11) | collective-permute-done | bytes 393248 | tf_op jit(solution)/shard_map/ppermute | solution.py:294
  127.6 2.2 %curl_div.5 = (f32[64,8,2048]{2,1,0:T(8,128)}, f32[64,8,2048]{2,1,0:T(8,128)}) custom-call(f32[2,64,2048]{2,1,0:T(8,128)S(1)} %get-tuple-element.36.keep_ref, bf16[2,48,2048]{2,1,0:T(8,128)(2,1)S(1)} %collective-permute-done.11.inner_ref, bf16[2,64,2048]{2,1,0:T(8,128)(2,1)S(1)} %collective-permute-done.12.low_ref, ...), custom_call_target="tpu_custom_call", output_to_operand_aliasing={{0}: (7, {}), {1}: (8, {})} | custom-call | flops 5242880 | bytes 2621440 | tf_op jit(solution)/shard_map/curl_div/pallas_call | solution.py:247
  (47 shorter events, 4.7 us)
Async XLA Ops:
  0.6 2.5 %collective-permute-start = (f32[2,64]{1,0:T(2,128)}, f32[2,64]{1,0:T(2,128)S(1)}, u32[]{:S(2)}, u32[]{:S(2)}) collective-permute-start(f32[2,64]{1,0:T(2,128)} %refs_0_.1), channel_id=1, source_target_pairs={{0,32},{32,0},{64,96},{96,64},{1,33},{33,1},{65,97},{97,65},{2,34}... | collective-permute-start | bytes 1544 | tf_op jit(solution)/shard_map/ppermute | solution.py:279
  3.2 2.2 %copy-start.14 = (f32[2,64]{1,0:T(2,128)}, f32[2,64]{1,0:T(2,128)S(1)}, u32[]{:S(2)}) copy-start(f32[2,64]{1,0:T(2,128)S(1)} %collective-permute-done.refs_4_.refs_1_) | copy-start | bytes 1540
  3.2 13.9 %collective-permute-start.3 = (bf16[2,1024,2048]{2,1,0:T(8,128)(2,1)}, bf16[2,1024,2048]{2,1,0:T(8,128)(2,1)}, u32[]{:S(2)}, u32[]{:S(2)}) collective-permute-start(bf16[2,1024,2048]{2,1,0:T(8,128)(2,1)} %bitcast.10), channel_id=1, source_target_pairs={{0,32},{32,0},{64,96},{96,64},{1,33},{33,1},{65,97},{97,65},{2,34}... | collective-permute-start | bytes 25165832 | tf_op jit(solution)/shard_map/ppermute | solution.py:285
  3.5 5.8 %collective-permute-start.1 = (f32[2,64]{1,0:T(2,128)}, f32[2,64]{1,0:T(2,128)S(1)}, u32[]{:S(2)}, u32[]{:S(2)}) collective-permute-start(f32[2,64]{1,0:T(2,128)} %refs_0_.1), channel_id=1, source_target_pairs={{0,64},{32,96},{64,0},{96,32},{1,65},{33,97},{65,1},{97,33},{2,66}... | collective-permute-start | bytes 1544 | tf_op jit(solution)/shard_map/ppermute | solution.py:279
  5.2 4.1 %collective-permute-start.2 = (f32[2,64]{1,0:T(2,128)}, f32[2,64]{1,0:T(2,128)S(1)}, u32[]{:S(2)}, u32[]{:S(2)}) collective-permute-start(f32[2,64]{1,0:T(2,128)} %refs_0_.1), channel_id=1, source_target_pairs={{0,96},{32,64},{64,32},{96,0},{1,97},{33,65},{65,33},{97,1},{2,98}... | collective-permute-start | bytes 1544 | tf_op jit(solution)/shard_map/ppermute | solution.py:279
  9.3 25.6 %collective-permute-start.4 = (bf16[2,128,2048]{2,1,0:T(8,128)(2,1)}, bf16[2,128,2048]{2,1,0:T(8,128)(2,1)S(1)}, u32[]{:S(2)}, u32[]{:S(2)}) collective-permute-start(bf16[2,128,2048]{2,1,0:T(8,128)(2,1)} %pick_end_rows.2.refs_4_.refs_0_), channel_id=1, source_target_pairs={{0,64},{32,96},{64,0},{96,32},{1,65},{33,97},{65,1},{97,33},{2,66}... | collective-permute-start | bytes 3145736 | tf_op jit(solution)/shard_map/ppermute | solution.py:283
  11.2 4.1 %copy-start.13 = (f32[2,120,512]{2,1,0:T(8,128)S(1)}, f32[2,120,512]{2,1,0:T(8,128)}, u32[]{:S(2)}) copy-start(f32[2,120,512]{2,1,0:T(8,128)} %refs_4_.1) | copy-start | bytes 1474564
  11.2 4.1 %copy-start.15 = (f32[2,64]{1,0:T(2,128)S(1)}, f32[2,64]{1,0:T(2,128)}, u32[]{:S(2)}) copy-start(f32[2,64]{1,0:T(2,128)} %copy-done.14) | copy-start | bytes 1540
  11.2 4.1 %copy-start.16 = (f32[2,64]{1,0:T(2,128)S(1)}, f32[2,64]{1,0:T(2,128)}, u32[]{:S(2)}) copy-start(f32[2,64]{1,0:T(2,128)} %refs_0_.1) | copy-start | bytes 1540
  17.1 3.4 %copy-start = (bf16[2,128,8,2048]{3,2,1,0:T(8,128)(2,1)S(1)}, bf16[2,128,8,2048]{3,2,1,0:T(8,128)(2,1)}, u32[]{:S(2)}) copy-start(bf16[2,128,8,2048]{3,2,1,0:T(8,128)(2,1)} %param.6) | copy-start | bytes 25165828
  20.4 15.0 %copy-start.5 = (bf16[2,128,2048]{2,1,0:T(8,128)(2,1)S(1)}, bf16[2,128,2048]{2,1,0:T(8,128)(2,1)}, u32[]{:S(2)}) copy-start(bf16[2,128,2048]{2,1,0:T(8,128)(2,1)} %pick_end_rows.3.refs_4_) | copy-start | bytes 3145732
  32.9 2.0 %copy-start.3 = (f32[2,256,2048]{2,1,0:T(8,128)}, f32[2,256,2048]{2,1,0:T(8,128)S(1)}, u32[]{:S(2)}) copy-start(f32[2,256,2048]{2,1,0:T(8,128)S(1)} %get-tuple-element.41.keep_ref) | copy-start | bytes 12582916
  34.9 14.9 %copy-start.9 = (bf16[2,128,2048]{2,1,0:T(8,128)(2,1)}, bf16[2,128,2048]{2,1,0:T(8,128)(2,1)S(1)}, u32[]{:S(2)}) copy-start(bf16[2,128,2048]{2,1,0:T(8,128)(2,1)S(1)} %collective-permute-done.4.refs_2_) | copy-start | bytes 3145732
  34.9 26.7 %copy-start.2 = (bf16[2,128,2048]{2,1,0:T(8,128)(2,1)S(1)}, bf16[2,128,2048]{2,1,0:T(8,128)(2,1)}, u32[]{:S(2)}) copy-start(bf16[2,128,2048]{2,1,0:T(8,128)(2,1)} %pick_end_rows.2.refs_4_.refs_0_) | copy-start | bytes 3145732
  34.9 32.1 %copy-start.8 = (s32[8,2048]{1,0:T(8,128)S(1)}, s32[8,2048]{1,0:T(8,128)}, u32[]{:S(2)}) copy-start(s32[8,2048]{1,0:T(8,128)} %land_ref.7) | copy-start | bytes 196612
  34.9 2.8 %collective-permute-start.5 = (bf16[2,128,2048]{2,1,0:T(8,128)(2,1)S(1)}, bf16[2,128,2048]{2,1,0:T(8,128)(2,1)S(1)}, u32[]{:S(2)}, u32[]{:S(2)}) collective-permute-start(bf16[2,128,2048]{2,1,0:T(8,128)(2,1)S(1)} %collective-permute-done.4.refs_2_), channel_id=1, source_target_pairs={{0,32},{32,0},{64,96},{96,64},{1,33},{33,1},{65,97},{97,65},{2,34}... | collective-permute-start | bytes 3145736 | tf_op jit(solution)/shard_map/ppermute | solution.py:297
  35.4 24.8 %collective-permute-start.6 = (bf16[2,128,2048]{2,1,0:T(8,128)(2,1)S(1)}, bf16[2,128,2048]{2,1,0:T(8,128)(2,1)}, u32[]{:S(2)}, u32[]{:S(2)}) collective-permute-start(bf16[2,128,2048]{2,1,0:T(8,128)(2,1)S(1)} %copy-done.5), channel_id=1, source_target_pairs={{0,64},{32,96},{64,0},{96,32},{1,65},{33,97},{65,1},{97,33},{2,66}... | collective-permute-start | bytes 3145736 | tf_op jit(solution)/shard_map/ppermute | solution.py:283
  36.9 57.1 %collective-permute-start.10 = (bf16[2,192,2048]{2,1,0:T(8,128)(2,1)}, bf16[2,192,2048]{2,1,0:T(8,128)(2,1)}, u32[]{:S(2)}, u32[]{:S(2)}) collective-permute-start(bf16[2,192,2048]{2,1,0:T(8,128)(2,1)} %get-tuple-element.26), channel_id=1, source_target_pairs={{0,64},{32,96},{64,0},{96,32},{1,65},{33,97},{65,1},{97,33},{2,66}... | collective-permute-start | bytes 4718600 | tf_op jit(solution)/shard_map/ppermute | solution.py:294
  37.7 1.0 copy-start.11
  49.8 1.6 %copy-start.6 = (f32[2,192,2048]{2,1,0:T(8,128)}, f32[2,192,2048]{2,1,0:T(8,128)S(1)}, u32[]{:S(2)}) copy-start(f32[2,192,2048]{2,1,0:T(8,128)S(1)} %get-tuple-element.40.keep_ref) | copy-start | bytes 9437188
  60.3 5.4 %collective-permute-start.7 = (bf16[2,128,2048]{2,1,0:T(8,128)(2,1)}, bf16[2,128,2048]{2,1,0:T(8,128)(2,1)}, u32[]{:S(2)}, u32[]{:S(2)}) collective-permute-start(bf16[2,128,2048]{2,1,0:T(8,128)(2,1)} %collective-permute-done.6.refs_6_), channel_id=1, source_target_pairs={{0,32},{32,0},{64,96},{96,64},{1,33},{33,1},{65,97},{97,65},{2,34}... | collective-permute-start | bytes 3145736 | tf_op jit(solution)/shard_map/ppermute | solution.py:297
  61.6 4.1 %collective-permute-start.8 = (bf16[2,128,2048]{2,1,0:T(8,128)(2,1)S(1)}, bf16[2,128,2048]{2,1,0:T(8,128)(2,1)}, u32[]{:S(2)}, u32[]{:S(2)}) collective-permute-start(bf16[2,128,2048]{2,1,0:T(8,128)(2,1)S(1)} %copy-done.2), channel_id=1, source_target_pairs={{0,32},{32,0},{64,96},{96,64},{1,33},{33,1},{65,97},{97,65},{2,34}... | collective-permute-start | bytes 3145736 | tf_op jit(solution)/shard_map/ppermute | solution.py:284
  61.6 5.4 %collective-permute-start.9 = (bf16[2,128,2048]{2,1,0:T(8,128)(2,1)S(1)}, bf16[2,128,2048]{2,1,0:T(8,128)(2,1)}, u32[]{:S(2)}, u32[]{:S(2)}) collective-permute-start(bf16[2,128,2048]{2,1,0:T(8,128)(2,1)S(1)} %copy-done.5), channel_id=1, source_target_pairs={{0,32},{32,0},{64,96},{96,64},{1,33},{33,1},{65,97},{97,65},{2,34}... | collective-permute-start | bytes 3145736 | tf_op jit(solution)/shard_map/ppermute | solution.py:284
  62.1 57.0 %collective-permute-start.14 = (bf16[2,144,2048]{2,1,0:T(8,128)(2,1)}, bf16[2,144,2048]{2,1,0:T(8,128)(2,1)S(1)}, u32[]{:S(2)}, u32[]{:S(2)}) collective-permute-start(bf16[2,144,2048]{2,1,0:T(8,128)(2,1)} %get-tuple-element.30), channel_id=1, source_target_pairs={{0,64},{32,96},{64,0},{96,32},{1,65},{33,97},{65,1},{97,33},{2,66}... | collective-permute-start | bytes 3538952 | tf_op jit(solution)/shard_map/ppermute | solution.py:294
  67.0 1.2 copy-start.10
  68.3 1.2 copy-start.12
  74.3 34.6 %collective-permute-start.12 = (bf16[2,64,2048]{2,1,0:T(8,128)(2,1)S(1)}, bf16[2,64,2048]{2,1,0:T(8,128)(2,1)S(1)}, u32[]{:S(2)}, u32[]{:S(2)}) collective-permute-start(bf16[2,64,2048]{2,1,0:T(8,128)(2,1)S(1)} %get-tuple-element.34), channel_id=1, source_target_pairs={{0,65},{1,66},{2,67},{3,68},{4,69},{5,70},{6,71},{7,72},{8,73},{9,... | collective-permute-start | bytes 1572872 | tf_op jit(solution)/shard_map/ppermute | solution.py:302
  94.0 16.4 %collective-permute-start.13 = (bf16[2,64,2048]{2,1,0:T(8,128)(2,1)S(1)}, bf16[2,64,2048]{2,1,0:T(8,128)(2,1)S(1)}, u32[]{:S(2)}, u32[]{:S(2)}) collective-permute-start(bf16[2,64,2048]{2,1,0:T(8,128)(2,1)S(1)} %get-tuple-element.38), channel_id=1, source_target_pairs={{1,64},{2,65},{3,66},{4,67},{5,68},{6,69},{7,70},{8,71},{9,72},{10... | collective-permute-start | bytes 1572872 | tf_op jit(solution)/shard_map/ppermute | solution.py:302
  95.3 3.4 %copy-start.1 = (bf16[2,128,8,2048]{3,2,1,0:T(8,128)(2,1)S(1)}, bf16[2,128,8,2048]{3,2,1,0:T(8,128)(2,1)}, u32[]{:S(2)}) copy-start(bf16[2,128,8,2048]{3,2,1,0:T(8,128)(2,1)} %param.6) | copy-start | bytes 25165828
  98.6 11.8 %copy-start.4 = (f32[2,256,2048]{2,1,0:T(8,128)S(1)}, f32[2,256,2048]{2,1,0:T(8,128)}, u32[]{:S(2)}) copy-start(f32[2,256,2048]{2,1,0:T(8,128)} %copy-done.3) | copy-start | bytes 12582916
  107.1 12.1 %copy-start.7 = (f32[2,192,2048]{2,1,0:T(8,128)S(1)}, f32[2,192,2048]{2,1,0:T(8,128)}, u32[]{:S(2)}) copy-start(f32[2,192,2048]{2,1,0:T(8,128)} %copy-done.6) | copy-start | bytes 9437188
  107.1 20.5 %collective-permute-start.11 = (bf16[2,48,2048]{2,1,0:T(8,128)(2,1)S(1)}, bf16[2,48,2048]{2,1,0:T(8,128)(2,1)S(1)}, u32[]{:S(2)}, u32[]{:S(2)}) collective-permute-start(bf16[2,48,2048]{2,1,0:T(8,128)(2,1)S(1)} %get-tuple-element.37), channel_id=1, source_target_pairs={{0,64},{32,96},{64,0},{96,32},{1,65},{33,97},{65,1},{97,33},{2,66}... | collective-permute-start | bytes 1179656 | tf_op jit(solution)/shard_map/ppermute | solution.py:294

commit v4 on v3

--- a/solution.py
+++ b/solution.py
@@ -14,6 +14,7 @@
 DAY_GROUPS = (32, 24, 8)
 SUB_DAYS = 8
 GROUP = 32
+PICK_BLOCK = 1024
 LON_BLOCK = 512
 BLOCK_DAYS = 16
 VMEM_LIMIT = 40 << 20
@@ -101,10 +102,10 @@
     count = share // GROUP
     return pl.pallas_call(
         functools.partial(pick_kernel, lat),
-        grid=(1,),
-        in_specs=[pl.BlockSpec((1, GROUP * lat, lon), lambda i, n=n: (x, n, 0)) for n in range(count)]
+        grid=(lon // PICK_BLOCK,),
+        in_specs=[pl.BlockSpec((1, GROUP * lat, PICK_BLOCK), lambda i, n=n: (x, n, i)) for n in range(count)]
         + [pl.BlockSpec(memory_space=pl.ANY)],
-        out_specs=pl.BlockSpec((2, share, lon), lambda i: (0, 0, 0)),
+        out_specs=pl.BlockSpec((2, share, PICK_BLOCK), lambda i: (0, 0, i)),
         out_shape=jax.ShapeDtypeStruct((2, share, lon), BF16),
         compiler_params=pltpu.CompilerParams(vmem_limit_bytes=57 << 20),
         cost_estimate=pl.CostEstimate(flops=0, bytes_accessed=16 << 20, transcendentals=0),

time: 131 us -> 131 us (level)
  transfers between devices with their start and end apart: 15 -> 15, of which waited for: 9 -> 10; matrix products, arithmetic and copies ran while one was open for 0% -> 0% of each run, Pallas kernels for 46% -> 45%
where the time goes in v4:
time: 131 us; the launch traced here: 130 us
  Pallas kernels  60.3 us (46%)
  waiting for transfers between devices  35 us (27%)
  starting transfers between devices  19.4 us (15%)
  local copies, waits for them, and re-layouts  14 us (11%)
    pallas_call x3, Pallas kernels, inner_call(): pl.pallas_call(functools.partial(inner_kernel, lat, first, span), grid=(l...  31.9 us
    ppermute x3, waiting for transfers between devices, shards(): inners.append((lax.ppermute(send, 'tm', swap_chip), keep))  19.3 us
    pallas_call x3, Pallas kernels, curl_call(): pl.pallas_call(functools.partial(curl_kernel, lat, first), grid=(span //...  14.7 us
    unnamed x34, local copies, waits for them, and re-layouts  13.9 us
    ppermute x2, waiting for transfers between devices, shards(): lax.ppermute(after(m, *pcs_all[2:]), 'tm', swap_chip)  9.13 us
    pallas_call x2, Pallas kernels, pick_call(): pl.pallas_call(functools.partial(pick_kernel, lat), grid=(lon // PICK_BLO...  7.06 us
    ppermute x1, starting transfers between devices, shards(): lax.ppermute(low, ('tm', 'tile'), north)  5.82 us
    pallas_call x1, Pallas kernels, edge_call(): pl.pallas_call(edge_kernel, grid=(lon // block,), in_specs=[pl.BlockSpec(...  4.84 us
  transfers between devices with their start and end apart: 15, of which 10 were waited for; matrix products, arithmetic and copies ran while one was open for 0% of the time, Pallas kernels for 45%

profile of v4, /device:TPU:1, one launch (start us, length us, event | category | flops | bytes accessed | tf_op | source)
XLA Modules:
  0.0 129.7 jit_solution(7828834672085353321)
XLA Ops:
  0.6 1.5 %collective-permute-start = (f32[2,64]{1,0:T(2,128)}, f32[2,64]{1,0:T(2,128)S(1)}, u32[]{:S(2)}, u32[]{:S(2)}) collective-permute-start(f32[2,64]{1,0:T(2,128)} %refs_0_.1), channel_id=1, source_target_pairs={{0,32},{32,0},{64,96},{96,64},{1,33},{33,1},{65,97},{97,65},{2,34}... | collective-permute-start | bytes 1544 | tf_op jit(solution)/shard_map/ppermute | solution.py:280
  2.1 1.0 collective-permute-done.refs_4_.refs_1_
  3.5 1.7 %collective-permute-start.1 = (f32[2,64]{1,0:T(2,128)}, f32[2,64]{1,0:T(2,128)S(1)}, u32[]{:S(2)}, u32[]{:S(2)}) collective-permute-start(f32[2,64]{1,0:T(2,128)} %refs_0_.1), channel_id=1, source_target_pairs={{0,64},{32,96},{64,0},{96,32},{1,65},{33,97},{65,1},{97,33},{2,66}... | collective-permute-start | bytes 1544 | tf_op jit(solution)/shard_map/ppermute | solution.py:280
  5.3 3.5 %pick_end_rows.2.refs_4_.refs_0_ = bf16[2,128,2048]{2,1,0:T(8,128)(2,1)} custom-call(bf16[2,1024,2048]{2,1,0:T(8,128)(2,1)} %bitcast.11, bf16[2,1024,2048]{2,1,0:T(8,128)(2,1)} %bitcast.12, bf16[2,1024,2048]{2,1,0:T(8,128)(2,1)} %bitcast.13, bf16[2,1024,2048]{2,1,0:T(8,128)(2,1)} %bitcast.14, f32[2,64]{1,0:T(2,128)} %copy-done.14), custom_call_target="tpu_custom_call" | custom-call | bytes 16777216 | tf_op jit(solution)/shard_map/pick_end_rows/pallas_call | solution.py:103
  8.9 1.8 %collective-permute-start.4 = (bf16[2,128,2048]{2,1,0:T(8,128)(2,1)}, bf16[2,128,2048]{2,1,0:T(8,128)(2,1)S(1)}, u32[]{:S(2)}, u32[]{:S(2)}) collective-permute-start(bf16[2,128,2048]{2,1,0:T(8,128)(2,1)} %pick_end_rows.2.refs_4_.refs_0_), channel_id=1, source_target_pairs={{0,64},{32,96},{64,0},{96,32},{1,65},{33,97},{65,1},{97,33},{2,66}... | collective-permute-start | bytes 3145736 | tf_op jit(solution)/shard_map/ppermute | solution.py:284
  10.7 3.5 %pick_end_rows.3.refs_4_ = bf16[2,128,2048]{2,1,0:T(8,128)(2,1)} custom-call(bf16[2,1024,2048]{2,1,0:T(8,128)(2,1)} %bitcast.15, bf16[2,1024,2048]{2,1,0:T(8,128)(2,1)} %bitcast.16, bf16[2,1024,2048]{2,1,0:T(8,128)(2,1)} %bitcast.17, bf16[2,1024,2048]{2,1,0:T(8,128)(2,1)} %bitcast.18, bf16[2,128,2048]{2,1,0:T(8,128)(2,1)} %pick_end_rows.2.refs_4_.refs_0_), custom_call_target="tpu_custom_call" | custom-call | bytes 16777216 | tf_op jit(solution)/shard_map/pick_end_rows/pallas_call | solution.py:103
  14.3 1.8 %components.1.comp_ref = bf16[128,512]{1,0:T(8,128)(2,1)S(1)} custom-call(s32[3]{0:T(128)S(1)} %pad_add_fusion.place, f32[2,64]{1,0:T(2,128)S(1)} %copy-done.16, f32[2,64]{1,0:T(2,128)S(1)} %copy-done.15, f32[2,64]{1,0:T(2,128)S(1)} %collective-permute-done.1.refs_2_, f32[2,64]{1,0:T(2,128)S(1)} %collective-permute-done.2.refs_3_, f32[2,120,512]{2,1,0:T(8,128)S(1)} %copy-done.13), custom_call_target="tpu_custom_call" | custom-call | bytes 134217728 | tf_op jit(solution)/shard_map/components/pallas_call | solution.py:74
  16.7 3.4 %copy-done = bf16[2,128,8,2048]{3,2,1,0:T(8,128)(2,1)S(1)} copy-done((bf16[2,128,8,2048]{3,2,1,0:T(8,128)(2,1)S(1)}, bf16[2,128,8,2048]{3,2,1,0:T(8,128)(2,1)}, u32[]{:S(2)}) %copy-start) | copy-done | bytes 8388632
  20.0 12.4 %inner_partials.3 = (bf16[2,192,2048]{2,1,0:T(8,128)(2,1)}, f32[2,256,2048]{2,1,0:T(8,128)S(1)}) custom-call(bf16[128,512]{1,0:T(8,128)(2,1)S(1)} %components.1.comp_ref, bf16[2,1024,2048]{2,1,0:T(8,128)(2,1)S(1)} %bitcast.19, bf16[2,1024,2048]{2,1,0:T(8,128)(2,1)} %collective-permute-done.3.oth_ref), custom_call_target="tpu_custom_call" | custom-call | flops 7516192768 | bytes 22282240 | tf_op jit(solution)/shard_map/inner_partials/pallas_call | solution.py:186
  32.5 2.0 %copy-done.3 = f32[2,256,2048]{2,1,0:T(8,128)} copy-done((f32[2,256,2048]{2,1,0:T(8,128)}, f32[2,256,2048]{2,1,0:T(8,128)S(1)}, u32[]{:S(2)}) %copy-start.3) | copy-done | bytes 4194328
  35.0 1.6 %collective-permute-start.6 = (bf16[2,128,2048]{2,1,0:T(8,128)(2,1)S(1)}, bf16[2,128,2048]{2,1,0:T(8,128)(2,1)}, u32[]{:S(2)}, u32[]{:S(2)}) collective-permute-start(bf16[2,128,2048]{2,1,0:T(8,128)(2,1)S(1)} %copy-done.5), channel_id=1, source_target_pairs={{0,64},{32,96},{64,0},{96,32},{1,65},{33,97},{65,1},{97,33},{2,66}... | collective-permute-start | bytes 3145736 | tf_op jit(solution)/shard_map/ppermute | solution.py:284
  38.3 11.1 %inner_partials.4 = (bf16[2,144,2048]{2,1,0:T(8,128)(2,1)}, f32[2,192,2048]{2,1,0:T(8,128)S(1)}) custom-call(bf16[128,512]{1,0:T(8,128)(2,1)S(1)} %components.1.comp_ref, bf16[2,1024,2048]{2,1,0:T(8,128)(2,1)S(1)} %bitcast.20, bf16[2,1024,2048]{2,1,0:T(8,128)(2,1)} %collective-permute-done.3.oth_ref), custom_call_target="tpu_custom_call" | custom-call | flops 5637144576 | bytes 20905984 | tf_op jit(solution)/shard_map/inner_partials/pallas_call | solution.py:186
  49.4 1.6 %copy-done.6 = f32[2,192,2048]{2,1,0:T(8,128)} copy-done((f32[2,192,2048]{2,1,0:T(8,128)}, f32[2,192,2048]{2,1,0:T(8,128)S(1)}, u32[]{:S(2)}) %copy-start.6) | copy-done | bytes 3145752
  51.0 9.1 %collective-permute-done.6.refs_6_ = bf16[2,128,2048]{2,1,0:T(8,128)(2,1)} collective-permute-done((bf16[2,128,2048]{2,1,0:T(8,128)(2,1)S(1)}, bf16[2,128,2048]{2,1,0:T(8,128)(2,1)}, u32[]{:S(2)}, u32[]{:S(2)}) %collective-permute-start.6) | collective-permute-done | bytes 1048608 | tf_op jit(solution)/shard_map/ppermute | solution.py:284
  61.7 1.8 %collective-permute-start.14 = (bf16[2,144,2048]{2,1,0:T(8,128)(2,1)}, bf16[2,144,2048]{2,1,0:T(8,128)(2,1)S(1)}, u32[]{:S(2)}, u32[]{:S(2)}) collective-permute-start(bf16[2,144,2048]{2,1,0:T(8,128)(2,1)} %get-tuple-element.30), channel_id=1, source_target_pairs={{0,64},{32,96},{64,0},{96,32},{1,65},{33,97},{65,1},{97,33},{2,66}... | collective-permute-start | bytes 3538952 | tf_op jit(solution)/shard_map/ppermute | solution.py:295
  63.4 1.8 %collective-permute-done.7.refs_7_ = bf16[2,128,2048]{2,1,0:T(8,128)(2,1)} collective-permute-done((bf16[2,128,2048]{2,1,0:T(8,128)(2,1)}, bf16[2,128,2048]{2,1,0:T(8,128)(2,1)}, u32[]{:S(2)}, u32[]{:S(2)}) %collective-permute-start.7) | collective-permute-done | bytes 1048608 | tf_op jit(solution)/shard_map/ppermute | solution.py:298
  65.2 1.4 %collective-permute-done.9.refs_5_ = bf16[2,128,2048]{2,1,0:T(8,128)(2,1)} collective-permute-done((bf16[2,128,2048]{2,1,0:T(8,128)(2,1)S(1)}, bf16[2,128,2048]{2,1,0:T(8,128)(2,1)}, u32[]{:S(2)}, u32[]{:S(2)}) %collective-permute-start.9) | collective-permute-done | bytes 1048608 | tf_op jit(solution)/shard_map/ppermute | solution.py:285
  66.6 1.2 copy-done.10
  67.8 1.2 copy-done.12
  69.0 4.8 %end_rows.1 = (bf16[2,64,2048]{2,1,0:T(8,128)(2,1)S(1)}, bf16[2,64,2048]{2,1,0:T(8,128)(2,1)S(1)}, bf16[2,2,64,2048]{3,2,1,0:T(8,128)(2,1)S(1)}) custom-call(bf16[128,512]{1,0:T(8,128)(2,1)S(1)} %components.1.comp_ref, s32[8,2048]{1,0:T(8,128)S(1)} %copy-done.8, bf16[2,128,2048]{2,1,0:T(8,128)(2,1)S(1)} %copy-done.2, ...), custom_call_target="tpu_custom_call" | custom-call | tf_op jit(solution)/shard_map/end_rows/pallas_call | solution.py:141
  73.9 5.8 %collective-permute-start.12 = (bf16[2,64,2048]{2,1,0:T(8,128)(2,1)S(1)}, bf16[2,64,2048]{2,1,0:T(8,128)(2,1)S(1)}, u32[]{:S(2)}, u32[]{:S(2)}) collective-permute-start(bf16[2,64,2048]{2,1,0:T(8,128)(2,1)S(1)} %get-tuple-element.34), channel_id=1, source_target_pairs={{0,65},{1,66},{2,67},{3,68},{4,69},{5,70},{6,71},{7,72},{8,73},{9,... | collective-permute-start | bytes 1572872 | tf_op jit(solution)/shard_map/ppermute | solution.py:303
  79.7 14.2 %collective-permute-done.10.inner_ref = bf16[2,192,2048]{2,1,0:T(8,128)(2,1)} collective-permute-done((bf16[2,192,2048]{2,1,0:T(8,128)(2,1)}, bf16[2,192,2048]{2,1,0:T(8,128)(2,1)}, u32[]{:S(2)}, u32[]{:S(2)}) %collective-permute-start.10) | collective-permute-done | bytes 1572896 | tf_op jit(solution)/shard_map/ppermute | solution.py:295
  93.8 1.3 collective-permute-start.13
  95.1 3.4 %copy-done.1 = bf16[2,128,8,2048]{3,2,1,0:T(8,128)(2,1)S(1)} copy-done((bf16[2,128,8,2048]{3,2,1,0:T(8,128)(2,1)S(1)}, bf16[2,128,8,2048]{3,2,1,0:T(8,128)(2,1)}, u32[]{:S(2)}) %copy-start.1) | copy-done | bytes 8388632
  98.5 8.4 %inner_partials.5 = (bf16[2,48,2048]{2,1,0:T(8,128)(2,1)S(1)}, f32[2,64,2048]{2,1,0:T(8,128)S(1)}) custom-call(bf16[128,512]{1,0:T(8,128)(2,1)S(1)} %components.1.comp_ref, bf16[2,1024,2048]{2,1,0:T(8,128)(2,1)S(1)} %bitcast.21, bf16[2,1024,2048]{2,1,0:T(8,128)(2,1)} %collective-permute-done.3.oth_ref), custom_call_target="tpu_custom_call" | custom-call | flops 1879048192 | bytes 18153472 | tf_op jit(solution)/shard_map/inner_partials/pallas_call | solution.py:186
  106.9 1.4 %collective-permute-start.11 = (bf16[2,48,2048]{2,1,0:T(8,128)(2,1)S(1)}, bf16[2,48,2048]{2,1,0:T(8,128)(2,1)S(1)}, u32[]{:S(2)}, u32[]{:S(2)}) collective-permute-start(bf16[2,48,2048]{2,1,0:T(8,128)(2,1)S(1)} %get-tuple-element.37), channel_id=1, source_target_pairs={{0,64},{32,96},{64,0},{96,32},{1,65},{33,97},{65,1},{97,33},{2,66}... | collective-permute-start | bytes 1179656 | tf_op jit(solution)/shard_map/ppermute | solution.py:295
  108.5 1.1 collective-permute-done.13.high_ref
  109.7 7.3 %curl_div.3 = (f32[64,8,2048]{2,1,0:T(8,128)}, f32[64,8,2048]{2,1,0:T(8,128)}) custom-call(f32[2,256,2048]{2,1,0:T(8,128)S(1)} %copy-done.4, bf16[2,192,2048]{2,1,0:T(8,128)(2,1)} %collective-permute-done.10.inner_ref, bf16[2,64,2048]{2,1,0:T(8,128)(2,1)S(1)} %collective-permute-done.12.low_ref, bf16[2,64,2048]{2,1,0:T(8,128)(2,1)S(1)} %collective-permute-done.13.high_ref, ...), custom_call_target="tpu_custom_call" | custom-call | flops 20971520 | bytes 10485760 | tf_op jit(solution)/shard_map/curl_div/pallas_call | solution.py:248
  117.1 1.9 %collective-permute-done.14.inner_ref = bf16[2,144,2048]{2,1,0:T(8,128)(2,1)S(1)} collective-permute-done((bf16[2,144,2048]{2,1,0:T(8,128)(2,1)}, bf16[2,144,2048]{2,1,0:T(8,128)(2,1)S(1)}, u32[]{:S(2)}, u32[]{:S(2)}) %collective-permute-start.14) | collective-permute-done | bytes 1179680 | tf_op jit(solution)/shard_map/ppermute | solution.py:295
  119.0 5.2 %curl_div.4 = (f32[64,8,2048]{2,1,0:T(8,128)}, f32[64,8,2048]{2,1,0:T(8,128)}) custom-call(f32[2,192,2048]{2,1,0:T(8,128)S(1)} %copy-done.7, bf16[2,144,2048]{2,1,0:T(8,128)(2,1)S(1)} %collective-permute-done.14.inner_ref, bf16[2,64,2048]{2,1,0:T(8,128)(2,1)S(1)} %collective-permute-done.12.low_ref, ...), custom_call_target="tpu_custom_call", output_to_operand_aliasing={{0}: (7, {}), {1}: (8, {})} | custom-call | flops 15728640 | bytes 7864320 | tf_op jit(solution)/shard_map/curl_div/pallas_call | solution.py:248
  124.2 3.2 %collective-permute-done.11.inner_ref = bf16[2,48,2048]{2,1,0:T(8,128)(2,1)S(1)} collective-permute-done((bf16[2,48,2048]{2,1,0:T(8,128)(2,1)S(1)}, bf16[2,48,2048]{2,1,0:T(8,128)(2,1)S(1)}, u32[]{:S(2)}, u32[]{:S(2)}) %collective-permute-start.11) | collective-permute-done | bytes 393248 | tf_op jit(solution)/shard_map/ppermute | solution.py:295
  127.4 2.2 %curl_div.5 = (f32[64,8,2048]{2,1,0:T(8,128)}, f32[64,8,2048]{2,1,0:T(8,128)}) custom-call(f32[2,64,2048]{2,1,0:T(8,128)S(1)} %get-tuple-element.36.keep_ref, bf16[2,48,2048]{2,1,0:T(8,128)(2,1)S(1)} %collective-permute-done.11.inner_ref, bf16[2,64,2048]{2,1,0:T(8,128)(2,1)S(1)} %collective-permute-done.12.low_ref, ...), custom_call_target="tpu_custom_call", output_to_operand_aliasing={{0}: (7, {}), {1}: (8, {})} | custom-call | flops 5242880 | bytes 2621440 | tf_op jit(solution)/shard_map/curl_div/pallas_call | solution.py:248
  (47 shorter events, 5.1 us)
Async XLA Ops:
  0.6 2.5 %collective-permute-start = (f32[2,64]{1,0:T(2,128)}, f32[2,64]{1,0:T(2,128)S(1)}, u32[]{:S(2)}, u32[]{:S(2)}) collective-permute-start(f32[2,64]{1,0:T(2,128)} %refs_0_.1), channel_id=1, source_target_pairs={{0,32},{32,0},{64,96},{96,64},{1,33},{33,1},{65,97},{97,65},{2,34}... | collective-permute-start | bytes 1544 | tf_op jit(solution)/shard_map/ppermute | solution.py:280
  3.2 2.2 %copy-start.14 = (f32[2,64]{1,0:T(2,128)}, f32[2,64]{1,0:T(2,128)S(1)}, u32[]{:S(2)}) copy-start(f32[2,64]{1,0:T(2,128)S(1)} %collective-permute-done.refs_4_.refs_1_) | copy-start | bytes 1540
  3.2 13.5 %collective-permute-start.3 = (bf16[2,1024,2048]{2,1,0:T(8,128)(2,1)}, bf16[2,1024,2048]{2,1,0:T(8,128)(2,1)}, u32[]{:S(2)}, u32[]{:S(2)}) collective-permute-start(bf16[2,1024,2048]{2,1,0:T(8,128)(2,1)} %bitcast.10), channel_id=1, source_target_pairs={{0,32},{32,0},{64,96},{96,64},{1,33},{33,1},{65,97},{97,65},{2,34}... | collective-permute-start | bytes 25165832 | tf_op jit(solution)/shard_map/ppermute | solution.py:286
  3.5 5.4 %collective-permute-start.1 = (f32[2,64]{1,0:T(2,128)}, f32[2,64]{1,0:T(2,128)S(1)}, u32[]{:S(2)}, u32[]{:S(2)}) collective-permute-start(f32[2,64]{1,0:T(2,128)} %refs_0_.1), channel_id=1, source_target_pairs={{0,64},{32,96},{64,0},{96,32},{1,65},{33,97},{65,1},{97,33},{2,66}... | collective-permute-start | bytes 1544 | tf_op jit(solution)/shard_map/ppermute | solution.py:280
  5.2 3.7 %collective-permute-start.2 = (f32[2,64]{1,0:T(2,128)}, f32[2,64]{1,0:T(2,128)S(1)}, u32[]{:S(2)}, u32[]{:S(2)}) collective-permute-start(f32[2,64]{1,0:T(2,128)} %refs_0_.1), channel_id=1, source_target_pairs={{0,96},{32,64},{64,32},{96,0},{1,97},{33,65},{65,33},{97,1},{2,98}... | collective-permute-start | bytes 1544 | tf_op jit(solution)/shard_map/ppermute | solution.py:280
  8.9 25.6 %collective-permute-start.4 = (bf16[2,128,2048]{2,1,0:T(8,128)(2,1)}, bf16[2,128,2048]{2,1,0:T(8,128)(2,1)S(1)}, u32[]{:S(2)}, u32[]{:S(2)}) collective-permute-start(bf16[2,128,2048]{2,1,0:T(8,128)(2,1)} %pick_end_rows.2.refs_4_.refs_0_), channel_id=1, source_target_pairs={{0,64},{32,96},{64,0},{96,32},{1,65},{33,97},{65,1},{97,33},{2,66}... | collective-permute-start | bytes 3145736 | tf_op jit(solution)/shard_map/ppermute | solution.py:284
  10.7 3.5 %copy-start.13 = (f32[2,120,512]{2,1,0:T(8,128)S(1)}, f32[2,120,512]{2,1,0:T(8,128)}, u32[]{:S(2)}) copy-start(f32[2,120,512]{2,1,0:T(8,128)} %refs_4_.1) | copy-start | bytes 1474564
  10.7 3.5 %copy-start.15 = (f32[2,64]{1,0:T(2,128)S(1)}, f32[2,64]{1,0:T(2,128)}, u32[]{:S(2)}) copy-start(f32[2,64]{1,0:T(2,128)} %copy-done.14) | copy-start | bytes 1540
  10.7 3.5 %copy-start.16 = (f32[2,64]{1,0:T(2,128)S(1)}, f32[2,64]{1,0:T(2,128)}, u32[]{:S(2)}) copy-start(f32[2,64]{1,0:T(2,128)} %refs_0_.1) | copy-start | bytes 1540
  16.7 3.4 %copy-start = (bf16[2,128,8,2048]{3,2,1,0:T(8,128)(2,1)S(1)}, bf16[2,128,8,2048]{3,2,1,0:T(8,128)(2,1)}, u32[]{:S(2)}) copy-start(bf16[2,128,8,2048]{3,2,1,0:T(8,128)(2,1)} %param.6) | copy-start | bytes 25165828
  20.0 14.9 %copy-start.5 = (bf16[2,128,2048]{2,1,0:T(8,128)(2,1)S(1)}, bf16[2,128,2048]{2,1,0:T(8,128)(2,1)}, u32[]{:S(2)}) copy-start(bf16[2,128,2048]{2,1,0:T(8,128)(2,1)} %pick_end_rows.3.refs_4_) | copy-start | bytes 3145732
  32.5 2.0 %copy-start.3 = (f32[2,256,2048]{2,1,0:T(8,128)}, f32[2,256,2048]{2,1,0:T(8,128)S(1)}, u32[]{:S(2)}) copy-start(f32[2,256,2048]{2,1,0:T(8,128)S(1)} %get-tuple-element.41.keep_ref) | copy-start | bytes 12582916
  34.5 14.9 %copy-start.9 = (bf16[2,128,2048]{2,1,0:T(8,128)(2,1)}, bf16[2,128,2048]{2,1,0:T(8,128)(2,1)S(1)}, u32[]{:S(2)}) copy-start(bf16[2,128,2048]{2,1,0:T(8,128)(2,1)S(1)} %collective-permute-done.4.refs_2_) | copy-start | bytes 3145732
  34.5 26.7 %copy-start.2 = (bf16[2,128,2048]{2,1,0:T(8,128)(2,1)S(1)}, bf16[2,128,2048]{2,1,0:T(8,128)(2,1)}, u32[]{:S(2)}) copy-start(bf16[2,128,2048]{2,1,0:T(8,128)(2,1)} %pick_end_rows.2.refs_4_.refs_0_) | copy-start | bytes 3145732
  34.5 32.1 %copy-start.8 = (s32[8,2048]{1,0:T(8,128)S(1)}, s32[8,2048]{1,0:T(8,128)}, u32[]{:S(2)}) copy-start(s32[8,2048]{1,0:T(8,128)} %land_ref.7) | copy-start | bytes 196612
  34.5 2.8 %collective-permute-start.5 = (bf16[2,128,2048]{2,1,0:T(8,128)(2,1)S(1)}, bf16[2,128,2048]{2,1,0:T(8,128)(2,1)S(1)}, u32[]{:S(2)}, u32[]{:S(2)}) collective-permute-start(bf16[2,128,2048]{2,1,0:T(8,128)(2,1)S(1)} %collective-permute-done.4.refs_2_), channel_id=1, source_target_pairs={{0,32},{32,0},{64,96},{96,64},{1,33},{33,1},{65,97},{97,65},{2,34}... | collective-permute-start | bytes 3145736 | tf_op jit(solution)/shard_map/ppermute | solution.py:298
  35.0 25.2 %collective-permute-start.6 = (bf16[2,128,2048]{2,1,0:T(8,128)(2,1)S(1)}, bf16[2,128,2048]{2,1,0:T(8,128)(2,1)}, u32[]{:S(2)}, u32[]{:S(2)}) collective-permute-start(bf16[2,128,2048]{2,1,0:T(8,128)(2,1)S(1)} %copy-done.5), channel_id=1, source_target_pairs={{0,64},{32,96},{64,0},{96,32},{1,65},{33,97},{65,1},{97,33},{2,66}... | collective-permute-start | bytes 3145736 | tf_op jit(solution)/shard_map/ppermute | solution.py:284
  36.6 57.2 %collective-permute-start.10 = (bf16[2,192,2048]{2,1,0:T(8,128)(2,1)}, bf16[2,192,2048]{2,1,0:T(8,128)(2,1)}, u32[]{:S(2)}, u32[]{:S(2)}) collective-permute-start(bf16[2,192,2048]{2,1,0:T(8,128)(2,1)} %get-tuple-element.26), channel_id=1, source_target_pairs={{0,64},{32,96},{64,0},{96,32},{1,65},{33,97},{65,1},{97,33},{2,66}... | collective-permute-start | bytes 4718600 | tf_op jit(solution)/shard_map/ppermute | solution.py:295
  37.3 1.0 copy-start.11
  49.4 1.6 %copy-start.6 = (f32[2,192,2048]{2,1,0:T(8,128)}, f32[2,192,2048]{2,1,0:T(8,128)S(1)}, u32[]{:S(2)}) copy-start(f32[2,192,2048]{2,1,0:T(8,128)S(1)} %get-tuple-element.40.keep_ref) | copy-start | bytes 9437188
  60.1 5.1 %collective-permute-start.7 = (bf16[2,128,2048]{2,1,0:T(8,128)(2,1)}, bf16[2,128,2048]{2,1,0:T(8,128)(2,1)}, u32[]{:S(2)}, u32[]{:S(2)}) collective-permute-start(bf16[2,128,2048]{2,1,0:T(8,128)(2,1)} %collective-permute-done.6.refs_6_), channel_id=1, source_target_pairs={{0,32},{32,0},{64,96},{96,64},{1,33},{33,1},{65,97},{97,65},{2,34}... | collective-permute-start | bytes 3145736 | tf_op jit(solution)/shard_map/ppermute | solution.py:298
  61.1 4.1 %collective-permute-start.8 = (bf16[2,128,2048]{2,1,0:T(8,128)(2,1)S(1)}, bf16[2,128,2048]{2,1,0:T(8,128)(2,1)}, u32[]{:S(2)}, u32[]{:S(2)}) collective-permute-start(bf16[2,128,2048]{2,1,0:T(8,128)(2,1)S(1)} %copy-done.2), channel_id=1, source_target_pairs={{0,32},{32,0},{64,96},{96,64},{1,33},{33,1},{65,97},{97,65},{2,34}... | collective-permute-start | bytes 3145736 | tf_op jit(solution)/shard_map/ppermute | solution.py:285
  61.1 5.4 %collective-permute-start.9 = (bf16[2,128,2048]{2,1,0:T(8,128)(2,1)S(1)}, bf16[2,128,2048]{2,1,0:T(8,128)(2,1)}, u32[]{:S(2)}, u32[]{:S(2)}) collective-permute-start(bf16[2,128,2048]{2,1,0:T(8,128)(2,1)S(1)} %copy-done.5), channel_id=1, source_target_pairs={{0,32},{32,0},{64,96},{96,64},{1,33},{33,1},{65,97},{97,65},{2,34}... | collective-permute-start | bytes 3145736 | tf_op jit(solution)/shard_map/ppermute | solution.py:285
  61.7 57.4 %collective-permute-start.14 = (bf16[2,144,2048]{2,1,0:T(8,128)(2,1)}, bf16[2,144,2048]{2,1,0:T(8,128)(2,1)S(1)}, u32[]{:S(2)}, u32[]{:S(2)}) collective-permute-start(bf16[2,144,2048]{2,1,0:T(8,128)(2,1)} %get-tuple-element.30), channel_id=1, source_target_pairs={{0,64},{32,96},{64,0},{96,32},{1,65},{33,97},{65,1},{97,33},{2,66}... | collective-permute-start | bytes 3538952 | tf_op jit(solution)/shard_map/ppermute | solution.py:295
  66.6 1.2 copy-start.10
  67.8 1.2 copy-start.12
  73.9 34.6 %collective-permute-start.12 = (bf16[2,64,2048]{2,1,0:T(8,128)(2,1)S(1)}, bf16[2,64,2048]{2,1,0:T(8,128)(2,1)S(1)}, u32[]{:S(2)}, u32[]{:S(2)}) collective-permute-start(bf16[2,64,2048]{2,1,0:T(8,128)(2,1)S(1)} %get-tuple-element.34), channel_id=1, source_target_pairs={{0,65},{1,66},{2,67},{3,68},{4,69},{5,70},{6,71},{7,72},{8,73},{9,... | collective-permute-start | bytes 1572872 | tf_op jit(solution)/shard_map/ppermute | solution.py:303
  93.8 15.8 %collective-permute-start.13 = (bf16[2,64,2048]{2,1,0:T(8,128)(2,1)S(1)}, bf16[2,64,2048]{2,1,0:T(8,128)(2,1)S(1)}, u32[]{:S(2)}, u32[]{:S(2)}) collective-permute-start(bf16[2,64,2048]{2,1,0:T(8,128)(2,1)S(1)} %get-tuple-element.38), channel_id=1, source_target_pairs={{1,64},{2,65},{3,66},{4,67},{5,68},{6,69},{7,70},{8,71},{9,72},{10... | collective-permute-start | bytes 1572872 | tf_op jit(solution)/shard_map/ppermute | solution.py:303
  95.1 3.4 %copy-start.1 = (bf16[2,128,8,2048]{3,2,1,0:T(8,128)(2,1)S(1)}, bf16[2,128,8,2048]{3,2,1,0:T(8,128)(2,1)}, u32[]{:S(2)}) copy-start(bf16[2,128,8,2048]{3,2,1,0:T(8,128)(2,1)} %param.6) | copy-start | bytes 25165828
  98.5 11.2 %copy-start.4 = (f32[2,256,2048]{2,1,0:T(8,128)S(1)}, f32[2,256,2048]{2,1,0:T(8,128)}, u32[]{:S(2)}) copy-start(f32[2,256,2048]{2,1,0:T(8,128)} %copy-done.3) | copy-start | bytes 12582916
  106.9 12.1 %copy-start.7 = (f32[2,192,2048]{2,1,0:T(8,128)S(1)}, f32[2,192,2048]{2,1,0:T(8,128)}, u32[]{:S(2)}) copy-start(f32[2,192,2048]{2,1,0:T(8,128)} %copy-done.6) | copy-start | bytes 9437188
  106.9 20.5 %collective-permute-start.11 = (bf16[2,48,2048]{2,1,0:T(8,128)(2,1)S(1)}, bf16[2,48,2048]{2,1,0:T(8,128)(2,1)S(1)}, u32[]{:S(2)}, u32[]{:S(2)}) collective-permute-start(bf16[2,48,2048]{2,1,0:T(8,128)(2,1)S(1)} %get-tuple-element.37), channel_id=1, source_target_pairs={{0,64},{32,96},{64,0},{96,32},{1,65},{33,97},{65,1},{97,33},{2,66}... | collective-permute-start | bytes 1179656 | tf_op jit(solution)/shard_map/ppermute | solution.py:295

commit v5 on v4

--- a/solution.py
+++ b/solution.py
@@ -11,7 +11,7 @@
 F32 = jnp.float32
 BF16 = jnp.bfloat16
 VMEM = pltpu.VMEM
-DAY_GROUPS = (32, 24, 8)
+DAY_GROUPS = (24, 32, 8)
 SUB_DAYS = 8
 GROUP = 32
 PICK_BLOCK = 1024
@@ -288,16 +288,17 @@
     place = jnp.stack([(tm ^ 2) * day_dev, tm * day_dev, tm]).astype(jnp.int32)
     comp = components_call(after(place, mine[1]), pcs_all, st_eof, share)
 
-    inners, across = [], []
+    inners = []
     first = 0
     for i, span in enumerate(DAY_GROUPS):
         send, keep = inner_call(comp, own, oth, lat, lon, first, span, LON_BLOCK)
         inners.append((lax.ppermute(send, "tm", swap_chip), keep))
         first += span
-        if i < 2:
-            across.append(lax.ppermute(after(crossed[i], send), "tm", swap_core))
-            comp = after(comp, send, across[i])
+        if i == 0:
+            comp = after(comp, send, crossed[0])
         if i == 1:
+            across = [lax.ppermute(after(c, send), "tm", swap_core) for c in crossed]
+            comp = after(comp, send)
             parts = [a for x in range(2) for a in (mine[x], swapped[x], crossed[x], across[x])]
             low, high, ends = edge_call(comp, land_sea, parts, LON_BLOCK)
             halos = [lax.ppermute(low, ("tm", "tile"), north), lax.ppermute(high, ("tm", "tile"), south)]

time: 131 us -> 127 us (0.969)
  waiting for transfers between devices: 35 us -> 31.9 us
    ppermute x3, waiting for transfers between devices: 19.3 us -> 23.8 us  [shards(): inners.append((lax.ppermute(send, 'tm', swap_chip), keep))]
    ppermute x2, waiting for transfers between devices: 9.13 us -> 6.64 us  [shards(): lax.ppermute(after(m, *pcs_all[2:]), 'tm', swap_chip)]
    ppermute x2, waiting for transfers between devices: 2.4 us -> 0.25 us  [shards(): across = [lax.ppermute(after(c, send), 'tm', swap_core) for c in crossed]]
    ppermute x3, starting transfers between devices: 3.22 us -> 4.9 us  [shards(): inners.append((lax.ppermute(send, 'tm', swap_chip), keep))]
    ppermute x2, starting transfers between devices: 3.42 us -> 1.81 us  [shards(): lax.ppermute(after(m, *pcs_all[2:]), 'tm', swap_chip)]
    ppermute x2, waiting for transfers between devices: 1.36 us -> 0.01 us  [shards(): swapped = [lax.ppermute(m, 'tm', swap_core) for m in mine]]
    unnamed x34 -> x30, local copies, waits for them, and re-layouts: 13.9 us -> 12.7 us
  transfers between devices with their start and end apart: 15 -> 15, of which waited for: 10 -> 7; matrix products, arithmetic and copies ran while one was open for 0% -> 0% of each run, Pallas kernels for 45% -> 46%
where the time goes in v5:
time: 127 us; the launch traced here: 126 us
  Pallas kernels  60.4 us (48%)
  waiting for transfers between devices  31.9 us (25%)
  starting transfers between devices  20 us (16%)
  local copies, waits for them, and re-layouts  12.8 us (10%)
    pallas_call x3, Pallas kernels, inner_call(): pl.pallas_call(functools.partial(inner_kernel, lat, first, span), grid=(l...  31.9 us
    ppermute x3, waiting for transfers between devices, shards(): inners.append((lax.ppermute(send, 'tm', swap_chip), keep))  23.8 us
    pallas_call x3, Pallas kernels, curl_call(): pl.pallas_call(functools.partial(curl_kernel, lat, first), grid=(span //...  14.8 us
    unnamed x30, local copies, waits for them, and re-layouts  12.7 us
    pallas_call x2, Pallas kernels, pick_call(): pl.pallas_call(functools.partial(pick_kernel, lat), grid=(lon // PICK_BLO...  7.02 us
    ppermute x2, waiting for transfers between devices, shards(): lax.ppermute(after(m, *pcs_all[2:]), 'tm', swap_chip)  6.64 us
    ppermute x1, starting transfers between devices, shards(): lax.ppermute(low, ('tm', 'tile'), north)  5.42 us
    pallas_call x1, Pallas kernels, edge_call(): pl.pallas_call(edge_kernel, grid=(lon // block,), in_specs=[pl.BlockSpec(...  5.06 us
  transfers between devices with their start and end apart: 15, of which 7 were waited for; matrix products, arithmetic and copies ran while one was open for 0% of the time, Pallas kernels for 46%

profile of v5, /device:TPU:1, one launch (start us, length us, event | category | flops | bytes accessed | tf_op | source)
XLA Modules:
  0.0 126.1 jit_solution(17361946488891159739)
XLA Ops:
  0.6 1.5 %collective-permute-start = (f32[2,64]{1,0:T(2,128)}, f32[2,64]{1,0:T(2,128)S(1)}, u32[]{:S(2)}, u32[]{:S(2)}) collective-permute-start(f32[2,64]{1,0:T(2,128)} %refs_0_.1), channel_id=1, source_target_pairs={{0,32},{32,0},{64,96},{96,64},{1,33},{33,1},{65,97},{97,65},{2,34}... | collective-permute-start | bytes 1544 | tf_op jit(solution)/shard_map/ppermute | solution.py:280
  2.1 1.0 collective-permute-done.refs_4_.refs_1_
  3.2 0.3 collective-permute-start.3
  3.5 1.7 %collective-permute-start.1 = (f32[2,64]{1,0:T(2,128)}, f32[2,64]{1,0:T(2,128)S(1)}, u32[]{:S(2)}, u32[]{:S(2)}) collective-permute-start(f32[2,64]{1,0:T(2,128)} %refs_0_.1), channel_id=1, source_target_pairs={{0,64},{32,96},{64,0},{96,32},{1,65},{33,97},{65,1},{97,33},{2,66}... | collective-permute-start | bytes 1544 | tf_op jit(solution)/shard_map/ppermute | solution.py:280
  5.3 3.5 %pick_end_rows.2.refs_4_.refs_0_ = bf16[2,128,2048]{2,1,0:T(8,128)(2,1)} custom-call(bf16[2,1024,2048]{2,1,0:T(8,128)(2,1)} %bitcast.11, bf16[2,1024,2048]{2,1,0:T(8,128)(2,1)} %bitcast.12, bf16[2,1024,2048]{2,1,0:T(8,128)(2,1)} %bitcast.13, bf16[2,1024,2048]{2,1,0:T(8,128)(2,1)} %bitcast.14, f32[2,64]{1,0:T(2,128)} %copy-done.12), custom_call_target="tpu_custom_call" | custom-call | bytes 16777216 | tf_op jit(solution)/shard_map/pick_end_rows/pallas_call | solution.py:103
  8.8 1.8 %collective-permute-start.4 = (bf16[2,128,2048]{2,1,0:T(8,128)(2,1)}, bf16[2,128,2048]{2,1,0:T(8,128)(2,1)}, u32[]{:S(2)}, u32[]{:S(2)}) collective-permute-start(bf16[2,128,2048]{2,1,0:T(8,128)(2,1)} %pick_end_rows.2.refs_4_.refs_0_), channel_id=1, source_target_pairs={{0,64},{32,96},{64,0},{96,32},{1,65},{33,97},{65,1},{97,33},{2,66}... | collective-permute-start | bytes 3145736 | tf_op jit(solution)/shard_map/ppermute | solution.py:284
  10.7 3.6 %pick_end_rows.3.refs_4_ = bf16[2,128,2048]{2,1,0:T(8,128)(2,1)} custom-call(bf16[2,1024,2048]{2,1,0:T(8,128)(2,1)} %bitcast.15, bf16[2,1024,2048]{2,1,0:T(8,128)(2,1)} %bitcast.16, bf16[2,1024,2048]{2,1,0:T(8,128)(2,1)} %bitcast.17, bf16[2,1024,2048]{2,1,0:T(8,128)(2,1)} %bitcast.18, bf16[2,128,2048]{2,1,0:T(8,128)(2,1)} %pick_end_rows.2.refs_4_.refs_0_), custom_call_target="tpu_custom_call" | custom-call | bytes 16777216 | tf_op jit(solution)/shard_map/pick_end_rows/pallas_call | solution.py:103
  14.8 1.8 %components.1.comp_ref = bf16[128,512]{1,0:T(8,128)(2,1)S(1)} custom-call(s32[3]{0:T(128)S(1)} %pad_add_fusion.place, f32[2,64]{1,0:T(2,128)S(1)} %copy-done.14, f32[2,64]{1,0:T(2,128)S(1)} %copy-done.13, f32[2,64]{1,0:T(2,128)S(1)} %collective-permute-done.1.refs_2_, f32[2,64]{1,0:T(2,128)S(1)} %collective-permute-done.2.refs_3_, f32[2,120,512]{2,1,0:T(8,128)S(1)} %copy-done.11), custom_call_target="tpu_custom_call" | custom-call | bytes 134217728 | tf_op jit(solution)/shard_map/components/pallas_call | solution.py:74
  16.7 3.4 %copy-done = bf16[2,128,8,2048]{3,2,1,0:T(8,128)(2,1)S(1)} copy-done((bf16[2,128,8,2048]{3,2,1,0:T(8,128)(2,1)S(1)}, bf16[2,128,8,2048]{3,2,1,0:T(8,128)(2,1)}, u32[]{:S(2)}) %copy-start) | copy-done | bytes 8388632
  20.0 11.1 %inner_partials.3 = (bf16[2,144,2048]{2,1,0:T(8,128)(2,1)}, f32[2,192,2048]{2,1,0:T(8,128)S(1)}) custom-call(bf16[128,512]{1,0:T(8,128)(2,1)S(1)} %components.1.comp_ref, bf16[2,1024,2048]{2,1,0:T(8,128)(2,1)S(1)} %bitcast.19, bf16[2,1024,2048]{2,1,0:T(8,128)(2,1)} %collective-permute-done.3.oth_ref), custom_call_target="tpu_custom_call" | custom-call | flops 5637144576 | bytes 20905984 | tf_op jit(solution)/shard_map/inner_partials/pallas_call | solution.py:186
  31.1 1.7 %copy-done.6 = f32[2,192,2048]{2,1,0:T(8,128)} copy-done((f32[2,192,2048]{2,1,0:T(8,128)}, f32[2,192,2048]{2,1,0:T(8,128)S(1)}, u32[]{:S(2)}) %copy-start.6) | copy-done | bytes 3145752
  32.8 1.7 %collective-permute-start.10 = (bf16[2,144,2048]{2,1,0:T(8,128)(2,1)}, bf16[2,144,2048]{2,1,0:T(8,128)(2,1)S(1)}, u32[]{:S(2)}, u32[]{:S(2)}) collective-permute-start(bf16[2,144,2048]{2,1,0:T(8,128)(2,1)} %get-tuple-element.26), channel_id=1, source_target_pairs={{0,64},{32,96},{64,0},{96,32},{1,65},{33,97},{65,1},{97,33},{2,66}... | collective-permute-start | bytes 3538952 | tf_op jit(solution)/shard_map/ppermute | solution.py:295
  34.5 12.4 %inner_partials.4 = (bf16[2,192,2048]{2,1,0:T(8,128)(2,1)}, f32[2,256,2048]{2,1,0:T(8,128)S(1)}) custom-call(bf16[128,512]{1,0:T(8,128)(2,1)S(1)} %components.1.comp_ref, bf16[2,1024,2048]{2,1,0:T(8,128)(2,1)S(1)} %bitcast.20, bf16[2,1024,2048]{2,1,0:T(8,128)(2,1)} %collective-permute-done.3.oth_ref), custom_call_target="tpu_custom_call" | custom-call | flops 7516192768 | bytes 22282240 | tf_op jit(solution)/shard_map/inner_partials/pallas_call | solution.py:186
  46.9 2.0 %copy-done.3 = f32[2,256,2048]{2,1,0:T(8,128)} copy-done((f32[2,256,2048]{2,1,0:T(8,128)}, f32[2,256,2048]{2,1,0:T(8,128)S(1)}, u32[]{:S(2)}) %copy-start.3) | copy-done | bytes 4194328
  48.9 1.0 collective-permute-start.6
  49.9 6.6 %collective-permute-done.8.refs_6_ = bf16[2,128,2048]{2,1,0:T(8,128)(2,1)} collective-permute-done((bf16[2,128,2048]{2,1,0:T(8,128)(2,1)}, bf16[2,128,2048]{2,1,0:T(8,128)(2,1)}, u32[]{:S(2)}, u32[]{:S(2)}) %collective-permute-start.8) | collective-permute-done | bytes 1048608 | tf_op jit(solution)/shard_map/ppermute | solution.py:284
  56.6 1.4 %collective-permute-start.9 = (bf16[2,128,2048]{2,1,0:T(8,128)(2,1)}, bf16[2,128,2048]{2,1,0:T(8,128)(2,1)}, u32[]{:S(2)}, u32[]{:S(2)}) collective-permute-start(bf16[2,128,2048]{2,1,0:T(8,128)(2,1)} %collective-permute-done.8.refs_6_), channel_id=1, source_target_pairs={{0,32},{32,0},{64,96},{96,64},{1,33},{33,1},{65,97},{97,65},{2,34}... | collective-permute-start | bytes 3145736 | tf_op jit(solution)/shard_map/ppermute | solution.py:300
  58.0 1.0 copy-done.9
  59.0 1.4 %collective-permute-start.14 = (bf16[2,192,2048]{2,1,0:T(8,128)(2,1)}, bf16[2,192,2048]{2,1,0:T(8,128)(2,1)}, u32[]{:S(2)}, u32[]{:S(2)}) collective-permute-start(bf16[2,192,2048]{2,1,0:T(8,128)(2,1)} %get-tuple-element.29), channel_id=1, source_target_pairs={{0,64},{32,96},{64,0},{96,32},{1,65},{33,97},{65,1},{97,33},{2,66}... | collective-permute-start | bytes 4718600 | tf_op jit(solution)/shard_map/ppermute | solution.py:295
  60.6 1.2 copy-done.10
  61.9 5.1 %end_rows.1 = (bf16[2,64,2048]{2,1,0:T(8,128)(2,1)S(1)}, bf16[2,64,2048]{2,1,0:T(8,128)(2,1)S(1)}, bf16[2,2,64,2048]{3,2,1,0:T(8,128)(2,1)S(1)}) custom-call(bf16[128,512]{1,0:T(8,128)(2,1)S(1)} %components.1.comp_ref, s32[8,2048]{1,0:T(8,128)S(1)} %copy-done.8, bf16[2,128,2048]{2,1,0:T(8,128)(2,1)S(1)} %copy-done.2, bf16[2,128,2048]{2,1,0:T(8,128)(2,1)S(1)} %copy-done.10, ...), custom_call_target="tpu_custom_call" | custom-call | tf_op jit(solution)/shard_map/end_rows/pallas_call | solution.py:141
  66.9 5.4 %collective-permute-start.12 = (bf16[2,64,2048]{2,1,0:T(8,128)(2,1)S(1)}, bf16[2,64,2048]{2,1,0:T(8,128)(2,1)S(1)}, u32[]{:S(2)}, u32[]{:S(2)}) collective-permute-start(bf16[2,64,2048]{2,1,0:T(8,128)(2,1)S(1)} %get-tuple-element.34), channel_id=1, source_target_pairs={{0,65},{1,66},{2,67},{3,68},{4,69},{5,70},{6,71},{7,72},{8,73},{9,... | collective-permute-start | bytes 1572872 | tf_op jit(solution)/shard_map/ppermute | solution.py:304
  72.3 1.3 %collective-permute-start.13 = (bf16[2,64,2048]{2,1,0:T(8,128)(2,1)S(1)}, bf16[2,64,2048]{2,1,0:T(8,128)(2,1)S(1)}, u32[]{:S(2)}, u32[]{:S(2)}) collective-permute-start(bf16[2,64,2048]{2,1,0:T(8,128)(2,1)S(1)} %get-tuple-element.38), channel_id=1, source_target_pairs={{1,64},{2,65},{3,66},{4,67},{5,68},{6,69},{7,70},{8,71},{9,72},{10... | collective-permute-start | bytes 1572872 | tf_op jit(solution)/shard_map/ppermute | solution.py:304
  73.6 8.1 %collective-permute-done.10.inner_ref = bf16[2,144,2048]{2,1,0:T(8,128)(2,1)S(1)} collective-permute-done((bf16[2,144,2048]{2,1,0:T(8,128)(2,1)}, bf16[2,144,2048]{2,1,0:T(8,128)(2,1)S(1)}, u32[]{:S(2)}, u32[]{:S(2)}) %collective-permute-start.10) | collective-permute-done | bytes 1179680 | tf_op jit(solution)/shard_map/ppermute | solution.py:295
  81.7 3.4 %copy-done.1 = bf16[2,128,8,2048]{3,2,1,0:T(8,128)(2,1)S(1)} copy-done((bf16[2,128,8,2048]{3,2,1,0:T(8,128)(2,1)S(1)}, bf16[2,128,8,2048]{3,2,1,0:T(8,128)(2,1)}, u32[]{:S(2)}) %copy-start.1) | copy-done | bytes 8388632
  85.1 8.4 %inner_partials.5 = (bf16[2,48,2048]{2,1,0:T(8,128)(2,1)S(1)}, f32[2,64,2048]{2,1,0:T(8,128)S(1)}) custom-call(bf16[128,512]{1,0:T(8,128)(2,1)S(1)} %components.1.comp_ref, bf16[2,1024,2048]{2,1,0:T(8,128)(2,1)S(1)} %bitcast.21, bf16[2,1024,2048]{2,1,0:T(8,128)(2,1)} %collective-permute-done.3.oth_ref), custom_call_target="tpu_custom_call" | custom-call | flops 1879048192 | bytes 18153472 | tf_op jit(solution)/shard_map/inner_partials/pallas_call | solution.py:186
  93.5 1.8 %collective-permute-start.11 = (bf16[2,48,2048]{2,1,0:T(8,128)(2,1)S(1)}, bf16[2,48,2048]{2,1,0:T(8,128)(2,1)S(1)}, u32[]{:S(2)}, u32[]{:S(2)}) collective-permute-start(bf16[2,48,2048]{2,1,0:T(8,128)(2,1)S(1)} %get-tuple-element.37), channel_id=1, source_target_pairs={{0,64},{32,96},{64,0},{96,32},{1,65},{33,97},{65,1},{97,33},{2,66}... | collective-permute-start | bytes 1179656 | tf_op jit(solution)/shard_map/ppermute | solution.py:295
  95.6 5.2 %curl_div.3 = (f32[64,8,2048]{2,1,0:T(8,128)}, f32[64,8,2048]{2,1,0:T(8,128)}) custom-call(f32[2,192,2048]{2,1,0:T(8,128)S(1)} %copy-done.7, bf16[2,144,2048]{2,1,0:T(8,128)(2,1)S(1)} %collective-permute-done.10.inner_ref, bf16[2,64,2048]{2,1,0:T(8,128)(2,1)S(1)} %collective-permute-done.12.low_ref, ...), custom_call_target="tpu_custom_call" | custom-call | flops 15728640 | bytes 7864320 | tf_op jit(solution)/shard_map/curl_div/pallas_call | solution.py:248
  100.8 14.8 %collective-permute-done.14.inner_ref = bf16[2,192,2048]{2,1,0:T(8,128)(2,1)} collective-permute-done((bf16[2,192,2048]{2,1,0:T(8,128)(2,1)}, bf16[2,192,2048]{2,1,0:T(8,128)(2,1)}, u32[]{:S(2)}, u32[]{:S(2)}) %collective-permute-start.14) | collective-permute-done | bytes 1572896 | tf_op jit(solution)/shard_map/ppermute | solution.py:295
  115.5 7.3 %curl_div.4 = (f32[64,8,2048]{2,1,0:T(8,128)}, f32[64,8,2048]{2,1,0:T(8,128)}) custom-call(f32[2,256,2048]{2,1,0:T(8,128)S(1)} %copy-done.4, bf16[2,192,2048]{2,1,0:T(8,128)(2,1)} %collective-permute-done.14.inner_ref, bf16[2,64,2048]{2,1,0:T(8,128)(2,1)S(1)} %collective-permute-done.12.low_ref, ...), custom_call_target="tpu_custom_call", output_to_operand_aliasing={{0}: (7, {}), {1}: (8, {})} | custom-call | flops 20971520 | bytes 10485760 | tf_op jit(solution)/shard_map/curl_div/pallas_call | solution.py:248
  122.9 1.0 collective-permute-done.11.inner_ref
  123.9 2.2 %curl_div.5 = (f32[64,8,2048]{2,1,0:T(8,128)}, f32[64,8,2048]{2,1,0:T(8,128)}) custom-call(f32[2,64,2048]{2,1,0:T(8,128)S(1)} %get-tuple-element.36.keep_ref, bf16[2,48,2048]{2,1,0:T(8,128)(2,1)S(1)} %collective-permute-done.11.inner_ref, bf16[2,64,2048]{2,1,0:T(8,128)(2,1)S(1)} %collective-permute-done.12.low_ref, ...), custom_call_target="tpu_custom_call", output_to_operand_aliasing={{0}: (7, {}), {1}: (8, {})} | custom-call | flops 5242880 | bytes 2621440 | tf_op jit(solution)/shard_map/curl_div/pallas_call | solution.py:248
  (43 shorter events, 1.4 us)
Async XLA Ops:
  0.6 2.5 %collective-permute-start = (f32[2,64]{1,0:T(2,128)}, f32[2,64]{1,0:T(2,128)S(1)}, u32[]{:S(2)}, u32[]{:S(2)}) collective-permute-start(f32[2,64]{1,0:T(2,128)} %refs_0_.1), channel_id=1, source_target_pairs={{0,32},{32,0},{64,96},{96,64},{1,33},{33,1},{65,97},{97,65},{2,34}... | collective-permute-start | bytes 1544 | tf_op jit(solution)/shard_map/ppermute | solution.py:280
  3.2 2.2 %copy-start.12 = (f32[2,64]{1,0:T(2,128)}, f32[2,64]{1,0:T(2,128)S(1)}, u32[]{:S(2)}) copy-start(f32[2,64]{1,0:T(2,128)S(1)} %collective-permute-done.refs_4_.refs_1_) | copy-start | bytes 1540
  3.2 13.5 %collective-permute-start.3 = (bf16[2,1024,2048]{2,1,0:T(8,128)(2,1)}, bf16[2,1024,2048]{2,1,0:T(8,128)(2,1)}, u32[]{:S(2)}, u32[]{:S(2)}) collective-permute-start(bf16[2,1024,2048]{2,1,0:T(8,128)(2,1)} %bitcast.10), channel_id=1, source_target_pairs={{0,32},{32,0},{64,96},{96,64},{1,33},{33,1},{65,97},{97,65},{2,34}... | collective-permute-start | bytes 25165832 | tf_op jit(solution)/shard_map/ppermute | solution.py:286
  3.5 5.3 %collective-permute-start.1 = (f32[2,64]{1,0:T(2,128)}, f32[2,64]{1,0:T(2,128)S(1)}, u32[]{:S(2)}, u32[]{:S(2)}) collective-permute-start(f32[2,64]{1,0:T(2,128)} %refs_0_.1), channel_id=1, source_target_pairs={{0,64},{32,96},{64,0},{96,32},{1,65},{33,97},{65,1},{97,33},{2,66}... | collective-permute-start | bytes 1544 | tf_op jit(solution)/shard_map/ppermute | solution.py:280
  5.2 3.6 %collective-permute-start.2 = (f32[2,64]{1,0:T(2,128)}, f32[2,64]{1,0:T(2,128)S(1)}, u32[]{:S(2)}, u32[]{:S(2)}) collective-permute-start(f32[2,64]{1,0:T(2,128)} %refs_0_.1), channel_id=1, source_target_pairs={{0,96},{32,64},{64,32},{96,0},{1,97},{33,65},{65,33},{97,1},{2,98}... | collective-permute-start | bytes 1544 | tf_op jit(solution)/shard_map/ppermute | solution.py:280
  8.8 25.7 %collective-permute-start.4 = (bf16[2,128,2048]{2,1,0:T(8,128)(2,1)}, bf16[2,128,2048]{2,1,0:T(8,128)(2,1)}, u32[]{:S(2)}, u32[]{:S(2)}) collective-permute-start(bf16[2,128,2048]{2,1,0:T(8,128)(2,1)} %pick_end_rows.2.refs_4_.refs_0_), channel_id=1, source_target_pairs={{0,64},{32,96},{64,0},{96,32},{1,65},{33,97},{65,1},{97,33},{2,66}... | collective-permute-start | bytes 3145736 | tf_op jit(solution)/shard_map/ppermute | solution.py:284
  10.6 3.6 %copy-start.2 = (bf16[2,128,2048]{2,1,0:T(8,128)(2,1)S(1)}, bf16[2,128,2048]{2,1,0:T(8,128)(2,1)}, u32[]{:S(2)}) copy-start(bf16[2,128,2048]{2,1,0:T(8,128)(2,1)} %pick_end_rows.2.refs_4_.refs_0_) | copy-start | bytes 3145732
  10.7 4.1 %copy-start.11 = (f32[2,120,512]{2,1,0:T(8,128)S(1)}, f32[2,120,512]{2,1,0:T(8,128)}, u32[]{:S(2)}) copy-start(f32[2,120,512]{2,1,0:T(8,128)} %refs_4_.1) | copy-start | bytes 1474564
  10.7 4.1 %copy-start.13 = (f32[2,64]{1,0:T(2,128)S(1)}, f32[2,64]{1,0:T(2,128)}, u32[]{:S(2)}) copy-start(f32[2,64]{1,0:T(2,128)} %copy-done.12) | copy-start | bytes 1540
  10.7 4.1 %copy-start.14 = (f32[2,64]{1,0:T(2,128)S(1)}, f32[2,64]{1,0:T(2,128)}, u32[]{:S(2)}) copy-start(f32[2,64]{1,0:T(2,128)} %refs_0_.1) | copy-start | bytes 1540
  14.2 43.8 %collective-permute-start.5 = (bf16[2,128,2048]{2,1,0:T(8,128)(2,1)S(1)}, bf16[2,128,2048]{2,1,0:T(8,128)(2,1)S(1)}, u32[]{:S(2)}, u32[]{:S(2)}) collective-permute-start(bf16[2,128,2048]{2,1,0:T(8,128)(2,1)S(1)} %copy-done.2), channel_id=1, source_target_pairs={{0,32},{32,0},{64,96},{96,64},{1,33},{33,1},{65,97},{97,65},{2,34}... | collective-permute-start | bytes 3145736 | tf_op jit(solution)/shard_map/ppermute | solution.py:285
  14.6 45.8 %collective-permute-start.7 = (bf16[2,128,2048]{2,1,0:T(8,128)(2,1)}, bf16[2,128,2048]{2,1,0:T(8,128)(2,1)}, u32[]{:S(2)}, u32[]{:S(2)}) collective-permute-start(bf16[2,128,2048]{2,1,0:T(8,128)(2,1)} %pick_end_rows.3.refs_4_), channel_id=1, source_target_pairs={{0,32},{32,0},{64,96},{96,64},{1,33},{33,1},{65,97},{97,65},{2,34}... | collective-permute-start | bytes 3145736 | tf_op jit(solution)/shard_map/ppermute | solution.py:285
  14.7 41.8 %collective-permute-start.8 = (bf16[2,128,2048]{2,1,0:T(8,128)(2,1)}, bf16[2,128,2048]{2,1,0:T(8,128)(2,1)}, u32[]{:S(2)}, u32[]{:S(2)}) collective-permute-start(bf16[2,128,2048]{2,1,0:T(8,128)(2,1)} %pick_end_rows.3.refs_4_), channel_id=1, source_target_pairs={{0,64},{32,96},{64,0},{96,32},{1,65},{33,97},{65,1},{97,33},{2,66}... | collective-permute-start | bytes 3145736 | tf_op jit(solution)/shard_map/ppermute | solution.py:284
  16.7 3.4 %copy-start = (bf16[2,128,8,2048]{3,2,1,0:T(8,128)(2,1)S(1)}, bf16[2,128,8,2048]{3,2,1,0:T(8,128)(2,1)}, u32[]{:S(2)}) copy-start(bf16[2,128,8,2048]{3,2,1,0:T(8,128)(2,1)} %param.6) | copy-start | bytes 25165828
  31.1 1.7 %copy-start.6 = (f32[2,192,2048]{2,1,0:T(8,128)}, f32[2,192,2048]{2,1,0:T(8,128)S(1)}, u32[]{:S(2)}) copy-start(f32[2,192,2048]{2,1,0:T(8,128)S(1)} %get-tuple-element.41.keep_ref) | copy-start | bytes 9437188
  32.8 27.8 %copy-start.5 = (bf16[2,128,2048]{2,1,0:T(8,128)(2,1)S(1)}, bf16[2,128,2048]{2,1,0:T(8,128)(2,1)}, u32[]{:S(2)}) copy-start(bf16[2,128,2048]{2,1,0:T(8,128)(2,1)} %pick_end_rows.3.refs_4_) | copy-start | bytes 3145732
  32.8 27.8 %copy-start.8 = (s32[8,2048]{1,0:T(8,128)S(1)}, s32[8,2048]{1,0:T(8,128)}, u32[]{:S(2)}) copy-start(s32[8,2048]{1,0:T(8,128)} %land_ref.7) | copy-start | bytes 196612
  32.8 48.9 %collective-permute-start.10 = (bf16[2,144,2048]{2,1,0:T(8,128)(2,1)}, bf16[2,144,2048]{2,1,0:T(8,128)(2,1)S(1)}, u32[]{:S(2)}, u32[]{:S(2)}) collective-permute-start(bf16[2,144,2048]{2,1,0:T(8,128)(2,1)} %get-tuple-element.26), channel_id=1, source_target_pairs={{0,64},{32,96},{64,0},{96,32},{1,65},{33,97},{65,1},{97,33},{2,66}... | collective-permute-start | bytes 3538952 | tf_op jit(solution)/shard_map/ppermute | solution.py:295
  46.9 2.0 %copy-start.3 = (f32[2,256,2048]{2,1,0:T(8,128)}, f32[2,256,2048]{2,1,0:T(8,128)S(1)}, u32[]{:S(2)}) copy-start(f32[2,256,2048]{2,1,0:T(8,128)S(1)} %get-tuple-element.40.keep_ref) | copy-start | bytes 12582916
  48.9 11.5 %collective-permute-start.6 = (bf16[2,128,2048]{2,1,0:T(8,128)(2,1)}, bf16[2,128,2048]{2,1,0:T(8,128)(2,1)}, u32[]{:S(2)}, u32[]{:S(2)}) collective-permute-start(bf16[2,128,2048]{2,1,0:T(8,128)(2,1)} %collective-permute-done.4.refs_2_), channel_id=1, source_target_pairs={{0,32},{32,0},{64,96},{96,64},{1,33},{33,1},{65,97},{97,65},{2,34}... | collective-permute-start | bytes 3145736 | tf_op jit(solution)/shard_map/ppermute | solution.py:300
  56.6 4.1 %collective-permute-start.9 = (bf16[2,128,2048]{2,1,0:T(8,128)(2,1)}, bf16[2,128,2048]{2,1,0:T(8,128)(2,1)}, u32[]{:S(2)}, u32[]{:S(2)}) collective-permute-start(bf16[2,128,2048]{2,1,0:T(8,128)(2,1)} %collective-permute-done.8.refs_6_), channel_id=1, source_target_pairs={{0,32},{32,0},{64,96},{96,64},{1,33},{33,1},{65,97},{97,65},{2,34}... | collective-permute-start | bytes 3145736 | tf_op jit(solution)/shard_map/ppermute | solution.py:300
  58.0 1.0 copy-start.9
  59.0 56.5 %collective-permute-start.14 = (bf16[2,192,2048]{2,1,0:T(8,128)(2,1)}, bf16[2,192,2048]{2,1,0:T(8,128)(2,1)}, u32[]{:S(2)}, u32[]{:S(2)}) collective-permute-start(bf16[2,192,2048]{2,1,0:T(8,128)(2,1)} %get-tuple-element.29), channel_id=1, source_target_pairs={{0,64},{32,96},{64,0},{96,32},{1,65},{33,97},{65,1},{97,33},{2,66}... | collective-permute-start | bytes 4718600 | tf_op jit(solution)/shard_map/ppermute | solution.py:295
  60.6 1.2 copy-start.10
  66.9 28.6 %collective-permute-start.12 = (bf16[2,64,2048]{2,1,0:T(8,128)(2,1)S(1)}, bf16[2,64,2048]{2,1,0:T(8,128)(2,1)S(1)}, u32[]{:S(2)}, u32[]{:S(2)}) collective-permute-start(bf16[2,64,2048]{2,1,0:T(8,128)(2,1)S(1)} %get-tuple-element.34), channel_id=1, source_target_pairs={{0,65},{1,66},{2,67},{3,68},{4,69},{5,70},{6,71},{7,72},{8,73},{9,... | collective-permute-start | bytes 1572872 | tf_op jit(solution)/shard_map/ppermute | solution.py:304
  72.3 23.2 %collective-permute-start.13 = (bf16[2,64,2048]{2,1,0:T(8,128)(2,1)S(1)}, bf16[2,64,2048]{2,1,0:T(8,128)(2,1)S(1)}, u32[]{:S(2)}, u32[]{:S(2)}) collective-permute-start(bf16[2,64,2048]{2,1,0:T(8,128)(2,1)S(1)} %get-tuple-element.38), channel_id=1, source_target_pairs={{1,64},{2,65},{3,66},{4,67},{5,68},{6,69},{7,70},{8,71},{9,72},{10... | collective-permute-start | bytes 1572872 | tf_op jit(solution)/shard_map/ppermute | solution.py:304
  81.7 3.4 %copy-start.1 = (bf16[2,128,8,2048]{3,2,1,0:T(8,128)(2,1)S(1)}, bf16[2,128,8,2048]{3,2,1,0:T(8,128)(2,1)}, u32[]{:S(2)}) copy-start(bf16[2,128,8,2048]{3,2,1,0:T(8,128)(2,1)} %param.6) | copy-start | bytes 25165828
  85.1 10.5 %copy-start.7 = (f32[2,192,2048]{2,1,0:T(8,128)S(1)}, f32[2,192,2048]{2,1,0:T(8,128)}, u32[]{:S(2)}) copy-start(f32[2,192,2048]{2,1,0:T(8,128)} %copy-done.6) | copy-start | bytes 9437188
  93.5 22.0 %copy-start.4 = (f32[2,256,2048]{2,1,0:T(8,128)S(1)}, f32[2,256,2048]{2,1,0:T(8,128)}, u32[]{:S(2)}) copy-start(f32[2,256,2048]{2,1,0:T(8,128)} %copy-done.3) | copy-start | bytes 12582916
  93.5 30.3 %collective-permute-start.11 = (bf16[2,48,2048]{2,1,0:T(8,128)(2,1)S(1)}, bf16[2,48,2048]{2,1,0:T(8,128)(2,1)S(1)}, u32[]{:S(2)}, u32[]{:S(2)}) collective-permute-start(bf16[2,48,2048]{2,1,0:T(8,128)(2,1)S(1)} %get-tuple-element.37), channel_id=1, source_target_pairs={{0,64},{32,96},{64,0},{96,32},{1,65},{33,97},{65,1},{97,33},{2,66}... | collective-permute-start | bytes 1179656 | tf_op jit(solution)/shard_map/ppermute | solution.py:295
